TPU v7x, 32 devices: a whole 2x2x4 slice. The times are simulated.
32 devices in a mesh: groups: 2 (over x), lvl: 8 (over z, y), stu: 2 (over core).
Axes of the slice: x: 2, y: 2, z: 4, core: 2. Of those that a mesh axis runs over, the one named last changes fastest.
Arguments:
- student_factor: float32 [4096, 256], P(('groups', 'stu', 'lvl')), parts along dimension 0, may hold values from -1.5 to 1.5
- level_factor: float32 [16384, 256], P(('groups', 'lvl', 'stu')), parts along dimension 0, may hold values from -1.5 to 1.5
- block_position: int32 [4, 8, 24], P(('groups', 'stu'), 'lvl'), parts along dimension 0, may hold values from 0 to 63, as said below
- block_count: int32 [4, 8], P(('groups', 'stu'), 'lvl'), parts along dimension 0, may hold values from 1 to 24, as said below
- outcome: int32 [4, 8, 24, 128, 128], P(('groups', 'stu'), 'lvl'), parts along dimension 0, may hold values 0 or 1
Outputs:
- student_out: float32 [4096, 256], P(('groups', 'stu', 'lvl')), parts along dimension 0
- level_out: float32 [16384, 256], P(('groups', 'lvl', 'stu')), parts along dimension 0
There are 2 independent parts, one for each index of `groups`. A program takes and returns all parts, laid end to end along the dimension named above; each array names one. Nothing has to cross between parts.
Inputs may be any that keep to these rules, and one draw needn't show every extreme that they name: `block_position`: within one tile the positions of all 24 slots are distinct, each names a block of the tile. `block_count`: counts are very uneven between tiles; some tile uses all its slots.
All inputs are finite; a program needn't handle non-finite values. No bound on the sum of `outcome` on one device may be relied on, other than what follows from the above.
Results may differ from a plain program's by a relative error of at most 0.008.
Values may be sent and summed in bfloat16 or wider, within the bound.
No kernel may reach another device: no remote copies, remote signals or barrier semaphores. Data moves between devices by JAX's collectives and lax.ppermute only.
A program may use at most 128 MiB of HBM per device.

v0:
```python
import jax
import jax.numpy as jnp
from jax import lax
from jax.sharding import PartitionSpec as P

ITERS = 2


learn_rate = 0.05
decay_rate = 0.1


def block_grads(stu_panel, lvl_panel, block_position, block_count, outcome):
    blocksize = outcome.shape[-1]
    rank_width = stu_panel.shape[1]
    position = block_position.reshape(-1)
    slots = position.shape[0]
    across = lvl_panel.shape[0] // blocksize
    down_count = stu_panel.shape[0] // blocksize
    row_block = position // across
    col_block = position % across
    stu_blocks = jnp.take(stu_panel.reshape(down_count, blocksize, rank_width), row_block, axis=0)
    lvl_blocks = jnp.take(lvl_panel.reshape(across, blocksize, rank_width), col_block, axis=0)
    logits = jnp.einsum("bir,bjr->bij", stu_blocks, lvl_blocks, preferred_element_type=jnp.float32)
    usable = (jnp.arange(slots, dtype=jnp.int32) < block_count.reshape(()))[:, None, None]
    labels = outcome.reshape(slots, blocksize, blocksize).astype(jnp.float32)
    residual = jnp.where(usable, jax.nn.sigmoid(logits) - labels, 0.0).astype(jnp.bfloat16)
    stu_terms = jnp.einsum("bij,bjr->bir", residual, lvl_blocks, preferred_element_type=jnp.float32)
    lvl_terms = jnp.einsum("bij,bir->bjr", residual, stu_blocks, preferred_element_type=jnp.float32)
    row_onehot = (row_block[None, :] == jnp.arange(down_count, dtype=jnp.int32)[:, None]).astype(
        jnp.float32
    )
    col_onehot = (col_block[None, :] == jnp.arange(across, dtype=jnp.int32)[:, None]).astype(
        jnp.float32
    )
    grad_stu = jnp.einsum("nb,bkr->nkr", row_onehot, stu_terms, precision=lax.Precision.HIGH)
    grad_lvl = jnp.einsum("nb,bkr->nkr", col_onehot, lvl_terms, precision=lax.Precision.HIGH)
    return (grad_stu.reshape(-1, rank_width), grad_lvl.reshape(-1, rank_width))


def settle(stu_own, lvl_own, grad_stu_panel, grad_lvl_panel):
    grad_stu = lax.psum_scatter(grad_stu_panel, "lvl", scatter_dimension=0, tiled=True)
    grad_lvl = lax.psum_scatter(
        grad_lvl_panel.astype(jnp.bfloat16), "stu", scatter_dimension=0, tiled=True
    ).astype(jnp.float32)
    stu_next = stu_own - learn_rate * (grad_stu + decay_rate * stu_own)
    lvl_next = lvl_own - learn_rate * (grad_lvl + decay_rate * lvl_own)
    return (stu_next, lvl_next)


def per_device(student_factor, level_factor, block_position, block_count, outcome):
    stu_own, lvl_own = (student_factor, level_factor)
    for step in range(ITERS):
        stu_panel = lax.all_gather(stu_own.astype(jnp.bfloat16), "lvl", axis=0, tiled=True)
        lvl_panel = lax.all_gather(lvl_own.astype(jnp.bfloat16), "stu", axis=0, tiled=True)
        grad_stu, grad_lvl = block_grads(stu_panel, lvl_panel, block_position, block_count, outcome)
        stu_own, lvl_own = settle(stu_own, lvl_own, grad_stu, grad_lvl)
    return (stu_own, lvl_own)


def solution(mesh):
    return jax.shard_map(
        per_device,
        mesh=mesh,
        in_specs=(
            P(("groups", "stu", "lvl"), None),
            P(("groups", "lvl", "stu"), None),
            P(("groups", "stu"), "lvl", None),
            P(("groups", "stu"), "lvl"),
            P(("groups", "stu"), "lvl", None, None, None),
        ),
        out_specs=(P(("groups", "stu", "lvl"), None), P(("groups", "lvl", "stu"), None)),
        check_vma=False,
    )
```

profile of v0, /device:TPU:0, one launch (start us, length us, event | category | flops | bytes accessed | tf_op | source)
XLA Modules:
  0.0 257.0 jit_solution(12019251375547155295)
XLA Ops:
  7.9 0.7 compare_and_fusion
  8.6 0.9 convert_element_type.47
  9.5 1.1 convert_element_type.48
  10.6 2.3 all_gather.13
  12.8 33.1 %all_gather.12 = bf16[1024,256]{1,0:T(8,128)(2,1)S(1)} all-gather(bf16[128,256]{1,0:T(8,128)(2,1)S(1)} %convert_element_type.47), channel_id=1, replica_groups=mesh['groups'=2,'lvl'=8,'stu'=2] {'lvl'}, dimensions={0}, use_global_device_ids=true | all-gather | bytes 589824 | tf_op jit(solution)/shard_map/all_gather | solution.py:54
  45.9 1.8 gather_fusion
  47.8 0.6 gather_fusion.1
  48.5 2.8 %fusion.9 = bf16[24,128,128]{2,1,0:T(8,128)(2,1)S(1)} fusion(s32[1,1,24,128,128]{4,3,2,1,0:T(8,128)} %param.11, pred[24]{0:T(512)(128)(4,1)S(1)} %get-tuple-element.9, bf16[24,128,256]{2,1,0:T(8,128)(2,1)} %gather_fusion, pred[24]{0:T(512)(128)(4,1)S(1)} %get-tuple-element.7, bf16[24,128,256]{2,1,0:T(8,128)(2,1)S(1)} %gather_fusion.1, ...), kind=kOutput, calls=%fused_computation.15 | convolution fusion | flops 205651968 | bytes 5505096 | tf_op jit(solution)/shard_map/bir,bjr->bij/dot_general | solution.py:24
  51.3 0.6 fusion.18
  52.0 2.3 fusion.12
  54.2 0.9 copy.8
  55.2 0.6 fusion.20
  55.8 2.3 fusion.6
  58.1 1.3 copy.7
  59.5 4.6 %reduce-scatter.7.cloned.1.call-done = bf16[512,256]{1,0:T(8,128)(2,1)} async-done(((bf16[1024,256]{1,0:T(8,128)(2,1)}), bf16[512,256]{1,0:T(8,128)(2,1)}) %reduce-scatter.7.cloned.1.call-update) | async-done | bytes 262160 | tf_op jit(solution)/shard_map/reduce_scatter | solution.py:43
  64.1 1.0 fusion.22
  65.1 2.2 all_gather.15
  67.3 0.6 gather_fusion.3
  68.0 64.4 %reduce-scatter.5.cloned.1.call-done = f32[128,256]{1,0:T(8,128)} async-done(((f32[1024,256]{1,0:T(8,128)}), f32[128,256]{1,0:T(8,128)}) %reduce-scatter.5.cloned.1.call-update) | async-done | bytes 131088 | tf_op jit(solution)/shard_map/reduce_scatter | solution.py:42
  132.4 0.9 fusion.23
  133.3 31.7 %all_gather.14 = bf16[1024,256]{1,0:T(8,128)(2,1)S(1)} all-gather(bf16[128,256]{1,0:T(8,128)(2,1)S(1)} %fusion.23), channel_id=1, replica_groups=mesh['groups'=2,'lvl'=8,'stu'=2] {'lvl'}, dimensions={0}, use_global_device_ids=true | all-gather | bytes 589824 | tf_op jit(solution)/shard_map/all_gather | solution.py:54
  165.0 1.8 gather_fusion.2
  166.9 2.8 %fusion.11 = bf16[24,128,128]{2,1,0:T(8,128)(2,1)S(1)} fusion(s32[1,1,24,128,128]{4,3,2,1,0:T(8,128)} %param.11, pred[24]{0:T(512)(128)(4,1)S(1)} %get-tuple-element.9, bf16[24,128,256]{2,1,0:T(8,128)(2,1)} %gather_fusion.2, pred[24]{0:T(512)(128)(4,1)S(1)} %get-tuple-element.7, bf16[24,128,256]{2,1,0:T(8,128)(2,1)S(1)} %gather_fusion.3, ...), kind=kOutput, calls=%fused_computation.17 | convolution fusion | flops 205651968 | bytes 5505096 | tf_op jit(solution)/shard_map/bir,bjr->bij/dot_general | solution.py:24
  169.7 0.7 fusion.19
  170.4 2.3 fusion.15
  172.6 0.9 copy.10
  174.3 2.3 fusion.2
  176.5 1.3 copy.9
  177.9 2.7 %reduce-scatter.11.cloned.1.call-done = bf16[512,256]{1,0:T(8,128)(2,1)} async-done(((bf16[1024,256]{1,0:T(8,128)(2,1)}), bf16[512,256]{1,0:T(8,128)(2,1)}) %reduce-scatter.11.cloned.1.call-update) | async-done | bytes 262160 | tf_op jit(solution)/shard_map/reduce_scatter | solution.py:43
  180.6 1.9 multiply_subtract_fusion
  182.5 66.4 %reduce-scatter.9.cloned.1.call-done = f32[128,256]{1,0:T(8,128)} async-done(((f32[1024,256]{1,0:T(8,128)}), f32[128,256]{1,0:T(8,128)}) %reduce-scatter.9.cloned.1.call-update) | async-done | bytes 131088 | tf_op jit(solution)/shard_map/reduce_scatter | solution.py:42
  248.9 1.6 multiply_subtract_fusion.2
  (25 shorter events, 0.9 us)
Async XLA Ops:
  7.2 56.9 %reduce-scatter.7.cloned.1.call-start = ((), (), s32[]{:S(2)}) async-start(), calls=%async_computation.5 | async-start | bytes 786432 | tf_op jit(solution)/shard_map/reduce_scatter | solution.py:43
  48.4 2.9 %copy-start = (bf16[24,128,256]{2,1,0:T(8,128)(2,1)S(1)}, bf16[24,128,256]{2,1,0:T(8,128)(2,1)}, u32[]{:S(2)}) copy-start(bf16[24,128,256]{2,1,0:T(8,128)(2,1)} %gather_fusion) | copy-start | bytes 4718596
  55.1 77.2 %reduce-scatter.5.cloned.1.call-start = ((), (), s32[]{:S(2)}) async-start(), calls=%async_computation.4 | async-start | bytes 1179648 | tf_op jit(solution)/shard_map/reduce_scatter | solution.py:42
  58.1 5.9 %copy-start.2 = (f32[512,256]{1,0:T(8,128)S(1)}, f32[512,256]{1,0:T(8,128)}, u32[]{:S(2)}) copy-start(f32[512,256]{1,0:T(8,128)} %param.8) | copy-start | bytes 1572868
  59.5 121.1 %reduce-scatter.11.cloned.1.call-start = ((), (), s32[]{:S(2)}) async-start(), calls=%async_computation.7 | async-start | bytes 786432 | tf_op jit(solution)/shard_map/reduce_scatter | solution.py:43
  67.3 65.1 %copy-start.3 = (f32[128,256]{1,0:T(8,128)S(1)}, f32[128,256]{1,0:T(8,128)}, u32[]{:S(2)}) copy-start(f32[128,256]{1,0:T(8,128)} %param.7) | copy-start | bytes 393220
  166.9 2.8 %copy-start.1 = (bf16[24,128,256]{2,1,0:T(8,128)(2,1)S(1)}, bf16[24,128,256]{2,1,0:T(8,128)(2,1)}, u32[]{:S(2)}) copy-start(bf16[24,128,256]{2,1,0:T(8,128)(2,1)} %gather_fusion.2) | copy-start | bytes 4718596
  173.6 75.4 %reduce-scatter.9.cloned.1.call-start = ((), (), s32[]{:S(2)}) async-start(), calls=%async_computation.6 | async-start | bytes 1179648 | tf_op jit(solution)/shard_map/reduce_scatter | solution.py:42
  176.5 4.1 %copy-start.4 = (bf16[512,256]{1,0:T(8,128)(2,1)S(1)}, bf16[512,256]{1,0:T(8,128)(2,1)}, u32[]{:S(2)}) copy-start(bf16[512,256]{1,0:T(8,128)(2,1)} %reduce-scatter.7.cloned.1.call-done) | copy-start | bytes 786436
  177.8 71.1 %copy-start.5 = (f32[128,256]{1,0:T(8,128)S(1)}, f32[128,256]{1,0:T(8,128)}, u32[]{:S(2)}) copy-start(f32[128,256]{1,0:T(8,128)} %reduce-scatter.5.cloned.1.call-done) | copy-start | bytes 393220
Sparse Core Ops, SparseCore 0:
  55.3 8.7 reduce-scatter.6
  67.8 64.4 reduce-scatter.4
  173.7 6.8 reduce-scatter.10
  184.2 64.6 reduce-scatter.8
where the time goes:
time: 257 us
  waiting for transfers between devices  138 us (54%)
  blocking collectives  69.3 us (27%)
  matrix products  17.3 us (7%)
  between operations  14.6 us (6%)
  local copies, waits for them, and re-layouts  9.37 us (4%)
  other arithmetic  8.16 us (3%)
    reduce_scatter x2, waiting for transfers between devices, settle(): lax.psum_scatter(grad_stu_panel, 'lvl', scatter_dimension=0, tiled=True)  131 us
    all_gather x2, blocking collectives, per_device(): lax.all_gather(stu_own.astype(jnp.bfloat16), 'lvl', axis=0, tiled=True)  64.8 us
    reduce_scatter x2, waiting for transfers between devices, settle(): lax.psum_scatter(grad_lvl_panel.astype(jnp.bfloat16), 'stu', scatter_dime...  7.29 us
    dot_general x2, matrix products, block_grads(): jnp.einsum('bir,bjr->bij', stu_blocks, lvl_blocks, preferred_element_type...  5.66 us
  transfers between devices with their start and end apart: 4, of which 4 were waited for; matrix products, arithmetic and copies ran while one was open for 5% of the time, Pallas kernels for 0%

commit v1 on v0

v1 whole, which is shorter than its diff:
```python
import functools

import jax
import jax.numpy as jnp
from jax import lax
from jax.experimental import pallas as pl
from jax.experimental.pallas import tpu as pltpu
from jax.sharding import PartitionSpec as P

ITERS = 2
GROUP = 4

learn_rate = 0.05
decay_rate = 0.1

F32, BF16 = jnp.float32, jnp.bfloat16
NN = (((1,), (0,)), ((), ()))
NT = (((1,), (1,)), ((), ()))
TN = (((0,), (0,)), ((), ()))


def dot(a, b, dims):
    return lax.dot_general(a, b, dims, preferred_element_type=F32)


def vmem():
    return pl.BlockSpec(memory_space=pltpu.VMEM)


def smem():
    return pl.BlockSpec(memory_space=pltpu.SMEM)


def call(body, out_shape, scalars, arrays, scratch=()):
    many = isinstance(out_shape, tuple)
    return pl.pallas_call(
        body,
        out_shape=out_shape,
        in_specs=[smem()] * len(scalars) + [vmem()] * len(arrays),
        out_specs=(vmem(),) * len(out_shape) if many else vmem(),
        scratch_shapes=list(scratch),
        compiler_params=pltpu.CompilerParams(vmem_limit_bytes=48 * 2**20),
    )(*scalars, *arrays)


def sds(shape, dtype):
    return jax.ShapeDtypeStruct(tuple(shape), dtype)


def cast_body(x, y):
    y[...] = x[...].astype(y.dtype)


def sign_body(outcome, sign):
    sign[...] = (1 - 2 * outcome[...]).astype(F32).astype(BF16)


def swap(x, axis, n, k):
    return lax.ppermute(x, axis, [(i, i ^ k) for i in range(n)])


def residual_body(n_lvl, n_stu, blk, position, count, sign, *refs):
    stu_parts, refs = refs[:n_lvl], refs[n_lvl:]
    lvl_parts, refs = refs[:n_stu], refs[n_stu:]
    res, grad, stu, lvl, acc = refs
    me_l, me_s = lax.axis_index("lvl"), lax.axis_index("stu")
    own = stu_parts[0].shape[0]
    for k, part in enumerate(stu_parts):
        stu[pl.ds(pl.multiple_of((me_l ^ k) * own, own), own), :] = part[...]
    half = lvl_parts[0].shape[0]
    for k, part in enumerate(lvl_parts):
        lvl[pl.ds(pl.multiple_of((me_s ^ k) * half, half), half), :] = part[...]
    acc[...] = jnp.zeros_like(acc)
    across = lvl.shape[0] // blk
    used = count[0]

    def step(i, _):
        got = []
        for g in range(GROUP):
            b = i * GROUP + g
            p = position[b]
            row = pl.multiple_of((p // across) * blk, blk)
            col = pl.multiple_of((p % across) * blk, blk)
            u, v = stu[pl.ds(row, blk), :], lvl[pl.ds(col, blk), :]
            two = jnp.tanh(0.5 * dot(u, v, NT)) + sign[b].astype(F32)
            two = jnp.where(b < used, two, 0.0).astype(BF16)
            res[b] = two
            got.append((row, dot(two, v, NN)))
        for row, part in got:
            acc[pl.ds(row, blk), :] += part
        return 0

    lax.fori_loop(0, (used + GROUP - 1) // GROUP, step, 0)
    grad[...] = acc[...].astype(BF16).reshape(grad.shape)


def level_body(blk, position, count, res, stu, keep, send, acc):
    me_s = lax.axis_index("stu")
    acc[...] = jnp.zeros_like(acc)
    across = acc.shape[0] // blk
    used = count[0]

    def step(i, _):
        got = []
        for g in range(GROUP):
            b = i * GROUP + g
            p = position[b]
            row = pl.multiple_of((p // across) * blk, blk)
            col = pl.multiple_of((p % across) * blk, blk)
            got.append((col, dot(res[b], stu[pl.ds(row, blk), :], TN)))
        for col, part in got:
            acc[pl.ds(col, blk), :] += part
        return 0

    lax.fori_loop(0, (used + GROUP - 1) // GROUP, step, 0)
    half = keep.shape[0]
    keep[...] = acc[pl.ds(pl.multiple_of(me_s * half, half), half), :]
    send[...] = acc[pl.ds(pl.multiple_of((me_s ^ 1) * half, half), half), :].astype(BF16)


def after(own, grad_twice):
    return own - learn_rate * (0.5 * grad_twice + decay_rate * own)


def settle_student_body(own, got, new, low):
    grad = got[0].astype(F32)
    for k in range(1, got.shape[0]):
        grad += got[k].astype(F32)
    value = after(own[...], grad)
    new[...] = value
    low[...] = value.astype(BF16)


def settle_level_body(own, keep, got, new, low):
    value = after(own[...], keep[...] + got[...].astype(F32))
    new[...] = value
    low[...] = value.astype(BF16)


def per_device(n_lvl, n_stu, student_factor, level_factor, block_position, block_count, outcome):
    blk = outcome.shape[-1]
    slots = outcome.shape[2]
    stu_own, lvl_own = student_factor, level_factor
    rank = stu_own.shape[1]
    position, count = block_position.reshape(-1), block_count.reshape(-1)
    stu_rows, lvl_rows = n_lvl * stu_own.shape[0], n_stu * lvl_own.shape[0]
    stu_low = call(cast_body, sds(stu_own.shape, BF16), (), (stu_own,))
    lvl_low = call(cast_body, sds(lvl_own.shape, BF16), (), (lvl_own,))
    sign = call(
        sign_body, sds((slots, blk, blk), BF16), (), (outcome.reshape(slots, blk, blk),)
    )
    for step in range(ITERS):
        lvl_parts = [lvl_low] + [swap(lvl_low, "stu", n_stu, k) for k in range(1, n_stu)]
        stu_parts = [stu_low] + [swap(stu_low, "lvl", n_lvl, k) for k in range(1, n_lvl)]
        res, grad, stu_panel = call(
            functools.partial(residual_body, n_lvl, n_stu, blk),
            (
                sds((slots, blk, blk), BF16),
                sds((n_lvl,) + stu_own.shape, BF16),
                sds((stu_rows, rank), BF16),
            ),
            (position, count),
            (sign, *stu_parts, *lvl_parts),
            (pltpu.VMEM((lvl_rows, rank), BF16), pltpu.VMEM((stu_rows, rank), F32)),
        )
        got = lax.all_to_all(grad, "lvl", 0, 0)
        keep, send = call(
            functools.partial(level_body, blk),
            (sds(lvl_own.shape, F32), sds(lvl_own.shape, BF16)),
            (position, count),
            (res, stu_panel),
            (pltpu.VMEM((lvl_rows, rank), F32),),
        )
        came = swap(send, "stu", n_stu, 1)
        lvl_own, lvl_low = call(
            settle_level_body,
            (sds(lvl_own.shape, F32), sds(lvl_own.shape, BF16)),
            (),
            (lvl_own, keep, came),
        )
        stu_own, stu_low = call(
            settle_student_body,
            (sds(stu_own.shape, F32), sds(stu_own.shape, BF16)),
            (),
            (stu_own, got),
        )
    return (stu_own, lvl_own)


def solution(mesh):
    return jax.shard_map(
        functools.partial(per_device, mesh.shape["lvl"], mesh.shape["stu"]),
        mesh=mesh,
        in_specs=(
            P(("groups", "stu", "lvl"), None),
            P(("groups", "lvl", "stu"), None),
            P(("groups", "stu"), "lvl", None),
            P(("groups", "stu"), "lvl"),
            P(("groups", "stu"), "lvl", None, None, None),
        ),
        out_specs=(P(("groups", "stu", "lvl"), None), P(("groups", "lvl", "stu"), None)),
        check_vma=False,
    )
```

time: 257 us -> 82.2 us (0.32)
  waiting for transfers between devices: 138 us -> 29.4 us
  blocking collectives: 69.3 us -> 0 us
  starting transfers between devices: 0.16 us -> 37.6 us
  matrix products: 17.3 us -> 0 us
  between operations: 14.6 us -> 1.42 us
  Pallas kernels: 0 us -> 9.84 us
  other arithmetic: 8.16 us -> 0 us
  local copies, waits for them, and re-layouts: 9.37 us -> 3.35 us
    reduce_scatter x4 -> x0, waiting for transfers between devices: 138 us -> none  [the longest x2 131 us: settle(): lax.psum_scatter(grad_stu_panel, 'lvl', scatter_dimension=0, tiled=True)]
    all_gather x4 -> x0, blocking collectives: 69.3 us -> none  [the longest x2 64.8 us: per_device(): lax.all_gather(stu_own.astype(jnp.bfloat16), 'lvl', axis=0, tiled=True)]
    ppermute x0 -> x18, starting transfers between devices: none -> 27.6 us  [swap(): return lax.ppermute(x, axis, [(i, i ^ k) for i in range(n)])]
    all_to_all x0 -> x2, waiting for transfers between devices: none -> 19.8 us  [per_device(): got = lax.all_to_all(grad, 'lvl', 0, 0)]
    dot_general x10 -> x0, matrix products: 17.3 us -> none  [the longest x2 5.66 us: block_grads(): jnp.einsum('bir,bjr->bij', stu_blocks, lvl_blocks, preferred_element_type...]
    all_to_all x0 -> x2, starting transfers between devices: none -> 9.98 us  [per_device(): got = lax.all_to_all(grad, 'lvl', 0, 0)]
    pallas_call x0 -> x11, Pallas kernels: none -> 9.84 us  [call(): pl.pallas_call(body, out_shape=out_shape, in_specs=[smem()] * len(scalars...]
    ppermute x0 -> x18, waiting for transfers between devices: none -> 9.59 us  [swap(): return lax.ppermute(x, axis, [(i, i ^ k) for i in range(n)])]
  transfers between devices with their start and end apart: 4 -> 20, of which waited for: 4 -> 10; matrix products, arithmetic and copies ran while one was open for 5% -> 0% of each run, Pallas kernels for 0% -> 5%
where the time goes in v1:
time: 82.2 us; the launch traced here: 81.6 us
  starting transfers between devices  37.6 us (46%)
  waiting for transfers between devices  29.4 us (36%)
  Pallas kernels  9.84 us (12%)
  local copies, waits for them, and re-layouts  3.35 us (4%)
  between operations  1.42 us (2%)
    ppermute x18, starting transfers between devices, swap(): return lax.ppermute(x, axis, [(i, i ^ k) for i in range(n)])  27.6 us
    all_to_all x2, waiting for transfers between devices, per_device(): got = lax.all_to_all(grad, 'lvl', 0, 0)  19.8 us
    all_to_all x2, starting transfers between devices, per_device(): got = lax.all_to_all(grad, 'lvl', 0, 0)  9.98 us
    pallas_call x11, Pallas kernels, call(): pl.pallas_call(body, out_shape=out_shape, in_specs=[smem()] * len(scalars...  9.84 us
    ppermute x18, waiting for transfers between devices, swap(): return lax.ppermute(x, axis, [(i, i ^ k) for i in range(n)])  9.59 us
    unnamed x12, local copies, waits for them, and re-layouts  3.35 us
  transfers between devices with their start and end apart: 20, of which 10 were waited for; matrix products, arithmetic and copies ran while one was open for 0% of the time, Pallas kernels for 5%

profile of v1, /device:TPU:0, one launch (start us, length us, event | category | flops | bytes accessed | tf_op | source)
XLA Modules:
  0.0 81.6 jit_solution(17517185007220454778)
XLA Ops:
  0.6 1.0 %copy-done = f32[512,256]{1,0:T(8,128)S(1)} copy-done((f32[512,256]{1,0:T(8,128)S(1)}, f32[512,256]{1,0:T(8,128)}, u32[]{:S(2)}) %copy-start) | copy-done | bytes 524312
  1.7 0.5 collective-permute-start.7
  2.2 0.9 %copy-done.3 = f32[128,256]{1,0:T(8,128)S(1)} copy-done((f32[128,256]{1,0:T(8,128)S(1)}, f32[128,256]{1,0:T(8,128)}, u32[]{:S(2)}) %copy-start.3) | copy-done | bytes 131096
  3.1 5.6 %collective-permute-start.6 = (bf16[128,256]{1,0:T(8,128)(2,1)S(1)}, bf16[128,256]{1,0:T(8,128)(2,1)S(1)}, u32[]{:S(2)}, u32[]{:S(2)}) collective-permute-start(bf16[128,256]{1,0:T(8,128)(2,1)S(1)} %shard_map.69.refs_0_), channel_id=1, source_target_pairs={{0,14},{2,12},{4,10},{6,8},{8,6},{10,4},{12,2},{14,0},{1,15},{3,13... | collective-permute-start | bytes 196616 | tf_op jit(solution)/shard_map/ppermute | solution.py:59
  8.8 0.2 collective-permute-start.5
  9.0 0.7 collective-permute-start.4
  9.7 2.0 %collective-permute-start.3 = (bf16[128,256]{1,0:T(8,128)(2,1)S(1)}, bf16[128,256]{1,0:T(8,128)(2,1)S(1)}, u32[]{:S(2)}, u32[]{:S(2)}) collective-permute-start(bf16[128,256]{1,0:T(8,128)(2,1)S(1)} %shard_map.69.refs_0_), channel_id=1, source_target_pairs={{0,8},{2,10},{4,12},{6,14},{8,0},{10,2},{12,4},{14,6},{1,9},{3,11}... | collective-permute-start | bytes 196616 | tf_op jit(solution)/shard_map/ppermute | solution.py:59
  11.8 2.3 %collective-permute-start.2 = (bf16[128,256]{1,0:T(8,128)(2,1)S(1)}, bf16[128,256]{1,0:T(8,128)(2,1)S(1)}, u32[]{:S(2)}, u32[]{:S(2)}) collective-permute-start(bf16[128,256]{1,0:T(8,128)(2,1)S(1)} %shard_map.69.refs_0_), channel_id=1, source_target_pairs={{0,6},{2,4},{4,2},{6,0},{8,14},{10,12},{12,10},{14,8},{1,7},{3,5},... | collective-permute-start | bytes 196616 | tf_op jit(solution)/shard_map/ppermute | solution.py:59
  14.1 1.6 %collective-permute-done.5.refs_6_ = bf16[128,256]{1,0:T(8,128)(2,1)S(1)} collective-permute-done((bf16[128,256]{1,0:T(8,128)(2,1)S(1)}, bf16[128,256]{1,0:T(8,128)(2,1)S(1)}, u32[]{:S(2)}, u32[]{:S(2)}) %collective-permute-start.5) | collective-permute-done | bytes 65568 | tf_op jit(solution)/shard_map/ppermute | solution.py:59
  15.7 2.6 %collective-permute-start.1 = (bf16[128,256]{1,0:T(8,128)(2,1)S(1)}, bf16[128,256]{1,0:T(8,128)(2,1)S(1)}, u32[]{:S(2)}, u32[]{:S(2)}) collective-permute-start(bf16[128,256]{1,0:T(8,128)(2,1)S(1)} %shard_map.69.refs_0_), channel_id=1, source_target_pairs={{0,4},{2,6},{4,0},{6,2},{8,12},{10,14},{12,8},{14,10},{1,5},{3,7},... | collective-permute-start | bytes 196616 | tf_op jit(solution)/shard_map/ppermute | solution.py:59
  18.3 0.7 collective-permute-done.4.refs_5_
  19.0 2.0 %collective-permute-start = (bf16[128,256]{1,0:T(8,128)(2,1)S(1)}, bf16[128,256]{1,0:T(8,128)(2,1)S(1)}, u32[]{:S(2)}, u32[]{:S(2)}) collective-permute-start(bf16[128,256]{1,0:T(8,128)(2,1)S(1)} %shard_map.69.refs_0_), channel_id=1, source_target_pairs={{0,2},{2,0},{4,6},{6,4},{8,10},{10,8},{12,14},{14,12},{1,3},{3,1},... | collective-permute-start | bytes 196616 | tf_op jit(solution)/shard_map/ppermute | solution.py:59
  21.7 1.4 %copy-done.2 = s32[1,1,24,128,128]{4,3,2,1,0:T(8,128)S(1)} copy-done((s32[1,1,24,128,128]{4,3,2,1,0:T(8,128)S(1)}, s32[1,1,24,128,128]{4,3,2,1,0:T(8,128)}, u32[]{:S(2)}) %copy-start.2) | copy-done | bytes 1572888
  23.4 2.6 %shard_map.71 = (bf16[24,128,128]{2,1,0:T(8,128)(2,1)S(1)}, bf16[8,128,256]{2,1,0:T(8,128)(2,1)}, bf16[1024,256]{1,0:T(8,128)(2,1)S(1)}) custom-call(s32[24]{0:T(128)S(1)} %bitcast.8, s32[1]{0:T(128)} %bitcast.3.count, bf16[24,128,128]{2,1,0:T(8,128)(2,1)S(1)} %shard_map.68.sign, bf16[128,256]{1,0:T(8,128)(2,1)S(1)} %shard_map.69.refs_0_, ...), custom_call_target="tpu_custom_call" | custom-call | tf_op jit(solution)/shard_map/pallas_call | solution.py:36
  26.0 6.3 %all-to-all-start = ((bf16[8,128,256]{2,1,0:T(8,128)(2,1)}), bf16[8,128,256]{2,1,0:T(8,128)(2,1)S(1)}, u32[]{:S(2)}, u32[]{:S(2)}) async-start(bf16[8,128,256]{2,1,0:T(8,128)(2,1)} %get-tuple-element.18), calls=%async_computation | async-start | bytes 1048576 | tf_op jit(solution)/shard_map/all_to_all | solution.py:166
  32.3 1.2 %shard_map.73 = (f32[512,256]{1,0:T(8,128)S(1)}, bf16[512,256]{1,0:T(8,128)(2,1)S(1)}) custom-call(s32[24]{0:T(128)S(1)} %bitcast.9, s32[1]{0:T(128)} %bitcast.4.count, bf16[24,128,128]{2,1,0:T(8,128)(2,1)S(1)} %get-tuple-element.21.res, bf16[1024,256]{1,0:T(8,128)(2,1)S(1)} %get-tuple-element.22.stu), custom_call_target="tpu_custom_call" | custom-call | tf_op jit(solution)/shard_map/pallas_call | solution.py:36
  33.6 1.5 %collective-permute-done.15.got = bf16[512,256]{1,0:T(8,128)(2,1)S(1)} collective-permute-done((bf16[512,256]{1,0:T(8,128)(2,1)S(1)}, bf16[512,256]{1,0:T(8,128)(2,1)S(1)}, u32[]{:S(2)}, u32[]{:S(2)}) %collective-permute-start.15) | collective-permute-done | bytes 262176 | tf_op jit(solution)/shard_map/ppermute | solution.py:59
  35.5 10.1 %all-to-all-done.got = bf16[8,128,256]{2,1,0:T(8,128)(2,1)S(1)} async-done(((bf16[8,128,256]{2,1,0:T(8,128)(2,1)}), bf16[8,128,256]{2,1,0:T(8,128)(2,1)S(1)}, u32[]{:S(2)}, u32[]{:S(2)}) %all-to-all-start) | async-done | bytes 524320 | tf_op jit(solution)/shard_map/all_to_all | solution.py:166
  45.7 2.5 %collective-permute-start.14 = (bf16[128,256]{1,0:T(8,128)(2,1)S(1)}, bf16[128,256]{1,0:T(8,128)(2,1)S(1)}, u32[]{:S(2)}, u32[]{:S(2)}) collective-permute-start(bf16[128,256]{1,0:T(8,128)(2,1)S(1)} %get-tuple-element.20.refs_0_), channel_id=1, source_target_pairs={{0,14},{2,12},{4,10},{6,8},{8,6},{10,4},{12,2},{14,0},{1,15},{3,13... | collective-permute-start | bytes 196616 | tf_op jit(solution)/shard_map/ppermute | solution.py:59
  48.2 2.8 %collective-permute-start.13 = (bf16[128,256]{1,0:T(8,128)(2,1)S(1)}, bf16[128,256]{1,0:T(8,128)(2,1)S(1)}, u32[]{:S(2)}, u32[]{:S(2)}) collective-permute-start(bf16[128,256]{1,0:T(8,128)(2,1)S(1)} %get-tuple-element.20.refs_0_), channel_id=1, source_target_pairs={{0,12},{2,14},{4,8},{6,10},{8,4},{10,6},{12,0},{14,2},{1,13},{3,15... | collective-permute-start | bytes 196616 | tf_op jit(solution)/shard_map/ppermute | solution.py:59
  51.0 2.5 %collective-permute-start.11 = (bf16[128,256]{1,0:T(8,128)(2,1)S(1)}, bf16[128,256]{1,0:T(8,128)(2,1)S(1)}, u32[]{:S(2)}, u32[]{:S(2)}) collective-permute-start(bf16[128,256]{1,0:T(8,128)(2,1)S(1)} %get-tuple-element.20.refs_0_), channel_id=1, source_target_pairs={{0,8},{2,10},{4,12},{6,14},{8,0},{10,2},{12,4},{14,6},{1,9},{3,11}... | collective-permute-start | bytes 196616 | tf_op jit(solution)/shard_map/ppermute | solution.py:59
  53.5 3.3 %collective-permute-start.9 = (bf16[128,256]{1,0:T(8,128)(2,1)S(1)}, bf16[128,256]{1,0:T(8,128)(2,1)S(1)}, u32[]{:S(2)}, u32[]{:S(2)}) collective-permute-start(bf16[128,256]{1,0:T(8,128)(2,1)S(1)} %get-tuple-element.20.refs_0_), channel_id=1, source_target_pairs={{0,4},{2,6},{4,0},{6,2},{8,12},{10,14},{12,8},{14,10},{1,5},{3,7},... | collective-permute-start | bytes 196616 | tf_op jit(solution)/shard_map/ppermute | solution.py:59
  56.9 2.0 %collective-permute-done.12.refs_5_ = bf16[128,256]{1,0:T(8,128)(2,1)S(1)} collective-permute-done((bf16[128,256]{1,0:T(8,128)(2,1)S(1)}, bf16[128,256]{1,0:T(8,128)(2,1)S(1)}, u32[]{:S(2)}, u32[]{:S(2)}) %collective-permute-start.12) | collective-permute-done | bytes 65568 | tf_op jit(solution)/shard_map/ppermute | solution.py:59
  59.0 1.0 %collective-permute-done.10.refs_3_ = bf16[128,256]{1,0:T(8,128)(2,1)S(1)} collective-permute-done((bf16[128,256]{1,0:T(8,128)(2,1)S(1)}, bf16[128,256]{1,0:T(8,128)(2,1)S(1)}, u32[]{:S(2)}, u32[]{:S(2)}) %collective-permute-start.10) | collective-permute-done | bytes 65568 | tf_op jit(solution)/shard_map/ppermute | solution.py:59
  60.2 0.9 %collective-permute-done.8.refs_1_ = bf16[128,256]{1,0:T(8,128)(2,1)S(1)} collective-permute-done((bf16[128,256]{1,0:T(8,128)(2,1)S(1)}, bf16[128,256]{1,0:T(8,128)(2,1)S(1)}, u32[]{:S(2)}, u32[]{:S(2)}) %collective-permute-start.8) | collective-permute-done | bytes 65568 | tf_op jit(solution)/shard_map/ppermute | solution.py:59
  61.1 2.6 %shard_map.75 = (bf16[24,128,128]{2,1,0:T(8,128)(2,1)S(1)}, bf16[8,128,256]{2,1,0:T(8,128)(2,1)}, bf16[1024,256]{1,0:T(8,128)(2,1)S(1)}) custom-call(s32[24]{0:T(128)S(1)} %bitcast.10, s32[1]{0:T(128)} %bitcast.5.count, bf16[24,128,128]{2,1,0:T(8,128)(2,1)S(1)} %shard_map.68.sign, bf16[128,256]{1,0:T(8,128)(2,1)S(1)} %get-tuple-element.20.refs_0_, ...), custom_call_target="tpu_custom_call" | custom-call | tf_op jit(solution)/shard_map/pallas_call | solution.py:36
  63.7 3.6 %all-to-all-start.1 = ((bf16[8,128,256]{2,1,0:T(8,128)(2,1)}), bf16[8,128,256]{2,1,0:T(8,128)(2,1)S(1)}, u32[]{:S(2)}, u32[]{:S(2)}) async-start(bf16[8,128,256]{2,1,0:T(8,128)(2,1)} %get-tuple-element.26), calls=%async_computation.1 | async-start | bytes 1048576 | tf_op jit(solution)/shard_map/all_to_all | solution.py:166
  67.3 1.2 %shard_map.77 = (f32[512,256]{1,0:T(8,128)S(1)}, bf16[512,256]{1,0:T(8,128)(2,1)S(1)}) custom-call(s32[24]{0:T(128)S(1)} %bitcast.11, s32[1]{0:T(128)} %bitcast.6.count, bf16[24,128,128]{2,1,0:T(8,128)(2,1)S(1)} %get-tuple-element.29.res, bf16[1024,256]{1,0:T(8,128)(2,1)S(1)} %get-tuple-element.30.stu), custom_call_target="tpu_custom_call" | custom-call | tf_op jit(solution)/shard_map/pallas_call | solution.py:36
  68.6 1.5 %collective-permute-done.17.got = bf16[512,256]{1,0:T(8,128)(2,1)S(1)} collective-permute-done((bf16[512,256]{1,0:T(8,128)(2,1)S(1)}, bf16[512,256]{1,0:T(8,128)(2,1)S(1)}, u32[]{:S(2)}, u32[]{:S(2)}) %collective-permute-start.17) | collective-permute-done | bytes 262176 | tf_op jit(solution)/shard_map/ppermute | solution.py:59
  70.1 1.0 %shard_map.78 = (f32[512,256]{1,0:T(8,128)}, bf16[512,256]{1,0:T(8,128)(2,1)}) custom-call(f32[512,256]{1,0:T(8,128)S(1)} %get-tuple-element.28.own, f32[512,256]{1,0:T(8,128)S(1)} %get-tuple-element.31.keep, bf16[512,256]{1,0:T(8,128)(2,1)S(1)} %collective-permute-done.17.got), custom_call_target="tpu_custom_call" | custom-call | tf_op jit(solution)/shard_map/pallas_call | solution.py:36
  71.2 9.7 %all-to-all-done.1.got = bf16[8,128,256]{2,1,0:T(8,128)(2,1)S(1)} async-done(((bf16[8,128,256]{2,1,0:T(8,128)(2,1)}), bf16[8,128,256]{2,1,0:T(8,128)(2,1)S(1)}, u32[]{:S(2)}, u32[]{:S(2)}) %all-to-all-start.1) | async-done | bytes 524320 | tf_op jit(solution)/shard_map/all_to_all | solution.py:166
  80.9 0.8 shard_map.76
  (31 shorter events, 1.2 us)
Async XLA Ops:
  0.6 1.0 %copy-start = (f32[512,256]{1,0:T(8,128)S(1)}, f32[512,256]{1,0:T(8,128)}, u32[]{:S(2)}) copy-start(f32[512,256]{1,0:T(8,128)} %own.3) | copy-start | bytes 1572868
  1.7 21.7 %copy-start.5 = (s32[1,1,24]{2,1,0:T(1,128)S(1)}, s32[1,1,24]{2,1,0:T(1,128)}, u32[]{:S(2)}) copy-start(s32[1,1,24]{2,1,0:T(1,128)} %param.7) | copy-start | bytes 292
  1.7 21.6 %collective-permute-start.7 = (bf16[512,256]{1,0:T(8,128)(2,1)S(1)}, bf16[512,256]{1,0:T(8,128)(2,1)S(1)}, u32[]{:S(2)}, u32[]{:S(2)}) collective-permute-start(bf16[512,256]{1,0:T(8,128)(2,1)S(1)} %shard_map.70.refs_8_), channel_id=1, source_target_pairs={{0,1},{1,0},{2,3},{3,2},{4,5},{5,4},{6,7},{7,6},{8,9},{9,8},{10,11... | collective-permute-start | bytes 786440 | tf_op jit(solution)/shard_map/ppermute | solution.py:59
  2.2 0.9 %copy-start.3 = (f32[128,256]{1,0:T(8,128)S(1)}, f32[128,256]{1,0:T(8,128)}, u32[]{:S(2)}) copy-start(f32[128,256]{1,0:T(8,128)} %own.2) | copy-start | bytes 393220
  3.1 8.6 %collective-permute-start.6 = (bf16[128,256]{1,0:T(8,128)(2,1)S(1)}, bf16[128,256]{1,0:T(8,128)(2,1)S(1)}, u32[]{:S(2)}, u32[]{:S(2)}) collective-permute-start(bf16[128,256]{1,0:T(8,128)(2,1)S(1)} %shard_map.69.refs_0_), channel_id=1, source_target_pairs={{0,14},{2,12},{4,10},{6,8},{8,6},{10,4},{12,2},{14,0},{1,15},{3,13... | collective-permute-start | bytes 196616 | tf_op jit(solution)/shard_map/ppermute | solution.py:59
  8.8 6.9 %collective-permute-start.5 = (bf16[128,256]{1,0:T(8,128)(2,1)S(1)}, bf16[128,256]{1,0:T(8,128)(2,1)S(1)}, u32[]{:S(2)}, u32[]{:S(2)}) collective-permute-start(bf16[128,256]{1,0:T(8,128)(2,1)S(1)} %shard_map.69.refs_0_), channel_id=1, source_target_pairs={{0,12},{2,14},{4,8},{6,10},{8,4},{10,6},{12,0},{14,2},{1,13},{3,15... | collective-permute-start | bytes 196616 | tf_op jit(solution)/shard_map/ppermute | solution.py:59
  9.0 10.0 %collective-permute-start.4 = (bf16[128,256]{1,0:T(8,128)(2,1)S(1)}, bf16[128,256]{1,0:T(8,128)(2,1)S(1)}, u32[]{:S(2)}, u32[]{:S(2)}) collective-permute-start(bf16[128,256]{1,0:T(8,128)(2,1)S(1)} %shard_map.69.refs_0_), channel_id=1, source_target_pairs={{0,10},{2,8},{4,14},{6,12},{8,2},{10,0},{12,6},{14,4},{1,11},{3,9}... | collective-permute-start | bytes 196616 | tf_op jit(solution)/shard_map/ppermute | solution.py:59
  9.7 13.6 %collective-permute-start.3 = (bf16[128,256]{1,0:T(8,128)(2,1)S(1)}, bf16[128,256]{1,0:T(8,128)(2,1)S(1)}, u32[]{:S(2)}, u32[]{:S(2)}) collective-permute-start(bf16[128,256]{1,0:T(8,128)(2,1)S(1)} %shard_map.69.refs_0_), channel_id=1, source_target_pairs={{0,8},{2,10},{4,12},{6,14},{8,0},{10,2},{12,4},{14,6},{1,9},{3,11}... | collective-permute-start | bytes 196616 | tf_op jit(solution)/shard_map/ppermute | solution.py:59
  11.8 11.5 %collective-permute-start.2 = (bf16[128,256]{1,0:T(8,128)(2,1)S(1)}, bf16[128,256]{1,0:T(8,128)(2,1)S(1)}, u32[]{:S(2)}, u32[]{:S(2)}) collective-permute-start(bf16[128,256]{1,0:T(8,128)(2,1)S(1)} %shard_map.69.refs_0_), channel_id=1, source_target_pairs={{0,6},{2,4},{4,2},{6,0},{8,14},{10,12},{12,10},{14,8},{1,7},{3,5},... | collective-permute-start | bytes 196616 | tf_op jit(solution)/shard_map/ppermute | solution.py:59
  15.7 7.6 %collective-permute-start.1 = (bf16[128,256]{1,0:T(8,128)(2,1)S(1)}, bf16[128,256]{1,0:T(8,128)(2,1)S(1)}, u32[]{:S(2)}, u32[]{:S(2)}) collective-permute-start(bf16[128,256]{1,0:T(8,128)(2,1)S(1)} %shard_map.69.refs_0_), channel_id=1, source_target_pairs={{0,4},{2,6},{4,0},{6,2},{8,12},{10,14},{12,8},{14,10},{1,5},{3,7},... | collective-permute-start | bytes 196616 | tf_op jit(solution)/shard_map/ppermute | solution.py:59
  19.0 4.3 %collective-permute-start = (bf16[128,256]{1,0:T(8,128)(2,1)S(1)}, bf16[128,256]{1,0:T(8,128)(2,1)S(1)}, u32[]{:S(2)}, u32[]{:S(2)}) collective-permute-start(bf16[128,256]{1,0:T(8,128)(2,1)S(1)} %shard_map.69.refs_0_), channel_id=1, source_target_pairs={{0,2},{2,0},{4,6},{6,4},{8,10},{10,8},{12,14},{14,12},{1,3},{3,1},... | collective-permute-start | bytes 196616 | tf_op jit(solution)/shard_map/ppermute | solution.py:59
  21.7 1.4 %copy-start.2 = (s32[1,1,24,128,128]{4,3,2,1,0:T(8,128)S(1)}, s32[1,1,24,128,128]{4,3,2,1,0:T(8,128)}, u32[]{:S(2)}) copy-start(s32[1,1,24,128,128]{4,3,2,1,0:T(8,128)} %param.9) | copy-start | bytes 4718596
  26.0 9.2 %copy-start.1 = (f32[512,256]{1,0:T(8,128)S(1)}, f32[512,256]{1,0:T(8,128)}, u32[]{:S(2)}) copy-start(f32[512,256]{1,0:T(8,128)} %own.3) | copy-start | bytes 1572868
  26.0 19.6 %all-to-all-start = ((bf16[8,128,256]{2,1,0:T(8,128)(2,1)}), bf16[8,128,256]{2,1,0:T(8,128)(2,1)S(1)}, u32[]{:S(2)}, u32[]{:S(2)}) async-start(bf16[8,128,256]{2,1,0:T(8,128)(2,1)} %get-tuple-element.18), calls=%async_computation | async-start | bytes 1048576 | tf_op jit(solution)/shard_map/all_to_all | solution.py:166
  32.3 13.3 %copy-start.4 = (f32[128,256]{1,0:T(8,128)S(1)}, f32[128,256]{1,0:T(8,128)}, u32[]{:S(2)}) copy-start(f32[128,256]{1,0:T(8,128)} %own.2) | copy-start | bytes 393220
  33.6 1.6 %collective-permute-start.15 = (bf16[512,256]{1,0:T(8,128)(2,1)S(1)}, bf16[512,256]{1,0:T(8,128)(2,1)S(1)}, u32[]{:S(2)}, u32[]{:S(2)}) collective-permute-start(bf16[512,256]{1,0:T(8,128)(2,1)S(1)} %get-tuple-element.24), channel_id=1, source_target_pairs={{0,1},{1,0},{2,3},{3,2},{4,5},{5,4},{6,7},{7,6},{8,9},{9,8},{10,11... | collective-permute-start | bytes 786440 | tf_op jit(solution)/shard_map/ppermute | solution.py:59
  35.3 18.1 %collective-permute-start.16 = (bf16[512,256]{1,0:T(8,128)(2,1)S(1)}, bf16[512,256]{1,0:T(8,128)(2,1)S(1)}, u32[]{:S(2)}, u32[]{:S(2)}) collective-permute-start(bf16[512,256]{1,0:T(8,128)(2,1)S(1)} %get-tuple-element.25.refs_8_), channel_id=1, source_target_pairs={{0,1},{1,0},{2,3},{3,2},{4,5},{5,4},{6,7},{7,6},{8,9},{9,8},{10,11... | collective-permute-start | bytes 786440 | tf_op jit(solution)/shard_map/ppermute | solution.py:59
  45.7 7.8 %collective-permute-start.14 = (bf16[128,256]{1,0:T(8,128)(2,1)S(1)}, bf16[128,256]{1,0:T(8,128)(2,1)S(1)}, u32[]{:S(2)}, u32[]{:S(2)}) collective-permute-start(bf16[128,256]{1,0:T(8,128)(2,1)S(1)} %get-tuple-element.20.refs_0_), channel_id=1, source_target_pairs={{0,14},{2,12},{4,10},{6,8},{8,6},{10,4},{12,2},{14,0},{1,15},{3,13... | collective-permute-start | bytes 196616 | tf_op jit(solution)/shard_map/ppermute | solution.py:59
  48.2 8.6 %collective-permute-start.13 = (bf16[128,256]{1,0:T(8,128)(2,1)S(1)}, bf16[128,256]{1,0:T(8,128)(2,1)S(1)}, u32[]{:S(2)}, u32[]{:S(2)}) collective-permute-start(bf16[128,256]{1,0:T(8,128)(2,1)S(1)} %get-tuple-element.20.refs_0_), channel_id=1, source_target_pairs={{0,12},{2,14},{4,8},{6,10},{8,4},{10,6},{12,0},{14,2},{1,13},{3,15... | collective-permute-start | bytes 196616 | tf_op jit(solution)/shard_map/ppermute | solution.py:59
  51.0 8.0 %collective-permute-start.12 = (bf16[128,256]{1,0:T(8,128)(2,1)S(1)}, bf16[128,256]{1,0:T(8,128)(2,1)S(1)}, u32[]{:S(2)}, u32[]{:S(2)}) collective-permute-start(bf16[128,256]{1,0:T(8,128)(2,1)S(1)} %get-tuple-element.20.refs_0_), channel_id=1, source_target_pairs={{0,10},{2,8},{4,14},{6,12},{8,2},{10,0},{12,6},{14,4},{1,11},{3,9}... | collective-permute-start | bytes 196616 | tf_op jit(solution)/shard_map/ppermute | solution.py:59
  51.0 8.0 %collective-permute-start.11 = (bf16[128,256]{1,0:T(8,128)(2,1)S(1)}, bf16[128,256]{1,0:T(8,128)(2,1)S(1)}, u32[]{:S(2)}, u32[]{:S(2)}) collective-permute-start(bf16[128,256]{1,0:T(8,128)(2,1)S(1)} %get-tuple-element.20.refs_0_), channel_id=1, source_target_pairs={{0,8},{2,10},{4,12},{6,14},{8,0},{10,2},{12,4},{14,6},{1,9},{3,11}... | collective-permute-start | bytes 196616 | tf_op jit(solution)/shard_map/ppermute | solution.py:59
  53.4 6.6 %collective-permute-start.10 = (bf16[128,256]{1,0:T(8,128)(2,1)S(1)}, bf16[128,256]{1,0:T(8,128)(2,1)S(1)}, u32[]{:S(2)}, u32[]{:S(2)}) collective-permute-start(bf16[128,256]{1,0:T(8,128)(2,1)S(1)} %get-tuple-element.20.refs_0_), channel_id=1, source_target_pairs={{0,6},{2,4},{4,2},{6,0},{8,14},{10,12},{12,10},{14,8},{1,7},{3,5},... | collective-permute-start | bytes 196616 | tf_op jit(solution)/shard_map/ppermute | solution.py:59
  53.5 6.7 %collective-permute-start.9 = (bf16[128,256]{1,0:T(8,128)(2,1)S(1)}, bf16[128,256]{1,0:T(8,128)(2,1)S(1)}, u32[]{:S(2)}, u32[]{:S(2)}) collective-permute-start(bf16[128,256]{1,0:T(8,128)(2,1)S(1)} %get-tuple-element.20.refs_0_), channel_id=1, source_target_pairs={{0,4},{2,6},{4,0},{6,2},{8,12},{10,14},{12,8},{14,10},{1,5},{3,7},... | collective-permute-start | bytes 196616 | tf_op jit(solution)/shard_map/ppermute | solution.py:59
  56.8 4.3 %collective-permute-start.8 = (bf16[128,256]{1,0:T(8,128)(2,1)S(1)}, bf16[128,256]{1,0:T(8,128)(2,1)S(1)}, u32[]{:S(2)}, u32[]{:S(2)}) collective-permute-start(bf16[128,256]{1,0:T(8,128)(2,1)S(1)} %get-tuple-element.20.refs_0_), channel_id=1, source_target_pairs={{0,2},{2,0},{4,6},{6,4},{8,10},{10,8},{12,14},{14,12},{1,3},{3,1},... | collective-permute-start | bytes 196616 | tf_op jit(solution)/shard_map/ppermute | solution.py:59
  63.7 17.2 %all-to-all-start.1 = ((bf16[8,128,256]{2,1,0:T(8,128)(2,1)}), bf16[8,128,256]{2,1,0:T(8,128)(2,1)S(1)}, u32[]{:S(2)}, u32[]{:S(2)}) async-start(bf16[8,128,256]{2,1,0:T(8,128)(2,1)} %get-tuple-element.26), calls=%async_computation.1 | async-start | bytes 1048576 | tf_op jit(solution)/shard_map/all_to_all | solution.py:166
  68.5 1.6 %collective-permute-start.17 = (bf16[512,256]{1,0:T(8,128)(2,1)S(1)}, bf16[512,256]{1,0:T(8,128)(2,1)S(1)}, u32[]{:S(2)}, u32[]{:S(2)}) collective-permute-start(bf16[512,256]{1,0:T(8,128)(2,1)S(1)} %get-tuple-element.32), channel_id=1, source_target_pairs={{0,1},{1,0},{2,3},{3,2},{4,5},{5,4},{6,7},{7,6},{8,9},{9,8},{10,11... | collective-permute-start | bytes 786440 | tf_op jit(solution)/shard_map/ppermute | solution.py:59

commit v2 on v0

v2 whole, which is shorter than its diff:
```python
import functools
import math

import jax
import jax.numpy as jnp
from jax import lax
from jax.experimental import pallas as pl
from jax.experimental.pallas import tpu as pltpu
from jax.sharding import PartitionSpec as P

ITERS = 2

learn_rate = 0.05
decay_rate = 0.1

F32, BF16 = jnp.float32, jnp.bfloat16
NN = (((1,), (0,)), ((), ()))
NT = (((1,), (1,)), ((), ()))
TN = (((0,), (0,)), ((), ()))


def dot(a, b, dims):
    return lax.dot_general(a, b, dims, preferred_element_type=F32)


def vmem():
    return pl.BlockSpec(memory_space=pltpu.VMEM)


def smem():
    return pl.BlockSpec(memory_space=pltpu.SMEM)


def sds(shape, dtype):
    return jax.ShapeDtypeStruct(tuple(shape), dtype)


def call(body, out_shape, scalars, arrays, scratch=(), cost=10000000000):
    room = sum(
        math.prod(x.shape) * jnp.dtype(x.dtype).itemsize for x in (*out_shape, *arrays, *scratch)
    )
    return pl.pallas_call(
        body,
        out_shape=tuple(out_shape),
        in_specs=[smem()] * len(scalars) + [vmem()] * len(arrays),
        out_specs=(vmem(),) * len(out_shape),
        scratch_shapes=list(scratch),
        cost_estimate=pl.CostEstimate(flops=cost, bytes_accessed=0, transcendentals=0),
        compiler_params=pltpu.CompilerParams(vmem_limit_bytes=room + 4 * 2**20),
    )(*scalars, *arrays)


def swap(x, axis, n, k):
    return lax.ppermute(x, axis, [(i, i ^ k) for i in range(n)])


def window(ref, place, size):
    return ref[pl.ds(pl.multiple_of(place * size, size), size), :]


def cast_body(stu, lvl, stu_low, lvl_low):
    stu_low[...] = stu[...].astype(BF16)
    lvl_low[...] = lvl[...].astype(BF16)


def sign_body(position, count, outcome, sign):
    sign[...] = jnp.zeros_like(sign)

    def step(b, _):
        sign[position[b]] = (1 - 2 * outcome[b]).astype(F32).astype(BF16)
        return 0

    lax.fori_loop(0, count[0], step, 0)


def panel_body(mine, other, panel):
    half, me = mine.shape[0], lax.axis_index("stu")
    panel[pl.ds(pl.multiple_of(me * half, half), half), :] = mine[...]
    panel[pl.ds(pl.multiple_of((me ^ 1) * half, half), half), :] = other[...]


def rows_body(odd, blk, n, *refs):
    parts, (lvl, sign), refs = refs[:n], refs[n : n + 2], refs[n + 2 :]
    res, stu, grads = refs
    own = parts[0].shape[0]
    owned, across = own // blk, lvl.shape[0] // blk
    wide = 2 if across % 2 == 0 else 1
    me = lax.axis_index("lvl")
    for i in range(n):
        stu[i * own : (i + 1) * own, :] = parts[i][...]
    for i in range(n):
        for q in range(owned):
            at = i * own + q * blk
            u = stu[at : at + blk, :]
            first = ((me ^ (2 * i + odd)) * owned + q) * across
            total = None
            for c in range(0, across, wide):
                v = lvl[c * blk : (c + wide) * blk, :]
                t = jnp.tanh(0.5 * dot(u, v, NT))
                twos = []
                for w in range(wide):
                    s = sign[first + c + w].astype(F32)
                    two = jnp.where(s == 0, 0.0, t[:, w * blk : (w + 1) * blk] + s).astype(BF16)
                    res[at : at + blk, (c + w) * blk : (c + w + 1) * blk] = two
                    twos.append(two)
                part = dot(jnp.concatenate(twos, 1), v, NN)
                total = part if total is None else total + part
            rows = slice(q * blk, (q + 1) * blk)
            grads[i, rows, :] = total.astype(grads.dtype)


def add_body(mine, other, *sums):
    for i, total in enumerate(sums):
        total[...] = (mine[i] + other[i].astype(F32)).astype(total.dtype)


def level_body(res0, stu0, res1, stu1, keep, send, acc):
    me, half = lax.axis_index("stu"), keep.shape[0]
    width = acc.shape[0] // 4

    def step(i, _):
        at = pl.ds(pl.multiple_of(i * width, width), width)
        acc[at, :] = dot(res0[:, at], stu0[...], TN) + dot(res1[:, at], stu1[...], TN)
        return 0

    lax.fori_loop(0, 4, step, 0)
    keep[...] = window(acc, me, half)
    send[...] = window(acc, me ^ 1, half).astype(BF16)


def settle_body(n_out, own, *refs):
    got, outs = refs[:-n_out], refs[-n_out:]
    grad = got[0][...].astype(F32)
    for other in got[1:]:
        grad += other[...].astype(F32)
    value = own[...] - learn_rate * (0.5 * grad + decay_rate * own[...])
    for out in outs:
        out[...] = value.astype(out.dtype)


def per_device(n_lvl, n_stu, order, student_factor, level_factor, block_position, block_count, outcome):
    blk, slots = outcome.shape[-1], outcome.shape[2]
    stu_own, lvl_own = student_factor, level_factor
    own, rank = stu_own.shape
    half = lvl_own.shape[0]
    lvl_rows = n_stu * half
    blocks = n_lvl * own // blk * (lvl_rows // blk)
    stu_low, lvl_low = call(
        cast_body, (sds((own, rank), BF16), sds((half, rank), BF16)), (), (stu_own, lvl_own)
    )
    (sign,) = call(
        sign_body,
        [sds((blocks, blk, blk), BF16)],
        (block_position.reshape(-1), block_count.reshape(-1)),
        (outcome.reshape(slots, blk, blk),),
    )
    for step in range(ITERS):
        last = step == ITERS - 1
        kinds = (F32,) if last else (F32, BF16)
        came = {k: swap(stu_low, "lvl", n_lvl, k) for k in order}
        came[0] = stu_low
        (panel,) = call(
            panel_body,
            [sds((lvl_rows, rank), BF16)],
            (),
            (lvl_low, swap(lvl_low, "stu", n_stu, 1)),
        )
        n = n_lvl // 2
        shapes = (sds((n * own, lvl_rows), BF16), sds((n * own, rank), BF16))
        res1, stu1, grad = call(
            functools.partial(rows_body, 1, blk, n),
            (*shapes, sds((n, own, rank), BF16)),
            (),
            (*(came[k] for k in range(1, n_lvl, 2)), panel, sign),
        )
        added = swap(grad, "lvl", n_lvl, 1)
        res0, stu0, grad = call(
            functools.partial(rows_body, 0, blk, n),
            (*shapes, sds((n, own, rank), F32)),
            (),
            (*(came[k] for k in range(0, n_lvl, 2)), panel, sign),
        )
        grads = call(
            add_body,
            (sds((own, rank), F32), *[sds((own, rank), BF16)] * (n - 1)),
            (),
            (grad, added),
        )
        back = [grads[0]] + [swap(grads[i], "lvl", n_lvl, 2 * i) for i in range(1, n)]
        keep, send = call(
            level_body,
            (sds((half, rank), F32), sds((half, rank), BF16)),
            (),
            (res0, stu0, res1, stu1),
            (pltpu.VMEM((lvl_rows, rank), F32),),
        )
        lvl_own, *lows = call(
            functools.partial(settle_body, len(kinds)),
            [sds((half, rank), kind) for kind in kinds],
            (),
            (lvl_own, keep, swap(send, "stu", n_stu, 1)),
        )
        lvl_low = lows[0] if lows else None
        stu_own, *lows = call(
            functools.partial(settle_body, len(kinds)),
            [sds((own, rank), kind) for kind in kinds],
            (),
            (stu_own, *back),
        )
        stu_low = lows[0] if lows else None
    return (stu_own, lvl_own)


def solution(mesh):
    n_lvl, n_stu = mesh.shape["lvl"], mesh.shape["stu"]
    order = sorted(range(1, n_lvl), reverse=True)
    return jax.shard_map(
        functools.partial(per_device, n_lvl, n_stu, order),
        mesh=mesh,
        in_specs=(
            P(("groups", "stu", "lvl"), None),
            P(("groups", "lvl", "stu"), None),
            P(("groups", "stu"), "lvl", None),
            P(("groups", "stu"), "lvl"),
            P(("groups", "stu"), "lvl", None, None, None),
        ),
        out_specs=(P(("groups", "stu", "lvl"), None), P(("groups", "lvl", "stu"), None)),
        check_vma=False,
    )
```

time: 257 us -> 65.3 us (0.25)
  waiting for transfers between devices: 138 us -> 15 us
  blocking collectives: 69.3 us -> 0 us
  starting transfers between devices: 0.16 us -> 34.7 us
  matrix products: 17.3 us -> 0 us
  between operations: 14.6 us -> 1.49 us
  Pallas kernels: 0 us -> 11.8 us
  other arithmetic: 8.16 us -> 0 us
  local copies, waits for them, and re-layouts: 9.37 us -> 2.07 us
    reduce_scatter x4 -> x0, waiting for transfers between devices: 138 us -> none  [the longest x2 131 us: settle(): lax.psum_scatter(grad_stu_panel, 'lvl', scatter_dimension=0, tiled=True)]
    all_gather x4 -> x0, blocking collectives: 69.3 us -> none  [the longest x2 64.8 us: per_device(): lax.all_gather(stu_own.astype(jnp.bfloat16), 'lvl', axis=0, tiled=True)]
    ppermute x0 -> x26, starting transfers between devices: none -> 34.7 us  [swap(): return lax.ppermute(x, axis, [(i, i ^ k) for i in range(n)])]
    dot_general x10 -> x0, matrix products: 17.3 us -> none  [the longest x2 5.66 us: block_grads(): jnp.einsum('bir,bjr->bij', stu_blocks, lvl_blocks, preferred_element_type...]
    ppermute x0 -> x26, waiting for transfers between devices: none -> 15 us  [swap(): return lax.ppermute(x, axis, [(i, i ^ k) for i in range(n)])]
    pallas_call x0 -> x16, Pallas kernels: none -> 11.8 us  [call(): pl.pallas_call(body, out_shape=tuple(out_shape), in_specs=[smem()] * len(...]
    gather x4 -> x0, local copies, waits for them, and re-layouts: 4.98 us -> none  [the longest x2 3.69 us: block_grads(): jnp.take(stu_panel.reshape(down_count, blocksize, rank_width), row_block,...]
    convert_element_type x4 -> x0, other arithmetic: 3.96 us -> none  [the longest x2 2.11 us: per_device(): lvl_own.astype(jnp.bfloat16)]
  transfers between devices with their start and end apart: 4 -> 26, of which waited for: 4 -> 9; matrix products, arithmetic and copies ran while one was open for 5% -> 0% of each run, Pallas kernels for 0% -> 17%
where the time goes in v2:
time: 65.3 us; the launch traced here: 65.1 us
  starting transfers between devices  34.7 us (53%)
  waiting for transfers between devices  15 us (23%)
  Pallas kernels  11.8 us (18%)
  local copies, waits for them, and re-layouts  2.07 us (3%)
  between operations  1.49 us (2%)
    ppermute x26, starting transfers between devices, swap(): return lax.ppermute(x, axis, [(i, i ^ k) for i in range(n)])  34.7 us
    ppermute x26, waiting for transfers between devices, swap(): return lax.ppermute(x, axis, [(i, i ^ k) for i in range(n)])  15 us
    pallas_call x16, Pallas kernels, call(): pl.pallas_call(body, out_shape=tuple(out_shape), in_specs=[smem()] * len(...  11.8 us
    unnamed x12, local copies, waits for them, and re-layouts  2.07 us
  transfers between devices with their start and end apart: 26, of which 9 were waited for; matrix products, arithmetic and copies ran while one was open for 0% of the time, Pallas kernels for 17%

profile of v2, /device:TPU:0, one launch (start us, length us, event | category | flops | bytes accessed | tf_op | source)
XLA Modules:
  0.0 65.1 jit_solution(5781970024584649804)
XLA Ops:
  0.7 1.1 %copy-done.1 = f32[512,256]{1,0:T(8,128)S(1)} copy-done((f32[512,256]{1,0:T(8,128)S(1)}, f32[512,256]{1,0:T(8,128)}, u32[]{:S(2)}) %copy-start.1) | copy-done | bytes 524312
  1.8 0.9 %copy-done.3 = f32[128,256]{1,0:T(8,128)S(1)} copy-done((f32[128,256]{1,0:T(8,128)S(1)}, f32[128,256]{1,0:T(8,128)}, u32[]{:S(2)}) %copy-start.3) | copy-done | bytes 131096
  2.7 6.1 %collective-permute-start.7 = (bf16[128,256]{1,0:T(8,128)(2,1)S(1)}, bf16[128,256]{1,0:T(8,128)(2,1)S(1)}, u32[]{:S(2)}, u32[]{:S(2)}) collective-permute-start(bf16[128,256]{1,0:T(8,128)(2,1)S(1)} %get-tuple-element.32.refs_0_), channel_id=1, source_target_pairs={{0,14},{2,12},{4,10},{6,8},{8,6},{10,4},{12,2},{14,0},{1,15},{3,13... | collective-permute-start | bytes 196616 | tf_op jit(solution)/shard_map/ppermute | solution.py:54
  8.8 1.7 %collective-permute-start.5 = (bf16[128,256]{1,0:T(8,128)(2,1)S(1)}, bf16[128,256]{1,0:T(8,128)(2,1)S(1)}, u32[]{:S(2)}, u32[]{:S(2)}) collective-permute-start(bf16[128,256]{1,0:T(8,128)(2,1)S(1)} %get-tuple-element.32.refs_0_), channel_id=1, source_target_pairs={{0,6},{2,4},{4,2},{6,0},{8,14},{10,12},{12,10},{14,8},{1,7},{3,5},... | collective-permute-start | bytes 196616 | tf_op jit(solution)/shard_map/ppermute | solution.py:54
  11.6 1.0 %shard_map.70.refs_5_ = bf16[64,128,128]{2,1,0:T(8,128)(2,1)S(1)} custom-call(s32[24]{0:T(128)S(1)} %bitcast.5, s32[1]{0:T(128)} %bitcast.3.count, s32[24,128,128]{2,1,0:T(8,128)S(1)} %bitcast.4), custom_call_target="tpu_custom_call" | custom-call | flops 10000000000 | tf_op jit(solution)/shard_map/pallas_call | solution.py:42
  12.6 3.8 %collective-permute-start.2 = (bf16[128,256]{1,0:T(8,128)(2,1)S(1)}, bf16[128,256]{1,0:T(8,128)(2,1)S(1)}, u32[]{:S(2)}, u32[]{:S(2)}) collective-permute-start(bf16[128,256]{1,0:T(8,128)(2,1)S(1)} %get-tuple-element.32.refs_0_), channel_id=1, source_target_pairs={{0,12},{2,14},{4,8},{6,10},{8,4},{10,6},{12,0},{14,2},{1,13},{3,15... | collective-permute-start | bytes 196616 | tf_op jit(solution)/shard_map/ppermute | solution.py:54
  17.2 1.4 %shard_map.72 = (bf16[512,1024]{1,0:T(8,128)(2,1)S(1)}, bf16[512,256]{1,0:T(8,128)(2,1)S(1)}, bf16[4,128,256]{2,1,0:T(8,128)(2,1)S(1)}) custom-call(bf16[128,256]{1,0:T(8,128)(2,1)S(1)} %collective-permute-done.4.refs_0_, bf16[128,256]{1,0:T(8,128)(2,1)S(1)} %collective-permute-done.5.refs_1_, bf16[128,256]{1,0:T(8,128)(2,1)S(1)} %collective-permute-done.6.refs_2_, ...), custom_call_target="tpu_custom_call" | custom-call | flops 10000000000 | tf_op jit(solution)/shard_map/pallas_call | solution.py:42
  18.6 1.7 %collective-permute-start.8 = (bf16[4,128,256]{2,1,0:T(8,128)(2,1)S(1)}, bf16[4,128,256]{2,1,0:T(8,128)(2,1)S(1)}, u32[]{:S(2)}, u32[]{:S(2)}) collective-permute-start(bf16[4,128,256]{2,1,0:T(8,128)(2,1)S(1)} %get-tuple-element.35), channel_id=1, source_target_pairs={{0,2},{2,0},{4,6},{6,4},{8,10},{10,8},{12,14},{14,12},{1,3},{3,1},... | collective-permute-start | bytes 786440 | tf_op jit(solution)/shard_map/ppermute | solution.py:54
  20.3 2.0 %collective-permute-done.1.refs_2_ = bf16[128,256]{1,0:T(8,128)(2,1)S(1)} collective-permute-done((bf16[128,256]{1,0:T(8,128)(2,1)S(1)}, bf16[128,256]{1,0:T(8,128)(2,1)S(1)}, u32[]{:S(2)}, u32[]{:S(2)}) %collective-permute-start.1) | collective-permute-done | bytes 65568 | tf_op jit(solution)/shard_map/ppermute | solution.py:54
  22.4 1.4 %shard_map.71 = (bf16[512,1024]{1,0:T(8,128)(2,1)S(1)}, bf16[512,256]{1,0:T(8,128)(2,1)S(1)}, f32[4,128,256]{2,1,0:T(8,128)S(1)}) custom-call(bf16[128,256]{1,0:T(8,128)(2,1)S(1)} %get-tuple-element.32.refs_0_, bf16[128,256]{1,0:T(8,128)(2,1)S(1)} %collective-permute-done.refs_1_, bf16[128,256]{1,0:T(8,128)(2,1)S(1)} %collective-permute-done.1.refs_2_, ...), custom_call_target="tpu_custom_call" | custom-call | flops 10000000000 | tf_op jit(solution)/shard_map/pallas_call | solution.py:42
  23.8 1.6 %shard_map.75 = (f32[512,256]{1,0:T(8,128)S(1)}, bf16[512,256]{1,0:T(8,128)(2,1)S(1)}) custom-call(bf16[512,1024]{1,0:T(8,128)(2,1)S(1)} %get-tuple-element.42.res0, bf16[512,256]{1,0:T(8,128)(2,1)S(1)} %get-tuple-element.43.stu0, bf16[512,1024]{1,0:T(8,128)(2,1)S(1)} %get-tuple-element.44.res1, bf16[512,256]{1,0:T(8,128)(2,1)S(1)} %get-tuple-element.45.stu1), custom_call_target="tpu_custom_call" | custom-call | flops 10000000000 | tf_op jit(solution)/shard_map/pallas_call | solution.py:42
  25.4 1.1 %collective-permute-done.8.other = bf16[4,128,256]{2,1,0:T(8,128)(2,1)S(1)} collective-permute-done((bf16[4,128,256]{2,1,0:T(8,128)(2,1)S(1)}, bf16[4,128,256]{2,1,0:T(8,128)(2,1)S(1)}, u32[]{:S(2)}, u32[]{:S(2)}) %collective-permute-start.8) | collective-permute-done | bytes 262176 | tf_op jit(solution)/shard_map/ppermute | solution.py:54
  26.6 1.6 %collective-permute-start.9 = (bf16[128,256]{1,0:T(8,128)(2,1)S(1)}, bf16[128,256]{1,0:T(8,128)(2,1)S(1)}, u32[]{:S(2)}, u32[]{:S(2)}) collective-permute-start(bf16[128,256]{1,0:T(8,128)(2,1)S(1)} %get-tuple-element.37), channel_id=1, source_target_pairs={{0,4},{2,6},{4,0},{6,2},{8,12},{10,14},{12,8},{14,10},{1,5},{3,7},... | collective-permute-start | bytes 196616 | tf_op jit(solution)/shard_map/ppermute | solution.py:54
  28.2 2.6 %collective-permute-start.10 = (bf16[128,256]{1,0:T(8,128)(2,1)S(1)}, bf16[128,256]{1,0:T(8,128)(2,1)S(1)}, u32[]{:S(2)}, u32[]{:S(2)}) collective-permute-start(bf16[128,256]{1,0:T(8,128)(2,1)S(1)} %get-tuple-element.38), channel_id=1, source_target_pairs={{0,8},{2,10},{4,12},{6,14},{8,0},{10,2},{12,4},{14,6},{1,9},{3,11}... | collective-permute-start | bytes 196616 | tf_op jit(solution)/shard_map/ppermute | solution.py:54
  31.3 3.5 %collective-permute-done.10.refs_2_ = bf16[128,256]{1,0:T(8,128)(2,1)S(1)} collective-permute-done((bf16[128,256]{1,0:T(8,128)(2,1)S(1)}, bf16[128,256]{1,0:T(8,128)(2,1)S(1)}, u32[]{:S(2)}, u32[]{:S(2)}) %collective-permute-start.10) | collective-permute-done | bytes 65568 | tf_op jit(solution)/shard_map/ppermute | solution.py:54
  34.8 2.1 %collective-permute-done.11.refs_3_ = bf16[128,256]{1,0:T(8,128)(2,1)S(1)} collective-permute-done((bf16[128,256]{1,0:T(8,128)(2,1)S(1)}, bf16[128,256]{1,0:T(8,128)(2,1)S(1)}, u32[]{:S(2)}, u32[]{:S(2)}) %collective-permute-start.11) | collective-permute-done | bytes 65568 | tf_op jit(solution)/shard_map/ppermute | solution.py:54
  37.0 2.1 %collective-permute-start.20 = (bf16[128,256]{1,0:T(8,128)(2,1)S(1)}, bf16[128,256]{1,0:T(8,128)(2,1)S(1)}, u32[]{:S(2)}, u32[]{:S(2)}) collective-permute-start(bf16[128,256]{1,0:T(8,128)(2,1)S(1)} %get-tuple-element.41.refs_0_), channel_id=1, source_target_pairs={{0,14},{2,12},{4,10},{6,8},{8,6},{10,4},{12,2},{14,0},{1,15},{3,13... | collective-permute-start | bytes 196616 | tf_op jit(solution)/shard_map/ppermute | solution.py:54
  39.5 3.8 %collective-permute-start.18 = (bf16[128,256]{1,0:T(8,128)(2,1)S(1)}, bf16[128,256]{1,0:T(8,128)(2,1)S(1)}, u32[]{:S(2)}, u32[]{:S(2)}) collective-permute-start(bf16[128,256]{1,0:T(8,128)(2,1)S(1)} %get-tuple-element.41.refs_0_), channel_id=1, source_target_pairs={{0,6},{2,4},{4,2},{6,0},{8,14},{10,12},{12,10},{14,8},{1,7},{3,5},... | collective-permute-start | bytes 196616 | tf_op jit(solution)/shard_map/ppermute | solution.py:54
  43.8 0.8 %collective-permute-start.14 = (bf16[128,256]{1,0:T(8,128)(2,1)S(1)}, bf16[128,256]{1,0:T(8,128)(2,1)S(1)}, u32[]{:S(2)}, u32[]{:S(2)}) collective-permute-start(bf16[128,256]{1,0:T(8,128)(2,1)S(1)} %get-tuple-element.41.refs_0_), channel_id=1, source_target_pairs={{0,12},{2,14},{4,8},{6,10},{8,4},{10,6},{12,0},{14,2},{1,13},{3,15... | collective-permute-start | bytes 196616 | tf_op jit(solution)/shard_map/ppermute | solution.py:54
  44.6 0.8 %collective-permute-start.13 = (bf16[128,256]{1,0:T(8,128)(2,1)S(1)}, bf16[128,256]{1,0:T(8,128)(2,1)S(1)}, u32[]{:S(2)}, u32[]{:S(2)}) collective-permute-start(bf16[128,256]{1,0:T(8,128)(2,1)S(1)} %get-tuple-element.41.refs_0_), channel_id=1, source_target_pairs={{0,8},{2,10},{4,12},{6,14},{8,0},{10,2},{12,4},{14,6},{1,9},{3,11}... | collective-permute-start | bytes 196616 | tf_op jit(solution)/shard_map/ppermute | solution.py:54
  45.4 1.6 %collective-permute-done.19.refs_2_ = bf16[128,256]{1,0:T(8,128)(2,1)S(1)} collective-permute-done((bf16[128,256]{1,0:T(8,128)(2,1)S(1)}, bf16[128,256]{1,0:T(8,128)(2,1)S(1)}, u32[]{:S(2)}, u32[]{:S(2)}) %collective-permute-start.19) | collective-permute-done | bytes 65568 | tf_op jit(solution)/shard_map/ppermute | solution.py:54
  47.0 1.3 %collective-permute-start.12 = (bf16[128,256]{1,0:T(8,128)(2,1)S(1)}, bf16[128,256]{1,0:T(8,128)(2,1)S(1)}, u32[]{:S(2)}, u32[]{:S(2)}) collective-permute-start(bf16[128,256]{1,0:T(8,128)(2,1)S(1)} %get-tuple-element.41.refs_0_), channel_id=1, source_target_pairs={{0,4},{2,6},{4,0},{6,2},{8,12},{10,14},{12,8},{14,10},{1,5},{3,7},... | collective-permute-start | bytes 196616 | tf_op jit(solution)/shard_map/ppermute | solution.py:54
  48.3 1.4 %shard_map.79 = (bf16[512,1024]{1,0:T(8,128)(2,1)S(1)}, bf16[512,256]{1,0:T(8,128)(2,1)S(1)}, bf16[4,128,256]{2,1,0:T(8,128)(2,1)S(1)}) custom-call(bf16[128,256]{1,0:T(8,128)(2,1)S(1)} %collective-permute-done.17.refs_0_, bf16[128,256]{1,0:T(8,128)(2,1)S(1)} %collective-permute-done.18.refs_1_, bf16[128,256]{1,0:T(8,128)(2,1)S(1)} %collective-permute-done.19.refs_2_, ...), custom_call_target="tpu_custom_call" | custom-call | flops 10000000000 | tf_op jit(solution)/shard_map/pallas_call | solution.py:42
  49.7 1.6 %collective-permute-start.21 = (bf16[4,128,256]{2,1,0:T(8,128)(2,1)S(1)}, bf16[4,128,256]{2,1,0:T(8,128)(2,1)S(1)}, u32[]{:S(2)}, u32[]{:S(2)}) collective-permute-start(bf16[4,128,256]{2,1,0:T(8,128)(2,1)S(1)} %get-tuple-element.50), channel_id=1, source_target_pairs={{0,2},{2,0},{4,6},{6,4},{8,10},{10,8},{12,14},{14,12},{1,3},{3,1},... | collective-permute-start | bytes 786440 | tf_op jit(solution)/shard_map/ppermute | solution.py:54
  51.9 1.4 %shard_map.78 = (bf16[512,1024]{1,0:T(8,128)(2,1)S(1)}, bf16[512,256]{1,0:T(8,128)(2,1)S(1)}, f32[4,128,256]{2,1,0:T(8,128)S(1)}) custom-call(bf16[128,256]{1,0:T(8,128)(2,1)S(1)} %get-tuple-element.41.refs_0_, bf16[128,256]{1,0:T(8,128)(2,1)S(1)} %collective-permute-done.12.refs_1_, bf16[128,256]{1,0:T(8,128)(2,1)S(1)} %collective-permute-done.13.refs_2_, ...), custom_call_target="tpu_custom_call" | custom-call | flops 10000000000 | tf_op jit(solution)/shard_map/pallas_call | solution.py:42
  53.3 1.6 %shard_map.82 = (f32[512,256]{1,0:T(8,128)S(1)}, bf16[512,256]{1,0:T(8,128)(2,1)S(1)}) custom-call(bf16[512,1024]{1,0:T(8,128)(2,1)S(1)} %get-tuple-element.56.res0, bf16[512,256]{1,0:T(8,128)(2,1)S(1)} %get-tuple-element.57.stu0, bf16[512,1024]{1,0:T(8,128)(2,1)S(1)} %get-tuple-element.58.res1, bf16[512,256]{1,0:T(8,128)(2,1)S(1)} %get-tuple-element.59.stu1), custom_call_target="tpu_custom_call" | custom-call | flops 10000000000 | tf_op jit(solution)/shard_map/pallas_call | solution.py:42
  55.0 1.2 %collective-permute-done.21.other = bf16[4,128,256]{2,1,0:T(8,128)(2,1)S(1)} collective-permute-done((bf16[4,128,256]{2,1,0:T(8,128)(2,1)S(1)}, bf16[4,128,256]{2,1,0:T(8,128)(2,1)S(1)}, u32[]{:S(2)}, u32[]{:S(2)}) %collective-permute-start.21) | collective-permute-done | bytes 262176 | tf_op jit(solution)/shard_map/ppermute | solution.py:54
  56.2 0.8 %collective-permute-start.22 = (bf16[128,256]{1,0:T(8,128)(2,1)S(1)}, bf16[128,256]{1,0:T(8,128)(2,1)S(1)}, u32[]{:S(2)}, u32[]{:S(2)}) collective-permute-start(bf16[128,256]{1,0:T(8,128)(2,1)S(1)} %get-tuple-element.52), channel_id=1, source_target_pairs={{0,4},{2,6},{4,0},{6,2},{8,12},{10,14},{12,8},{14,10},{1,5},{3,7},... | collective-permute-start | bytes 196616 | tf_op jit(solution)/shard_map/ppermute | solution.py:54
  57.0 1.1 %collective-permute-start.23 = (bf16[128,256]{1,0:T(8,128)(2,1)S(1)}, bf16[128,256]{1,0:T(8,128)(2,1)S(1)}, u32[]{:S(2)}, u32[]{:S(2)}) collective-permute-start(bf16[128,256]{1,0:T(8,128)(2,1)S(1)} %get-tuple-element.53), channel_id=1, source_target_pairs={{0,8},{2,10},{4,12},{6,14},{8,0},{10,2},{12,4},{14,6},{1,9},{3,11}... | collective-permute-start | bytes 196616 | tf_op jit(solution)/shard_map/ppermute | solution.py:54
  58.1 2.6 %collective-permute-start.24 = (bf16[128,256]{1,0:T(8,128)(2,1)S(1)}, bf16[128,256]{1,0:T(8,128)(2,1)S(1)}, u32[]{:S(2)}, u32[]{:S(2)}) collective-permute-start(bf16[128,256]{1,0:T(8,128)(2,1)S(1)} %get-tuple-element.54), channel_id=1, source_target_pairs={{0,12},{2,14},{4,8},{6,10},{8,4},{10,6},{12,0},{14,2},{1,13},{3,15... | collective-permute-start | bytes 196616 | tf_op jit(solution)/shard_map/ppermute | solution.py:54
  60.7 0.9 %shard_map.83 = f32[512,256]{1,0:T(8,128)} custom-call(f32[512,256]{1,0:T(8,128)S(1)} %get-tuple-element.55.own, f32[512,256]{1,0:T(8,128)S(1)} %get-tuple-element.60.refs_0_, bf16[512,256]{1,0:T(8,128)(2,1)S(1)} %collective-permute-done.25.refs_1_), custom_call_target="tpu_custom_call" | custom-call | flops 10000000000 | tf_op jit(solution)/shard_map/pallas_call | solution.py:42
  61.6 2.8 %collective-permute-done.23.refs_2_ = bf16[128,256]{1,0:T(8,128)(2,1)S(1)} collective-permute-done((bf16[128,256]{1,0:T(8,128)(2,1)S(1)}, bf16[128,256]{1,0:T(8,128)(2,1)S(1)}, u32[]{:S(2)}, u32[]{:S(2)}) %collective-permute-start.23) | collective-permute-done | bytes 65568 | tf_op jit(solution)/shard_map/ppermute | solution.py:54
  (48 shorter events, 4.3 us)
Async XLA Ops:
  0.6 10.9 %copy-start = (s32[1,1,24,128,128]{4,3,2,1,0:T(8,128)S(1)}, s32[1,1,24,128,128]{4,3,2,1,0:T(8,128)}, u32[]{:S(2)}) copy-start(s32[1,1,24,128,128]{4,3,2,1,0:T(8,128)} %param.9) | copy-start | bytes 4718596
  0.6 1.2 %copy-start.1 = (f32[512,256]{1,0:T(8,128)S(1)}, f32[512,256]{1,0:T(8,128)}, u32[]{:S(2)}) copy-start(f32[512,256]{1,0:T(8,128)} %own.3) | copy-start | bytes 1572868
  1.8 0.9 %copy-start.3 = (f32[128,256]{1,0:T(8,128)S(1)}, f32[128,256]{1,0:T(8,128)}, u32[]{:S(2)}) copy-start(f32[128,256]{1,0:T(8,128)} %own.2) | copy-start | bytes 393220
  2.7 8.9 %copy-start.5 = (s32[1,1,24]{2,1,0:T(1,128)S(1)}, s32[1,1,24]{2,1,0:T(1,128)}, u32[]{:S(2)}) copy-start(s32[1,1,24]{2,1,0:T(1,128)} %param.7) | copy-start | bytes 292
  2.7 13.8 %collective-permute-start.7 = (bf16[128,256]{1,0:T(8,128)(2,1)S(1)}, bf16[128,256]{1,0:T(8,128)(2,1)S(1)}, u32[]{:S(2)}, u32[]{:S(2)}) collective-permute-start(bf16[128,256]{1,0:T(8,128)(2,1)S(1)} %get-tuple-element.32.refs_0_), channel_id=1, source_target_pairs={{0,14},{2,12},{4,10},{6,8},{8,6},{10,4},{12,2},{14,0},{1,15},{3,13... | collective-permute-start | bytes 196616 | tf_op jit(solution)/shard_map/ppermute | solution.py:54
  8.8 7.8 %collective-permute-start.6 = (bf16[128,256]{1,0:T(8,128)(2,1)S(1)}, bf16[128,256]{1,0:T(8,128)(2,1)S(1)}, u32[]{:S(2)}, u32[]{:S(2)}) collective-permute-start(bf16[128,256]{1,0:T(8,128)(2,1)S(1)} %get-tuple-element.32.refs_0_), channel_id=1, source_target_pairs={{0,10},{2,8},{4,14},{6,12},{8,2},{10,0},{12,6},{14,4},{1,11},{3,9}... | collective-permute-start | bytes 196616 | tf_op jit(solution)/shard_map/ppermute | solution.py:54
  8.8 8.4 %collective-permute-start.5 = (bf16[128,256]{1,0:T(8,128)(2,1)S(1)}, bf16[128,256]{1,0:T(8,128)(2,1)S(1)}, u32[]{:S(2)}, u32[]{:S(2)}) collective-permute-start(bf16[128,256]{1,0:T(8,128)(2,1)S(1)} %get-tuple-element.32.refs_0_), channel_id=1, source_target_pairs={{0,6},{2,4},{4,2},{6,0},{8,14},{10,12},{12,10},{14,8},{1,7},{3,5},... | collective-permute-start | bytes 196616 | tf_op jit(solution)/shard_map/ppermute | solution.py:54
  10.5 6.7 %collective-permute-start.4 = (bf16[128,256]{1,0:T(8,128)(2,1)S(1)}, bf16[128,256]{1,0:T(8,128)(2,1)S(1)}, u32[]{:S(2)}, u32[]{:S(2)}) collective-permute-start(bf16[128,256]{1,0:T(8,128)(2,1)S(1)} %get-tuple-element.32.refs_0_), channel_id=1, source_target_pairs={{0,2},{2,0},{4,6},{6,4},{8,10},{10,8},{12,14},{14,12},{1,3},{3,1},... | collective-permute-start | bytes 196616 | tf_op jit(solution)/shard_map/ppermute | solution.py:54
  10.9 1.7 %collective-permute-start.3 = (bf16[512,256]{1,0:T(8,128)(2,1)S(1)}, bf16[512,256]{1,0:T(8,128)(2,1)S(1)}, u32[]{:S(2)}, u32[]{:S(2)}) collective-permute-start(bf16[512,256]{1,0:T(8,128)(2,1)S(1)} %get-tuple-element.33.mine), channel_id=1, source_target_pairs={{0,1},{1,0},{2,3},{3,2},{4,5},{5,4},{6,7},{7,6},{8,9},{9,8},{10,11... | collective-permute-start | bytes 786440 | tf_op jit(solution)/shard_map/ppermute | solution.py:54
  12.6 7.7 %collective-permute-start.2 = (bf16[128,256]{1,0:T(8,128)(2,1)S(1)}, bf16[128,256]{1,0:T(8,128)(2,1)S(1)}, u32[]{:S(2)}, u32[]{:S(2)}) collective-permute-start(bf16[128,256]{1,0:T(8,128)(2,1)S(1)} %get-tuple-element.32.refs_0_), channel_id=1, source_target_pairs={{0,12},{2,14},{4,8},{6,10},{8,4},{10,6},{12,0},{14,2},{1,13},{3,15... | collective-permute-start | bytes 196616 | tf_op jit(solution)/shard_map/ppermute | solution.py:54
  16.5 5.8 %collective-permute-start.1 = (bf16[128,256]{1,0:T(8,128)(2,1)S(1)}, bf16[128,256]{1,0:T(8,128)(2,1)S(1)}, u32[]{:S(2)}, u32[]{:S(2)}) collective-permute-start(bf16[128,256]{1,0:T(8,128)(2,1)S(1)} %get-tuple-element.32.refs_0_), channel_id=1, source_target_pairs={{0,8},{2,10},{4,12},{6,14},{8,0},{10,2},{12,4},{14,6},{1,9},{3,11}... | collective-permute-start | bytes 196616 | tf_op jit(solution)/shard_map/ppermute | solution.py:54
  16.6 5.7 %collective-permute-start = (bf16[128,256]{1,0:T(8,128)(2,1)S(1)}, bf16[128,256]{1,0:T(8,128)(2,1)S(1)}, u32[]{:S(2)}, u32[]{:S(2)}) collective-permute-start(bf16[128,256]{1,0:T(8,128)(2,1)S(1)} %get-tuple-element.32.refs_0_), channel_id=1, source_target_pairs={{0,4},{2,6},{4,0},{6,2},{8,12},{10,14},{12,8},{14,10},{1,5},{3,7},... | collective-permute-start | bytes 196616 | tf_op jit(solution)/shard_map/ppermute | solution.py:54
  18.6 8.0 %collective-permute-start.8 = (bf16[4,128,256]{2,1,0:T(8,128)(2,1)S(1)}, bf16[4,128,256]{2,1,0:T(8,128)(2,1)S(1)}, u32[]{:S(2)}, u32[]{:S(2)}) collective-permute-start(bf16[4,128,256]{2,1,0:T(8,128)(2,1)S(1)} %get-tuple-element.35), channel_id=1, source_target_pairs={{0,2},{2,0},{4,6},{6,4},{8,10},{10,8},{12,14},{14,12},{1,3},{3,1},... | collective-permute-start | bytes 786440 | tf_op jit(solution)/shard_map/ppermute | solution.py:54
  25.4 5.7 %collective-permute-start.15 = (bf16[512,256]{1,0:T(8,128)(2,1)S(1)}, bf16[512,256]{1,0:T(8,128)(2,1)S(1)}, u32[]{:S(2)}, u32[]{:S(2)}) collective-permute-start(bf16[512,256]{1,0:T(8,128)(2,1)S(1)} %get-tuple-element.47), channel_id=1, source_target_pairs={{0,1},{1,0},{2,3},{3,2},{4,5},{5,4},{6,7},{7,6},{8,9},{9,8},{10,11... | collective-permute-start | bytes 786440 | tf_op jit(solution)/shard_map/ppermute | solution.py:54
  26.6 4.5 %copy-start.2 = (f32[512,256]{1,0:T(8,128)S(1)}, f32[512,256]{1,0:T(8,128)}, u32[]{:S(2)}) copy-start(f32[512,256]{1,0:T(8,128)} %own.3) | copy-start | bytes 1572868
  26.6 4.7 %collective-permute-start.9 = (bf16[128,256]{1,0:T(8,128)(2,1)S(1)}, bf16[128,256]{1,0:T(8,128)(2,1)S(1)}, u32[]{:S(2)}, u32[]{:S(2)}) collective-permute-start(bf16[128,256]{1,0:T(8,128)(2,1)S(1)} %get-tuple-element.37), channel_id=1, source_target_pairs={{0,4},{2,6},{4,0},{6,2},{8,12},{10,14},{12,8},{14,10},{1,5},{3,7},... | collective-permute-start | bytes 196616 | tf_op jit(solution)/shard_map/ppermute | solution.py:54
  28.2 6.6 %collective-permute-start.10 = (bf16[128,256]{1,0:T(8,128)(2,1)S(1)}, bf16[128,256]{1,0:T(8,128)(2,1)S(1)}, u32[]{:S(2)}, u32[]{:S(2)}) collective-permute-start(bf16[128,256]{1,0:T(8,128)(2,1)S(1)} %get-tuple-element.38), channel_id=1, source_target_pairs={{0,8},{2,10},{4,12},{6,14},{8,0},{10,2},{12,4},{14,6},{1,9},{3,11}... | collective-permute-start | bytes 196616 | tf_op jit(solution)/shard_map/ppermute | solution.py:54
  30.8 6.1 %collective-permute-start.11 = (bf16[128,256]{1,0:T(8,128)(2,1)S(1)}, bf16[128,256]{1,0:T(8,128)(2,1)S(1)}, u32[]{:S(2)}, u32[]{:S(2)}) collective-permute-start(bf16[128,256]{1,0:T(8,128)(2,1)S(1)} %get-tuple-element.39), channel_id=1, source_target_pairs={{0,12},{2,14},{4,8},{6,10},{8,4},{10,6},{12,0},{14,2},{1,13},{3,15... | collective-permute-start | bytes 196616 | tf_op jit(solution)/shard_map/ppermute | solution.py:54
  31.1 5.8 %copy-start.4 = (f32[128,256]{1,0:T(8,128)S(1)}, f32[128,256]{1,0:T(8,128)}, u32[]{:S(2)}) copy-start(f32[128,256]{1,0:T(8,128)} %own.2) | copy-start | bytes 393220
  31.3 12.5 %collective-permute-start.16 = (bf16[512,256]{1,0:T(8,128)(2,1)S(1)}, bf16[512,256]{1,0:T(8,128)(2,1)S(1)}, u32[]{:S(2)}, u32[]{:S(2)}) collective-permute-start(bf16[512,256]{1,0:T(8,128)(2,1)S(1)} %get-tuple-element.48.mine), channel_id=1, source_target_pairs={{0,1},{1,0},{2,3},{3,2},{4,5},{5,4},{6,7},{7,6},{8,9},{9,8},{10,11... | collective-permute-start | bytes 786440 | tf_op jit(solution)/shard_map/ppermute | solution.py:54
  37.0 7.6 %collective-permute-start.20 = (bf16[128,256]{1,0:T(8,128)(2,1)S(1)}, bf16[128,256]{1,0:T(8,128)(2,1)S(1)}, u32[]{:S(2)}, u32[]{:S(2)}) collective-permute-start(bf16[128,256]{1,0:T(8,128)(2,1)S(1)} %get-tuple-element.41.refs_0_), channel_id=1, source_target_pairs={{0,14},{2,12},{4,10},{6,8},{8,6},{10,4},{12,2},{14,0},{1,15},{3,13... | collective-permute-start | bytes 196616 | tf_op jit(solution)/shard_map/ppermute | solution.py:54
  39.1 8.0 %collective-permute-start.19 = (bf16[128,256]{1,0:T(8,128)(2,1)S(1)}, bf16[128,256]{1,0:T(8,128)(2,1)S(1)}, u32[]{:S(2)}, u32[]{:S(2)}) collective-permute-start(bf16[128,256]{1,0:T(8,128)(2,1)S(1)} %get-tuple-element.41.refs_0_), channel_id=1, source_target_pairs={{0,10},{2,8},{4,14},{6,12},{8,2},{10,0},{12,6},{14,4},{1,11},{3,9}... | collective-permute-start | bytes 196616 | tf_op jit(solution)/shard_map/ppermute | solution.py:54
  39.5 8.8 %collective-permute-start.18 = (bf16[128,256]{1,0:T(8,128)(2,1)S(1)}, bf16[128,256]{1,0:T(8,128)(2,1)S(1)}, u32[]{:S(2)}, u32[]{:S(2)}) collective-permute-start(bf16[128,256]{1,0:T(8,128)(2,1)S(1)} %get-tuple-element.41.refs_0_), channel_id=1, source_target_pairs={{0,6},{2,4},{4,2},{6,0},{8,14},{10,12},{12,10},{14,8},{1,7},{3,5},... | collective-permute-start | bytes 196616 | tf_op jit(solution)/shard_map/ppermute | solution.py:54
  43.3 5.0 %collective-permute-start.17 = (bf16[128,256]{1,0:T(8,128)(2,1)S(1)}, bf16[128,256]{1,0:T(8,128)(2,1)S(1)}, u32[]{:S(2)}, u32[]{:S(2)}) collective-permute-start(bf16[128,256]{1,0:T(8,128)(2,1)S(1)} %get-tuple-element.41.refs_0_), channel_id=1, source_target_pairs={{0,2},{2,0},{4,6},{6,4},{8,10},{10,8},{12,14},{14,12},{1,3},{3,1},... | collective-permute-start | bytes 196616 | tf_op jit(solution)/shard_map/ppermute | solution.py:54
  43.8 7.5 %collective-permute-start.14 = (bf16[128,256]{1,0:T(8,128)(2,1)S(1)}, bf16[128,256]{1,0:T(8,128)(2,1)S(1)}, u32[]{:S(2)}, u32[]{:S(2)}) collective-permute-start(bf16[128,256]{1,0:T(8,128)(2,1)S(1)} %get-tuple-element.41.refs_0_), channel_id=1, source_target_pairs={{0,12},{2,14},{4,8},{6,10},{8,4},{10,6},{12,0},{14,2},{1,13},{3,15... | collective-permute-start | bytes 196616 | tf_op jit(solution)/shard_map/ppermute | solution.py:54
  44.6 6.7 %collective-permute-start.13 = (bf16[128,256]{1,0:T(8,128)(2,1)S(1)}, bf16[128,256]{1,0:T(8,128)(2,1)S(1)}, u32[]{:S(2)}, u32[]{:S(2)}) collective-permute-start(bf16[128,256]{1,0:T(8,128)(2,1)S(1)} %get-tuple-element.41.refs_0_), channel_id=1, source_target_pairs={{0,8},{2,10},{4,12},{6,14},{8,0},{10,2},{12,4},{14,6},{1,9},{3,11}... | collective-permute-start | bytes 196616 | tf_op jit(solution)/shard_map/ppermute | solution.py:54
  47.0 4.9 %collective-permute-start.12 = (bf16[128,256]{1,0:T(8,128)(2,1)S(1)}, bf16[128,256]{1,0:T(8,128)(2,1)S(1)}, u32[]{:S(2)}, u32[]{:S(2)}) collective-permute-start(bf16[128,256]{1,0:T(8,128)(2,1)S(1)} %get-tuple-element.41.refs_0_), channel_id=1, source_target_pairs={{0,4},{2,6},{4,0},{6,2},{8,12},{10,14},{12,8},{14,10},{1,5},{3,7},... | collective-permute-start | bytes 196616 | tf_op jit(solution)/shard_map/ppermute | solution.py:54
  49.7 6.4 %collective-permute-start.21 = (bf16[4,128,256]{2,1,0:T(8,128)(2,1)S(1)}, bf16[4,128,256]{2,1,0:T(8,128)(2,1)S(1)}, u32[]{:S(2)}, u32[]{:S(2)}) collective-permute-start(bf16[4,128,256]{2,1,0:T(8,128)(2,1)S(1)} %get-tuple-element.50), channel_id=1, source_target_pairs={{0,2},{2,0},{4,6},{6,4},{8,10},{10,8},{12,14},{14,12},{1,3},{3,1},... | collective-permute-start | bytes 786440 | tf_op jit(solution)/shard_map/ppermute | solution.py:54
  54.9 5.8 %collective-permute-start.25 = (bf16[512,256]{1,0:T(8,128)(2,1)S(1)}, bf16[512,256]{1,0:T(8,128)(2,1)S(1)}, u32[]{:S(2)}, u32[]{:S(2)}) collective-permute-start(bf16[512,256]{1,0:T(8,128)(2,1)S(1)} %get-tuple-element.61), channel_id=1, source_target_pairs={{0,1},{1,0},{2,3},{3,2},{4,5},{5,4},{6,7},{7,6},{8,9},{9,8},{10,11... | collective-permute-start | bytes 786440 | tf_op jit(solution)/shard_map/ppermute | solution.py:54
  56.2 5.4 %collective-permute-start.22 = (bf16[128,256]{1,0:T(8,128)(2,1)S(1)}, bf16[128,256]{1,0:T(8,128)(2,1)S(1)}, u32[]{:S(2)}, u32[]{:S(2)}) collective-permute-start(bf16[128,256]{1,0:T(8,128)(2,1)S(1)} %get-tuple-element.52), channel_id=1, source_target_pairs={{0,4},{2,6},{4,0},{6,2},{8,12},{10,14},{12,8},{14,10},{1,5},{3,7},... | collective-permute-start | bytes 196616 | tf_op jit(solution)/shard_map/ppermute | solution.py:54
  57.0 7.4 %collective-permute-start.23 = (bf16[128,256]{1,0:T(8,128)(2,1)S(1)}, bf16[128,256]{1,0:T(8,128)(2,1)S(1)}, u32[]{:S(2)}, u32[]{:S(2)}) collective-permute-start(bf16[128,256]{1,0:T(8,128)(2,1)S(1)} %get-tuple-element.53), channel_id=1, source_target_pairs={{0,8},{2,10},{4,12},{6,14},{8,0},{10,2},{12,4},{14,6},{1,9},{3,11}... | collective-permute-start | bytes 196616 | tf_op jit(solution)/shard_map/ppermute | solution.py:54
  58.1 6.3 %collective-permute-start.24 = (bf16[128,256]{1,0:T(8,128)(2,1)S(1)}, bf16[128,256]{1,0:T(8,128)(2,1)S(1)}, u32[]{:S(2)}, u32[]{:S(2)}) collective-permute-start(bf16[128,256]{1,0:T(8,128)(2,1)S(1)} %get-tuple-element.54), channel_id=1, source_target_pairs={{0,12},{2,14},{4,8},{6,10},{8,4},{10,6},{12,0},{14,2},{1,13},{3,15... | collective-permute-start | bytes 196616 | tf_op jit(solution)/shard_map/ppermute | solution.py:54

commit v3 on v2

--- a/solution.py
+++ b/solution.py
@@ -9,6 +9,7 @@
 from jax.sharding import PartitionSpec as P
 
 ITERS = 2
+COST = 10**10
 
 learn_rate = 0.05
 decay_rate = 0.1
@@ -35,7 +36,7 @@
     return jax.ShapeDtypeStruct(tuple(shape), dtype)
 
 
-def call(body, out_shape, scalars, arrays, scratch=(), cost=10000000000):
+def call(body, out_shape, scalars, arrays, scratch=()):
     room = sum(
         math.prod(x.shape) * jnp.dtype(x.dtype).itemsize for x in (*out_shape, *arrays, *scratch)
     )
@@ -45,7 +46,7 @@
         in_specs=[smem()] * len(scalars) + [vmem()] * len(arrays),
         out_specs=(vmem(),) * len(out_shape),
         scratch_shapes=list(scratch),
-        cost_estimate=pl.CostEstimate(flops=cost, bytes_accessed=0, transcendentals=0),
+        cost_estimate=pl.CostEstimate(flops=COST, bytes_accessed=0, transcendentals=0),
         compiler_params=pltpu.CompilerParams(vmem_limit_bytes=room + 4 * 2**20),
     )(*scalars, *arrays)
 
@@ -58,9 +59,8 @@
     return ref[pl.ds(pl.multiple_of(place * size, size), size), :]
 
 
-def cast_body(stu, lvl, stu_low, lvl_low):
-    stu_low[...] = stu[...].astype(BF16)
-    lvl_low[...] = lvl[...].astype(BF16)
+def cast_body(rows, low):
+    low[...] = rows[...].astype(BF16)
 
 
 def sign_body(position, count, outcome, sign):
@@ -79,20 +79,25 @@
     panel[pl.ds(pl.multiple_of((me ^ 1) * half, half), half), :] = other[...]
 
 
-def rows_body(odd, blk, n, *refs):
+def turned(n):
+    return [*range(n // 2, n), *range(n // 2)]
+
+
+def rows_body(partners, blk, *refs):
+    n = len(partners)
     parts, (lvl, sign), refs = refs[:n], refs[n : n + 2], refs[n + 2 :]
     res, stu, grads = refs
     own = parts[0].shape[0]
     owned, across = own // blk, lvl.shape[0] // blk
     wide = 2 if across % 2 == 0 else 1
     me = lax.axis_index("lvl")
-    for i in range(n):
-        stu[i * own : (i + 1) * own, :] = parts[i][...]
+    for part, i in zip(parts, turned(n)):
+        stu[i * own : (i + 1) * own, :] = part[...]
     for i in range(n):
         for q in range(owned):
             at = i * own + q * blk
             u = stu[at : at + blk, :]
-            first = ((me ^ (2 * i + odd)) * owned + q) * across
+            first = ((me ^ partners[i]) * owned + q) * across
             total = None
             for c in range(0, across, wide):
                 v = lvl[c * blk : (c + wide) * blk, :]
@@ -114,13 +119,17 @@
         total[...] = (mine[i] + other[i].astype(F32)).astype(total.dtype)
 
 
-def level_body(res0, stu0, res1, stu1, keep, send, acc):
+def level_body(n, *refs):
+    res, stu, (keep, send, acc) = refs[:n], refs[n : 2 * n], refs[2 * n :]
     me, half = lax.axis_index("stu"), keep.shape[0]
     width = acc.shape[0] // 4
 
     def step(i, _):
         at = pl.ds(pl.multiple_of(i * width, width), width)
-        acc[at, :] = dot(res0[:, at], stu0[...], TN) + dot(res1[:, at], stu1[...], TN)
+        total = dot(res[0][:, at], stu[0][...], TN)
+        for i in range(1, n):
+            total += dot(res[i][:, at], stu[i][...], TN)
+        acc[at, :] = total
         return 0
 
     lax.fori_loop(0, 4, step, 0)
@@ -138,16 +147,16 @@
         out[...] = value.astype(out.dtype)
 
 
-def per_device(n_lvl, n_stu, order, student_factor, level_factor, block_position, block_count, outcome):
+def per_device(n_lvl, n_stu, groups, student_factor, level_factor, block_position, block_count, outcome):
     blk, slots = outcome.shape[-1], outcome.shape[2]
     stu_own, lvl_own = student_factor, level_factor
     own, rank = stu_own.shape
     half = lvl_own.shape[0]
     lvl_rows = n_stu * half
     blocks = n_lvl * own // blk * (lvl_rows // blk)
-    stu_low, lvl_low = call(
-        cast_body, (sds((own, rank), BF16), sds((half, rank), BF16)), (), (stu_own, lvl_own)
-    )
+    (stu_low,) = call(cast_body, [sds((own, rank), BF16)], (), (stu_own,))
+    later, _ = lax.optimization_barrier((lvl_own, stu_low))
+    (lvl_low,) = call(cast_body, [sds((half, rank), BF16)], (), (later,))
     (sign,) = call(
         sign_body,
         [sds((blocks, blk, blk), BF16)],
@@ -157,41 +166,43 @@
     for step in range(ITERS):
         last = step == ITERS - 1
         kinds = (F32,) if last else (F32, BF16)
-        came = {k: swap(stu_low, "lvl", n_lvl, k) for k in order}
-        came[0] = stu_low
+        came = {k: swap(stu_low, "lvl", n_lvl, k) if k else stu_low for k in range(n_lvl)}
         (panel,) = call(
             panel_body,
             [sds((lvl_rows, rank), BF16)],
             (),
             (lvl_low, swap(lvl_low, "stu", n_stu, 1)),
         )
-        n = n_lvl // 2
-        shapes = (sds((n * own, lvl_rows), BF16), sds((n * own, rank), BF16))
-        res1, stu1, grad = call(
-            functools.partial(rows_body, 1, blk, n),
-            (*shapes, sds((n, own, rank), BF16)),
-            (),
-            (*(came[k] for k in range(1, n_lvl, 2)), panel, sign),
-        )
-        added = swap(grad, "lvl", n_lvl, 1)
-        res0, stu0, grad = call(
-            functools.partial(rows_body, 0, blk, n),
-            (*shapes, sds((n, own, rank), F32)),
-            (),
-            (*(came[k] for k in range(0, n_lvl, 2)), panel, sign),
-        )
-        grads = call(
-            add_body,
-            (sds((own, rank), F32), *[sds((own, rank), BF16)] * (n - 1)),
-            (),
-            (grad, added),
-        )
-        back = [grads[0]] + [swap(grads[i], "lvl", n_lvl, 2 * i) for i in range(1, n)]
+        back, res, stu = [], [], []
+        for evens in groups:
+            made = []
+            for partners, kind in (([k ^ 1 for k in evens], BF16), (evens, F32)):
+                rows = len(partners) * own
+                *panels, grad = call(
+                    functools.partial(rows_body, partners, blk),
+                    (
+                        sds((rows, lvl_rows), BF16),
+                        sds((rows, rank), BF16),
+                        sds((len(partners), own, rank), kind),
+                    ),
+                    (),
+                    (*(came[partners[i]] for i in turned(len(partners))), panel, sign),
+                )
+                res.append(panels[0])
+                stu.append(panels[1])
+                made.append(grad)
+            sums = call(
+                add_body,
+                [sds((own, rank), BF16 if k else F32) for k in evens],
+                (),
+                (made[1], swap(made[0], "lvl", n_lvl, 1)),
+            )
+            back += [swap(x, "lvl", n_lvl, k) if k else x for k, x in zip(evens, sums)]
         keep, send = call(
-            level_body,
+            functools.partial(level_body, len(res)),
             (sds((half, rank), F32), sds((half, rank), BF16)),
             (),
-            (res0, stu0, res1, stu1),
+            (*res, *stu),
             (pltpu.VMEM((lvl_rows, rank), F32),),
         )
         lvl_own, *lows = call(
@@ -213,9 +224,10 @@
 
 def solution(mesh):
     n_lvl, n_stu = mesh.shape["lvl"], mesh.shape["stu"]
-    order = sorted(range(1, n_lvl), reverse=True)
+    evens = sorted(range(0, n_lvl, 2), reverse=True)
+    groups = (evens,)
     return jax.shard_map(
-        functools.partial(per_device, n_lvl, n_stu, order),
+        functools.partial(per_device, n_lvl, n_stu, groups),
         mesh=mesh,
         in_specs=(
             P(("groups", "stu", "lvl"), None),

time: 65.3 us -> 63.2 us (0.968)
  waiting for transfers between devices: 15 us -> 13.4 us
  local copies, waits for them, and re-layouts: 2.07 us -> 0.98 us
  starting transfers between devices: 34.7 us -> 35.4 us
    ppermute x26, waiting for transfers between devices: 15 us -> 13.4 us  [swap(): return lax.ppermute(x, axis, [(i, i ^ k) for i in range(n)])]
    unnamed x12 -> x10, local copies, waits for them, and re-layouts: 2.07 us -> 0.98 us
    ppermute x26, starting transfers between devices: 34.7 us -> 35.4 us  [swap(): return lax.ppermute(x, axis, [(i, i ^ k) for i in range(n)])]
    pallas_call x16 -> x17, Pallas kernels: 11.8 us -> 11.8 us  [call(): pl.pallas_call(body, out_shape=tuple(out_shape), in_specs=[smem()] * len(...]
  transfers between devices with their start and end apart: 26 -> 26, of which waited for: 9 -> 11; matrix products, arithmetic and copies ran while one was open for 0% -> 0% of each run, Pallas kernels for 17% -> 18%
where the time goes in v3:
time: 63.2 us; the launch traced here: 63.1 us
  starting transfers between devices  35.4 us (56%)
  waiting for transfers between devices  13.4 us (21%)
  Pallas kernels  11.8 us (19%)
  between operations  1.49 us (2%)
  local copies, waits for them, and re-layouts  0.98 us (2%)
    ppermute x26, starting transfers between devices, swap(): return lax.ppermute(x, axis, [(i, i ^ k) for i in range(n)])  35.4 us
    ppermute x26, waiting for transfers between devices, swap(): return lax.ppermute(x, axis, [(i, i ^ k) for i in range(n)])  13.4 us
    pallas_call x17, Pallas kernels, call(): pl.pallas_call(body, out_shape=tuple(out_shape), in_specs=[smem()] * len(...  11.8 us
  transfers between devices with their start and end apart: 26, of which 11 were waited for; matrix products, arithmetic and copies ran while one was open for 0% of the time, Pallas kernels for 18%

profile of v3, /device:TPU:0, one launch (start us, length us, event | category | flops | bytes accessed | tf_op | source)
XLA Modules:
  0.0 63.1 jit_solution(15629595284812652269)
XLA Ops:
  1.6 5.1 %collective-permute-start.7 = (bf16[128,256]{1,0:T(8,128)(2,1)S(1)}, bf16[128,256]{1,0:T(8,128)(2,1)S(1)}, u32[]{:S(2)}, u32[]{:S(2)}) collective-permute-start(bf16[128,256]{1,0:T(8,128)(2,1)S(1)} %shard_map.68.refs_1_), channel_id=1, source_target_pairs={{0,10},{2,8},{4,14},{6,12},{8,2},{10,0},{12,6},{14,4},{1,11},{3,9}... | collective-permute-start | bytes 196616 | tf_op jit(solution)/shard_map/ppermute | solution.py:55
  6.7 1.3 %collective-permute-start.6 = (bf16[128,256]{1,0:T(8,128)(2,1)S(1)}, bf16[128,256]{1,0:T(8,128)(2,1)S(1)}, u32[]{:S(2)}, u32[]{:S(2)}) collective-permute-start(bf16[128,256]{1,0:T(8,128)(2,1)S(1)} %shard_map.68.refs_1_), channel_id=1, source_target_pairs={{0,14},{2,12},{4,10},{6,8},{8,6},{10,4},{12,2},{14,0},{1,15},{3,13... | collective-permute-start | bytes 196616 | tf_op jit(solution)/shard_map/ppermute | solution.py:55
  8.0 1.5 %collective-permute-start.5 = (bf16[128,256]{1,0:T(8,128)(2,1)S(1)}, bf16[128,256]{1,0:T(8,128)(2,1)S(1)}, u32[]{:S(2)}, u32[]{:S(2)}) collective-permute-start(bf16[128,256]{1,0:T(8,128)(2,1)S(1)} %shard_map.68.refs_1_), channel_id=1, source_target_pairs={{0,2},{2,0},{4,6},{6,4},{8,10},{10,8},{12,14},{14,12},{1,3},{3,1},... | collective-permute-start | bytes 196616 | tf_op jit(solution)/shard_map/ppermute | solution.py:55
  10.5 1.0 %shard_map.71.refs_5_ = bf16[64,128,128]{2,1,0:T(8,128)(2,1)S(1)} custom-call(s32[24]{0:T(128)S(1)} %bitcast.5, s32[1]{0:T(128)} %bitcast.3.count, s32[24,128,128]{2,1,0:T(8,128)S(1)} %bitcast.4), custom_call_target="tpu_custom_call" | custom-call | flops 10000000000 | tf_op jit(solution)/shard_map/pallas_call | solution.py:43
  11.6 2.7 %collective-permute-start.2 = (bf16[128,256]{1,0:T(8,128)(2,1)S(1)}, bf16[128,256]{1,0:T(8,128)(2,1)S(1)}, u32[]{:S(2)}, u32[]{:S(2)}) collective-permute-start(bf16[128,256]{1,0:T(8,128)(2,1)S(1)} %shard_map.68.refs_1_), channel_id=1, source_target_pairs={{0,8},{2,10},{4,12},{6,14},{8,0},{10,2},{12,4},{14,6},{1,9},{3,11}... | collective-permute-start | bytes 196616 | tf_op jit(solution)/shard_map/ppermute | solution.py:55
  14.3 1.4 %collective-permute-start.1 = (bf16[128,256]{1,0:T(8,128)(2,1)S(1)}, bf16[128,256]{1,0:T(8,128)(2,1)S(1)}, u32[]{:S(2)}, u32[]{:S(2)}) collective-permute-start(bf16[128,256]{1,0:T(8,128)(2,1)S(1)} %shard_map.68.refs_1_), channel_id=1, source_target_pairs={{0,12},{2,14},{4,8},{6,10},{8,4},{10,6},{12,0},{14,2},{1,13},{3,15... | collective-permute-start | bytes 196616 | tf_op jit(solution)/shard_map/ppermute | solution.py:55
  15.7 1.4 %shard_map.73 = (bf16[512,1024]{1,0:T(8,128)(2,1)S(1)}, bf16[512,256]{1,0:T(8,128)(2,1)S(1)}, bf16[4,128,256]{2,1,0:T(8,128)(2,1)S(1)}) custom-call(bf16[128,256]{1,0:T(8,128)(2,1)S(1)} %collective-permute-done.4.refs_0_, bf16[128,256]{1,0:T(8,128)(2,1)S(1)} %collective-permute-done.5.refs_1_, bf16[128,256]{1,0:T(8,128)(2,1)S(1)} %collective-permute-done.6.refs_2_, ...), custom_call_target="tpu_custom_call" | custom-call | flops 10000000000 | tf_op jit(solution)/shard_map/pallas_call | solution.py:43
  17.1 1.6 %collective-permute-start.8 = (bf16[4,128,256]{2,1,0:T(8,128)(2,1)S(1)}, bf16[4,128,256]{2,1,0:T(8,128)(2,1)S(1)}, u32[]{:S(2)}, u32[]{:S(2)}) collective-permute-start(bf16[4,128,256]{2,1,0:T(8,128)(2,1)S(1)} %get-tuple-element.33), channel_id=1, source_target_pairs={{0,2},{2,0},{4,6},{6,4},{8,10},{10,8},{12,14},{14,12},{1,3},{3,1},... | collective-permute-start | bytes 786440 | tf_op jit(solution)/shard_map/ppermute | solution.py:55
  18.7 2.4 %collective-permute-done.1.refs_2_ = bf16[128,256]{1,0:T(8,128)(2,1)S(1)} collective-permute-done((bf16[128,256]{1,0:T(8,128)(2,1)S(1)}, bf16[128,256]{1,0:T(8,128)(2,1)S(1)}, u32[]{:S(2)}, u32[]{:S(2)}) %collective-permute-start.1) | collective-permute-done | bytes 65568 | tf_op jit(solution)/shard_map/ppermute | solution.py:55
  21.3 1.4 %shard_map.72 = (bf16[512,1024]{1,0:T(8,128)(2,1)S(1)}, bf16[512,256]{1,0:T(8,128)(2,1)S(1)}, f32[4,128,256]{2,1,0:T(8,128)S(1)}) custom-call(bf16[128,256]{1,0:T(8,128)(2,1)S(1)} %collective-permute-done.refs_0_, bf16[128,256]{1,0:T(8,128)(2,1)S(1)} %shard_map.68.refs_1_, bf16[128,256]{1,0:T(8,128)(2,1)S(1)} %collective-permute-done.1.refs_2_, ...), custom_call_target="tpu_custom_call" | custom-call | flops 10000000000 | tf_op jit(solution)/shard_map/pallas_call | solution.py:43
  22.7 1.6 %shard_map.76 = (f32[512,256]{1,0:T(8,128)S(1)}, bf16[512,256]{1,0:T(8,128)(2,1)S(1)}) custom-call(bf16[512,1024]{1,0:T(8,128)(2,1)S(1)} %get-tuple-element.40.refs_0_, bf16[512,1024]{1,0:T(8,128)(2,1)S(1)} %get-tuple-element.41.refs_1_, bf16[512,256]{1,0:T(8,128)(2,1)S(1)} %get-tuple-element.42.refs_2_, bf16[512,256]{1,0:T(8,128)(2,1)S(1)} %get-tuple-element.43.refs_3_), custom_call_target="tpu_custom_call" | custom-call | flops 10000000000 | tf_op jit(solution)/shard_map/pallas_call | solution.py:43
  24.4 1.2 %collective-permute-done.8.other = bf16[4,128,256]{2,1,0:T(8,128)(2,1)S(1)} collective-permute-done((bf16[4,128,256]{2,1,0:T(8,128)(2,1)S(1)}, bf16[4,128,256]{2,1,0:T(8,128)(2,1)S(1)}, u32[]{:S(2)}, u32[]{:S(2)}) %collective-permute-start.8) | collective-permute-done | bytes 262176 | tf_op jit(solution)/shard_map/ppermute | solution.py:55
  25.6 2.4 %collective-permute-start.9 = (bf16[128,256]{1,0:T(8,128)(2,1)S(1)}, bf16[128,256]{1,0:T(8,128)(2,1)S(1)}, u32[]{:S(2)}, u32[]{:S(2)}) collective-permute-start(bf16[128,256]{1,0:T(8,128)(2,1)S(1)} %get-tuple-element.34), channel_id=1, source_target_pairs={{0,12},{2,14},{4,8},{6,10},{8,4},{10,6},{12,0},{14,2},{1,13},{3,15... | collective-permute-start | bytes 196616 | tf_op jit(solution)/shard_map/ppermute | solution.py:55
  28.9 1.2 %collective-permute-start.11 = (bf16[128,256]{1,0:T(8,128)(2,1)S(1)}, bf16[128,256]{1,0:T(8,128)(2,1)S(1)}, u32[]{:S(2)}, u32[]{:S(2)}) collective-permute-start(bf16[128,256]{1,0:T(8,128)(2,1)S(1)} %get-tuple-element.36), channel_id=1, source_target_pairs={{0,4},{2,6},{4,0},{6,2},{8,12},{10,14},{12,8},{14,10},{1,5},{3,7},... | collective-permute-start | bytes 196616 | tf_op jit(solution)/shard_map/ppermute | solution.py:55
  30.3 1.5 %collective-permute-done.9.refs_0_ = bf16[128,256]{1,0:T(8,128)(2,1)S(1)} collective-permute-done((bf16[128,256]{1,0:T(8,128)(2,1)S(1)}, bf16[128,256]{1,0:T(8,128)(2,1)S(1)}, u32[]{:S(2)}, u32[]{:S(2)}) %collective-permute-start.9) | collective-permute-done | bytes 65568 | tf_op jit(solution)/shard_map/ppermute | solution.py:55
  31.8 2.7 %collective-permute-done.10.refs_1_ = bf16[128,256]{1,0:T(8,128)(2,1)S(1)} collective-permute-done((bf16[128,256]{1,0:T(8,128)(2,1)S(1)}, bf16[128,256]{1,0:T(8,128)(2,1)S(1)}, u32[]{:S(2)}, u32[]{:S(2)}) %collective-permute-start.10) | collective-permute-done | bytes 65568 | tf_op jit(solution)/shard_map/ppermute | solution.py:55
  34.6 1.9 %collective-permute-start.20 = (bf16[128,256]{1,0:T(8,128)(2,1)S(1)}, bf16[128,256]{1,0:T(8,128)(2,1)S(1)}, u32[]{:S(2)}, u32[]{:S(2)}) collective-permute-start(bf16[128,256]{1,0:T(8,128)(2,1)S(1)} %get-tuple-element.39.refs_1_), channel_id=1, source_target_pairs={{0,10},{2,8},{4,14},{6,12},{8,2},{10,0},{12,6},{14,4},{1,11},{3,9}... | collective-permute-start | bytes 196616 | tf_op jit(solution)/shard_map/ppermute | solution.py:55
  36.5 1.7 %collective-permute-start.19 = (bf16[128,256]{1,0:T(8,128)(2,1)S(1)}, bf16[128,256]{1,0:T(8,128)(2,1)S(1)}, u32[]{:S(2)}, u32[]{:S(2)}) collective-permute-start(bf16[128,256]{1,0:T(8,128)(2,1)S(1)} %get-tuple-element.39.refs_1_), channel_id=1, source_target_pairs={{0,14},{2,12},{4,10},{6,8},{8,6},{10,4},{12,2},{14,0},{1,15},{3,13... | collective-permute-start | bytes 196616 | tf_op jit(solution)/shard_map/ppermute | solution.py:55
  38.2 1.3 %collective-permute-start.18 = (bf16[128,256]{1,0:T(8,128)(2,1)S(1)}, bf16[128,256]{1,0:T(8,128)(2,1)S(1)}, u32[]{:S(2)}, u32[]{:S(2)}) collective-permute-start(bf16[128,256]{1,0:T(8,128)(2,1)S(1)} %get-tuple-element.39.refs_1_), channel_id=1, source_target_pairs={{0,2},{2,0},{4,6},{6,4},{8,10},{10,8},{12,14},{14,12},{1,3},{3,1},... | collective-permute-start | bytes 196616 | tf_op jit(solution)/shard_map/ppermute | solution.py:55
  39.5 1.1 %collective-permute-start.17 = (bf16[128,256]{1,0:T(8,128)(2,1)S(1)}, bf16[128,256]{1,0:T(8,128)(2,1)S(1)}, u32[]{:S(2)}, u32[]{:S(2)}) collective-permute-start(bf16[128,256]{1,0:T(8,128)(2,1)S(1)} %get-tuple-element.39.refs_1_), channel_id=1, source_target_pairs={{0,6},{2,4},{4,2},{6,0},{8,14},{10,12},{12,10},{14,8},{1,7},{3,5},... | collective-permute-start | bytes 196616 | tf_op jit(solution)/shard_map/ppermute | solution.py:55
  40.5 1.7 %collective-permute-start.14 = (bf16[128,256]{1,0:T(8,128)(2,1)S(1)}, bf16[128,256]{1,0:T(8,128)(2,1)S(1)}, u32[]{:S(2)}, u32[]{:S(2)}) collective-permute-start(bf16[128,256]{1,0:T(8,128)(2,1)S(1)} %get-tuple-element.39.refs_1_), channel_id=1, source_target_pairs={{0,8},{2,10},{4,12},{6,14},{8,0},{10,2},{12,4},{14,6},{1,9},{3,11}... | collective-permute-start | bytes 196616 | tf_op jit(solution)/shard_map/ppermute | solution.py:55
  42.5 2.5 %collective-permute-start.13 = (bf16[128,256]{1,0:T(8,128)(2,1)S(1)}, bf16[128,256]{1,0:T(8,128)(2,1)S(1)}, u32[]{:S(2)}, u32[]{:S(2)}) collective-permute-start(bf16[128,256]{1,0:T(8,128)(2,1)S(1)} %get-tuple-element.39.refs_1_), channel_id=1, source_target_pairs={{0,12},{2,14},{4,8},{6,10},{8,4},{10,6},{12,0},{14,2},{1,13},{3,15... | collective-permute-start | bytes 196616 | tf_op jit(solution)/shard_map/ppermute | solution.py:55
  45.0 1.2 %collective-permute-start.12 = (bf16[128,256]{1,0:T(8,128)(2,1)S(1)}, bf16[128,256]{1,0:T(8,128)(2,1)S(1)}, u32[]{:S(2)}, u32[]{:S(2)}) collective-permute-start(bf16[128,256]{1,0:T(8,128)(2,1)S(1)} %get-tuple-element.39.refs_1_), channel_id=1, source_target_pairs={{0,4},{2,6},{4,0},{6,2},{8,12},{10,14},{12,8},{14,10},{1,5},{3,7},... | collective-permute-start | bytes 196616 | tf_op jit(solution)/shard_map/ppermute | solution.py:55
  46.3 1.4 %shard_map.80 = (bf16[512,1024]{1,0:T(8,128)(2,1)S(1)}, bf16[512,256]{1,0:T(8,128)(2,1)S(1)}, bf16[4,128,256]{2,1,0:T(8,128)(2,1)S(1)}) custom-call(bf16[128,256]{1,0:T(8,128)(2,1)S(1)} %collective-permute-done.17.refs_0_, bf16[128,256]{1,0:T(8,128)(2,1)S(1)} %collective-permute-done.18.refs_1_, bf16[128,256]{1,0:T(8,128)(2,1)S(1)} %collective-permute-done.19.refs_2_, ...), custom_call_target="tpu_custom_call" | custom-call | flops 10000000000 | tf_op jit(solution)/shard_map/pallas_call | solution.py:43
  47.7 1.2 %collective-permute-start.21 = (bf16[4,128,256]{2,1,0:T(8,128)(2,1)S(1)}, bf16[4,128,256]{2,1,0:T(8,128)(2,1)S(1)}, u32[]{:S(2)}, u32[]{:S(2)}) collective-permute-start(bf16[4,128,256]{2,1,0:T(8,128)(2,1)S(1)} %get-tuple-element.48), channel_id=1, source_target_pairs={{0,2},{2,0},{4,6},{6,4},{8,10},{10,8},{12,14},{14,12},{1,3},{3,1},... | collective-permute-start | bytes 786440 | tf_op jit(solution)/shard_map/ppermute | solution.py:55
  49.4 1.4 %shard_map.79 = (bf16[512,1024]{1,0:T(8,128)(2,1)S(1)}, bf16[512,256]{1,0:T(8,128)(2,1)S(1)}, f32[4,128,256]{2,1,0:T(8,128)S(1)}) custom-call(bf16[128,256]{1,0:T(8,128)(2,1)S(1)} %collective-permute-done.12.refs_0_, bf16[128,256]{1,0:T(8,128)(2,1)S(1)} %get-tuple-element.39.refs_1_, bf16[128,256]{1,0:T(8,128)(2,1)S(1)} %collective-permute-done.13.refs_2_, ...), custom_call_target="tpu_custom_call" | custom-call | flops 10000000000 | tf_op jit(solution)/shard_map/pallas_call | solution.py:43
  50.8 1.6 %shard_map.83 = (f32[512,256]{1,0:T(8,128)S(1)}, bf16[512,256]{1,0:T(8,128)(2,1)S(1)}) custom-call(bf16[512,1024]{1,0:T(8,128)(2,1)S(1)} %get-tuple-element.54.refs_0_, bf16[512,1024]{1,0:T(8,128)(2,1)S(1)} %get-tuple-element.55.refs_1_, bf16[512,256]{1,0:T(8,128)(2,1)S(1)} %get-tuple-element.56.refs_2_, bf16[512,256]{1,0:T(8,128)(2,1)S(1)} %get-tuple-element.57.refs_3_), custom_call_target="tpu_custom_call" | custom-call | flops 10000000000 | tf_op jit(solution)/shard_map/pallas_call | solution.py:43
  52.5 1.7 %collective-permute-done.21.other = bf16[4,128,256]{2,1,0:T(8,128)(2,1)S(1)} collective-permute-done((bf16[4,128,256]{2,1,0:T(8,128)(2,1)S(1)}, bf16[4,128,256]{2,1,0:T(8,128)(2,1)S(1)}, u32[]{:S(2)}, u32[]{:S(2)}) %collective-permute-start.21) | collective-permute-done | bytes 262176 | tf_op jit(solution)/shard_map/ppermute | solution.py:55
  54.2 2.8 %collective-permute-start.22 = (bf16[128,256]{1,0:T(8,128)(2,1)S(1)}, bf16[128,256]{1,0:T(8,128)(2,1)S(1)}, u32[]{:S(2)}, u32[]{:S(2)}) collective-permute-start(bf16[128,256]{1,0:T(8,128)(2,1)S(1)} %get-tuple-element.49), channel_id=1, source_target_pairs={{0,12},{2,14},{4,8},{6,10},{8,4},{10,6},{12,0},{14,2},{1,13},{3,15... | collective-permute-start | bytes 196616 | tf_op jit(solution)/shard_map/ppermute | solution.py:55
  57.1 1.6 %collective-permute-start.24 = (bf16[128,256]{1,0:T(8,128)(2,1)S(1)}, bf16[128,256]{1,0:T(8,128)(2,1)S(1)}, u32[]{:S(2)}, u32[]{:S(2)}) collective-permute-start(bf16[128,256]{1,0:T(8,128)(2,1)S(1)} %get-tuple-element.51), channel_id=1, source_target_pairs={{0,4},{2,6},{4,0},{6,2},{8,12},{10,14},{12,8},{14,10},{1,5},{3,7},... | collective-permute-start | bytes 196616 | tf_op jit(solution)/shard_map/ppermute | solution.py:55
  59.6 1.4 %collective-permute-done.22.refs_0_ = bf16[128,256]{1,0:T(8,128)(2,1)S(1)} collective-permute-done((bf16[128,256]{1,0:T(8,128)(2,1)S(1)}, bf16[128,256]{1,0:T(8,128)(2,1)S(1)}, u32[]{:S(2)}, u32[]{:S(2)}) %collective-permute-start.22) | collective-permute-done | bytes 65568 | tf_op jit(solution)/shard_map/ppermute | solution.py:55
  61.0 1.4 %collective-permute-done.23.refs_1_ = bf16[128,256]{1,0:T(8,128)(2,1)S(1)} collective-permute-done((bf16[128,256]{1,0:T(8,128)(2,1)S(1)}, bf16[128,256]{1,0:T(8,128)(2,1)S(1)}, u32[]{:S(2)}, u32[]{:S(2)}) %collective-permute-start.23) | collective-permute-done | bytes 65568 | tf_op jit(solution)/shard_map/ppermute | solution.py:55
  (47 shorter events, 5.4 us)
Async XLA Ops:
  0.6 9.1 %copy-start.1 = (f32[512,256]{1,0:T(8,128)S(1)}, f32[512,256]{1,0:T(8,128)}, u32[]{:S(2)}) copy-start(f32[512,256]{1,0:T(8,128)} %own.3) | copy-start | bytes 1572868
  0.6 1.0 %copy-start.2 = (f32[128,256]{1,0:T(8,128)S(1)}, f32[128,256]{1,0:T(8,128)}, u32[]{:S(2)}) copy-start(f32[128,256]{1,0:T(8,128)} %own.2) | copy-start | bytes 393220
  1.6 8.9 %copy-start = (s32[1,1,24,128,128]{4,3,2,1,0:T(8,128)S(1)}, s32[1,1,24,128,128]{4,3,2,1,0:T(8,128)}, u32[]{:S(2)}) copy-start(s32[1,1,24,128,128]{4,3,2,1,0:T(8,128)} %param.9) | copy-start | bytes 4718596
  1.6 8.9 %copy-start.4 = (s32[1,1,24]{2,1,0:T(1,128)S(1)}, s32[1,1,24]{2,1,0:T(1,128)}, u32[]{:S(2)}) copy-start(s32[1,1,24]{2,1,0:T(1,128)} %param.7) | copy-start | bytes 292
  1.6 12.6 %collective-permute-start.7 = (bf16[128,256]{1,0:T(8,128)(2,1)S(1)}, bf16[128,256]{1,0:T(8,128)(2,1)S(1)}, u32[]{:S(2)}, u32[]{:S(2)}) collective-permute-start(bf16[128,256]{1,0:T(8,128)(2,1)S(1)} %shard_map.68.refs_1_), channel_id=1, source_target_pairs={{0,10},{2,8},{4,14},{6,12},{8,2},{10,0},{12,6},{14,4},{1,11},{3,9}... | collective-permute-start | bytes 196616 | tf_op jit(solution)/shard_map/ppermute | solution.py:55
  6.7 9.0 %collective-permute-start.6 = (bf16[128,256]{1,0:T(8,128)(2,1)S(1)}, bf16[128,256]{1,0:T(8,128)(2,1)S(1)}, u32[]{:S(2)}, u32[]{:S(2)}) collective-permute-start(bf16[128,256]{1,0:T(8,128)(2,1)S(1)} %shard_map.68.refs_1_), channel_id=1, source_target_pairs={{0,14},{2,12},{4,10},{6,8},{8,6},{10,4},{12,2},{14,0},{1,15},{3,13... | collective-permute-start | bytes 196616 | tf_op jit(solution)/shard_map/ppermute | solution.py:55
  8.0 7.7 %collective-permute-start.5 = (bf16[128,256]{1,0:T(8,128)(2,1)S(1)}, bf16[128,256]{1,0:T(8,128)(2,1)S(1)}, u32[]{:S(2)}, u32[]{:S(2)}) collective-permute-start(bf16[128,256]{1,0:T(8,128)(2,1)S(1)} %shard_map.68.refs_1_), channel_id=1, source_target_pairs={{0,2},{2,0},{4,6},{6,4},{8,10},{10,8},{12,14},{14,12},{1,3},{3,1},... | collective-permute-start | bytes 196616 | tf_op jit(solution)/shard_map/ppermute | solution.py:55
  9.5 6.2 %collective-permute-start.4 = (bf16[128,256]{1,0:T(8,128)(2,1)S(1)}, bf16[128,256]{1,0:T(8,128)(2,1)S(1)}, u32[]{:S(2)}, u32[]{:S(2)}) collective-permute-start(bf16[128,256]{1,0:T(8,128)(2,1)S(1)} %shard_map.68.refs_1_), channel_id=1, source_target_pairs={{0,6},{2,4},{4,2},{6,0},{8,14},{10,12},{12,10},{14,8},{1,7},{3,5},... | collective-permute-start | bytes 196616 | tf_op jit(solution)/shard_map/ppermute | solution.py:55
  9.8 1.8 %collective-permute-start.3 = (bf16[512,256]{1,0:T(8,128)(2,1)S(1)}, bf16[512,256]{1,0:T(8,128)(2,1)S(1)}, u32[]{:S(2)}, u32[]{:S(2)}) collective-permute-start(bf16[512,256]{1,0:T(8,128)(2,1)S(1)} %shard_map.69.mine), channel_id=1, source_target_pairs={{0,1},{1,0},{2,3},{3,2},{4,5},{5,4},{6,7},{7,6},{8,9},{9,8},{10,11... | collective-permute-start | bytes 786440 | tf_op jit(solution)/shard_map/ppermute | solution.py:55
  11.6 7.1 %collective-permute-start.2 = (bf16[128,256]{1,0:T(8,128)(2,1)S(1)}, bf16[128,256]{1,0:T(8,128)(2,1)S(1)}, u32[]{:S(2)}, u32[]{:S(2)}) collective-permute-start(bf16[128,256]{1,0:T(8,128)(2,1)S(1)} %shard_map.68.refs_1_), channel_id=1, source_target_pairs={{0,8},{2,10},{4,12},{6,14},{8,0},{10,2},{12,4},{14,6},{1,9},{3,11}... | collective-permute-start | bytes 196616 | tf_op jit(solution)/shard_map/ppermute | solution.py:55
  14.3 6.8 %collective-permute-start.1 = (bf16[128,256]{1,0:T(8,128)(2,1)S(1)}, bf16[128,256]{1,0:T(8,128)(2,1)S(1)}, u32[]{:S(2)}, u32[]{:S(2)}) collective-permute-start(bf16[128,256]{1,0:T(8,128)(2,1)S(1)} %shard_map.68.refs_1_), channel_id=1, source_target_pairs={{0,12},{2,14},{4,8},{6,10},{8,4},{10,6},{12,0},{14,2},{1,13},{3,15... | collective-permute-start | bytes 196616 | tf_op jit(solution)/shard_map/ppermute | solution.py:55
  15.7 5.7 %collective-permute-start = (bf16[128,256]{1,0:T(8,128)(2,1)S(1)}, bf16[128,256]{1,0:T(8,128)(2,1)S(1)}, u32[]{:S(2)}, u32[]{:S(2)}) collective-permute-start(bf16[128,256]{1,0:T(8,128)(2,1)S(1)} %shard_map.68.refs_1_), channel_id=1, source_target_pairs={{0,4},{2,6},{4,0},{6,2},{8,12},{10,14},{12,8},{14,10},{1,5},{3,7},... | collective-permute-start | bytes 196616 | tf_op jit(solution)/shard_map/ppermute | solution.py:55
  17.1 8.5 %collective-permute-start.8 = (bf16[4,128,256]{2,1,0:T(8,128)(2,1)S(1)}, bf16[4,128,256]{2,1,0:T(8,128)(2,1)S(1)}, u32[]{:S(2)}, u32[]{:S(2)}) collective-permute-start(bf16[4,128,256]{2,1,0:T(8,128)(2,1)S(1)} %get-tuple-element.33), channel_id=1, source_target_pairs={{0,2},{2,0},{4,6},{6,4},{8,10},{10,8},{12,14},{14,12},{1,3},{3,1},... | collective-permute-start | bytes 786440 | tf_op jit(solution)/shard_map/ppermute | solution.py:55
  24.3 5.7 %collective-permute-start.15 = (bf16[512,256]{1,0:T(8,128)(2,1)S(1)}, bf16[512,256]{1,0:T(8,128)(2,1)S(1)}, u32[]{:S(2)}, u32[]{:S(2)}) collective-permute-start(bf16[512,256]{1,0:T(8,128)(2,1)S(1)} %get-tuple-element.45), channel_id=1, source_target_pairs={{0,1},{1,0},{2,3},{3,2},{4,5},{5,4},{6,7},{7,6},{8,9},{9,8},{10,11... | collective-permute-start | bytes 786440 | tf_op jit(solution)/shard_map/ppermute | solution.py:55
  25.6 6.2 %collective-permute-start.9 = (bf16[128,256]{1,0:T(8,128)(2,1)S(1)}, bf16[128,256]{1,0:T(8,128)(2,1)S(1)}, u32[]{:S(2)}, u32[]{:S(2)}) collective-permute-start(bf16[128,256]{1,0:T(8,128)(2,1)S(1)} %get-tuple-element.34), channel_id=1, source_target_pairs={{0,12},{2,14},{4,8},{6,10},{8,4},{10,6},{12,0},{14,2},{1,13},{3,15... | collective-permute-start | bytes 196616 | tf_op jit(solution)/shard_map/ppermute | solution.py:55
  28.0 6.5 %collective-permute-start.10 = (bf16[128,256]{1,0:T(8,128)(2,1)S(1)}, bf16[128,256]{1,0:T(8,128)(2,1)S(1)}, u32[]{:S(2)}, u32[]{:S(2)}) collective-permute-start(bf16[128,256]{1,0:T(8,128)(2,1)S(1)} %get-tuple-element.35), channel_id=1, source_target_pairs={{0,8},{2,10},{4,12},{6,14},{8,0},{10,2},{12,4},{14,6},{1,9},{3,11}... | collective-permute-start | bytes 196616 | tf_op jit(solution)/shard_map/ppermute | solution.py:55
  28.9 5.7 %collective-permute-start.11 = (bf16[128,256]{1,0:T(8,128)(2,1)S(1)}, bf16[128,256]{1,0:T(8,128)(2,1)S(1)}, u32[]{:S(2)}, u32[]{:S(2)}) collective-permute-start(bf16[128,256]{1,0:T(8,128)(2,1)S(1)} %get-tuple-element.36), channel_id=1, source_target_pairs={{0,4},{2,6},{4,0},{6,2},{8,12},{10,14},{12,8},{14,10},{1,5},{3,7},... | collective-permute-start | bytes 196616 | tf_op jit(solution)/shard_map/ppermute | solution.py:55
  30.1 4.5 %copy-start.3 = (f32[128,256]{1,0:T(8,128)S(1)}, f32[128,256]{1,0:T(8,128)}, u32[]{:S(2)}) copy-start(f32[128,256]{1,0:T(8,128)} %own.2) | copy-start | bytes 393220
  30.2 10.3 %collective-permute-start.16 = (bf16[512,256]{1,0:T(8,128)(2,1)S(1)}, bf16[512,256]{1,0:T(8,128)(2,1)S(1)}, u32[]{:S(2)}, u32[]{:S(2)}) collective-permute-start(bf16[512,256]{1,0:T(8,128)(2,1)S(1)} %get-tuple-element.46.mine), channel_id=1, source_target_pairs={{0,1},{1,0},{2,3},{3,2},{4,5},{5,4},{6,7},{7,6},{8,9},{9,8},{10,11... | collective-permute-start | bytes 786440 | tf_op jit(solution)/shard_map/ppermute | solution.py:55
  34.6 7.9 %collective-permute-start.20 = (bf16[128,256]{1,0:T(8,128)(2,1)S(1)}, bf16[128,256]{1,0:T(8,128)(2,1)S(1)}, u32[]{:S(2)}, u32[]{:S(2)}) collective-permute-start(bf16[128,256]{1,0:T(8,128)(2,1)S(1)} %get-tuple-element.39.refs_1_), channel_id=1, source_target_pairs={{0,10},{2,8},{4,14},{6,12},{8,2},{10,0},{12,6},{14,4},{1,11},{3,9}... | collective-permute-start | bytes 196616 | tf_op jit(solution)/shard_map/ppermute | solution.py:55
  36.5 8.5 %collective-permute-start.19 = (bf16[128,256]{1,0:T(8,128)(2,1)S(1)}, bf16[128,256]{1,0:T(8,128)(2,1)S(1)}, u32[]{:S(2)}, u32[]{:S(2)}) collective-permute-start(bf16[128,256]{1,0:T(8,128)(2,1)S(1)} %get-tuple-element.39.refs_1_), channel_id=1, source_target_pairs={{0,14},{2,12},{4,10},{6,8},{8,6},{10,4},{12,2},{14,0},{1,15},{3,13... | collective-permute-start | bytes 196616 | tf_op jit(solution)/shard_map/ppermute | solution.py:55
  38.2 8.0 %collective-permute-start.18 = (bf16[128,256]{1,0:T(8,128)(2,1)S(1)}, bf16[128,256]{1,0:T(8,128)(2,1)S(1)}, u32[]{:S(2)}, u32[]{:S(2)}) collective-permute-start(bf16[128,256]{1,0:T(8,128)(2,1)S(1)} %get-tuple-element.39.refs_1_), channel_id=1, source_target_pairs={{0,2},{2,0},{4,6},{6,4},{8,10},{10,8},{12,14},{14,12},{1,3},{3,1},... | collective-permute-start | bytes 196616 | tf_op jit(solution)/shard_map/ppermute | solution.py:55
  39.5 6.9 %collective-permute-start.17 = (bf16[128,256]{1,0:T(8,128)(2,1)S(1)}, bf16[128,256]{1,0:T(8,128)(2,1)S(1)}, u32[]{:S(2)}, u32[]{:S(2)}) collective-permute-start(bf16[128,256]{1,0:T(8,128)(2,1)S(1)} %get-tuple-element.39.refs_1_), channel_id=1, source_target_pairs={{0,6},{2,4},{4,2},{6,0},{8,14},{10,12},{12,10},{14,8},{1,7},{3,5},... | collective-permute-start | bytes 196616 | tf_op jit(solution)/shard_map/ppermute | solution.py:55
  40.5 8.4 %collective-permute-start.14 = (bf16[128,256]{1,0:T(8,128)(2,1)S(1)}, bf16[128,256]{1,0:T(8,128)(2,1)S(1)}, u32[]{:S(2)}, u32[]{:S(2)}) collective-permute-start(bf16[128,256]{1,0:T(8,128)(2,1)S(1)} %get-tuple-element.39.refs_1_), channel_id=1, source_target_pairs={{0,8},{2,10},{4,12},{6,14},{8,0},{10,2},{12,4},{14,6},{1,9},{3,11}... | collective-permute-start | bytes 196616 | tf_op jit(solution)/shard_map/ppermute | solution.py:55
  42.5 6.5 %collective-permute-start.13 = (bf16[128,256]{1,0:T(8,128)(2,1)S(1)}, bf16[128,256]{1,0:T(8,128)(2,1)S(1)}, u32[]{:S(2)}, u32[]{:S(2)}) collective-permute-start(bf16[128,256]{1,0:T(8,128)(2,1)S(1)} %get-tuple-element.39.refs_1_), channel_id=1, source_target_pairs={{0,12},{2,14},{4,8},{6,10},{8,4},{10,6},{12,0},{14,2},{1,13},{3,15... | collective-permute-start | bytes 196616 | tf_op jit(solution)/shard_map/ppermute | solution.py:55
  45.0 4.4 %collective-permute-start.12 = (bf16[128,256]{1,0:T(8,128)(2,1)S(1)}, bf16[128,256]{1,0:T(8,128)(2,1)S(1)}, u32[]{:S(2)}, u32[]{:S(2)}) collective-permute-start(bf16[128,256]{1,0:T(8,128)(2,1)S(1)} %get-tuple-element.39.refs_1_), channel_id=1, source_target_pairs={{0,4},{2,6},{4,0},{6,2},{8,12},{10,14},{12,8},{14,10},{1,5},{3,7},... | collective-permute-start | bytes 196616 | tf_op jit(solution)/shard_map/ppermute | solution.py:55
  47.7 6.4 %collective-permute-start.21 = (bf16[4,128,256]{2,1,0:T(8,128)(2,1)S(1)}, bf16[4,128,256]{2,1,0:T(8,128)(2,1)S(1)}, u32[]{:S(2)}, u32[]{:S(2)}) collective-permute-start(bf16[4,128,256]{2,1,0:T(8,128)(2,1)S(1)} %get-tuple-element.48), channel_id=1, source_target_pairs={{0,2},{2,0},{4,6},{6,4},{8,10},{10,8},{12,14},{14,12},{1,3},{3,1},... | collective-permute-start | bytes 786440 | tf_op jit(solution)/shard_map/ppermute | solution.py:55
  52.4 6.3 %collective-permute-start.25 = (bf16[512,256]{1,0:T(8,128)(2,1)S(1)}, bf16[512,256]{1,0:T(8,128)(2,1)S(1)}, u32[]{:S(2)}, u32[]{:S(2)}) collective-permute-start(bf16[512,256]{1,0:T(8,128)(2,1)S(1)} %get-tuple-element.59), channel_id=1, source_target_pairs={{0,1},{1,0},{2,3},{3,2},{4,5},{5,4},{6,7},{7,6},{8,9},{9,8},{10,11... | collective-permute-start | bytes 786440 | tf_op jit(solution)/shard_map/ppermute | solution.py:55
  54.2 6.8 %collective-permute-start.22 = (bf16[128,256]{1,0:T(8,128)(2,1)S(1)}, bf16[128,256]{1,0:T(8,128)(2,1)S(1)}, u32[]{:S(2)}, u32[]{:S(2)}) collective-permute-start(bf16[128,256]{1,0:T(8,128)(2,1)S(1)} %get-tuple-element.49), channel_id=1, source_target_pairs={{0,12},{2,14},{4,8},{6,10},{8,4},{10,6},{12,0},{14,2},{1,13},{3,15... | collective-permute-start | bytes 196616 | tf_op jit(solution)/shard_map/ppermute | solution.py:55
  57.1 5.3 %collective-permute-start.23 = (bf16[128,256]{1,0:T(8,128)(2,1)S(1)}, bf16[128,256]{1,0:T(8,128)(2,1)S(1)}, u32[]{:S(2)}, u32[]{:S(2)}) collective-permute-start(bf16[128,256]{1,0:T(8,128)(2,1)S(1)} %get-tuple-element.50), channel_id=1, source_target_pairs={{0,8},{2,10},{4,12},{6,14},{8,0},{10,2},{12,4},{14,6},{1,9},{3,11}... | collective-permute-start | bytes 196616 | tf_op jit(solution)/shard_map/ppermute | solution.py:55
  57.1 5.3 %collective-permute-start.24 = (bf16[128,256]{1,0:T(8,128)(2,1)S(1)}, bf16[128,256]{1,0:T(8,128)(2,1)S(1)}, u32[]{:S(2)}, u32[]{:S(2)}) collective-permute-start(bf16[128,256]{1,0:T(8,128)(2,1)S(1)} %get-tuple-element.51), channel_id=1, source_target_pairs={{0,4},{2,6},{4,0},{6,2},{8,12},{10,14},{12,8},{14,10},{1,5},{3,7},... | collective-permute-start | bytes 196616 | tf_op jit(solution)/shard_map/ppermute | solution.py:55

commit v4 on v3

--- a/solution.py
+++ b/solution.py
@@ -9,6 +9,7 @@
 from jax.sharding import PartitionSpec as P
 
 ITERS = 2
+TALL = 2
 COST = 10**10
 
 learn_rate = 0.05
@@ -70,7 +71,7 @@
         sign[position[b]] = (1 - 2 * outcome[b]).astype(F32).astype(BF16)
         return 0
 
-    lax.fori_loop(0, count[0], step, 0)
+    lax.fori_loop(0, count[0, 0], step, 0)
 
 
 def panel_body(mine, other, panel):
@@ -93,25 +94,24 @@
     me = lax.axis_index("lvl")
     for part, i in zip(parts, turned(n)):
         stu[i * own : (i + 1) * own, :] = part[...]
-    for i in range(n):
-        for q in range(owned):
-            at = i * own + q * blk
-            u = stu[at : at + blk, :]
-            first = ((me ^ partners[i]) * owned + q) * across
-            total = None
-            for c in range(0, across, wide):
-                v = lvl[c * blk : (c + wide) * blk, :]
-                t = jnp.tanh(0.5 * dot(u, v, NT))
-                twos = []
+    rows = n * own
+    tall = min(TALL * blk, rows)
+    for at in range(0, rows, tall):
+        u = stu[at : at + tall, :]
+        total = None
+        for c in range(0, across, wide):
+            v = lvl[c * blk : (c + wide) * blk, :]
+            t = jnp.tanh(0.5 * dot(u, v, NT))
+            for g in range(0, tall, blk):
+                i, q = divmod((at + g) // blk, owned)
+                first = ((me ^ partners[i]) * owned + q) * across
                 for w in range(wide):
                     s = sign[first + c + w].astype(F32)
-                    two = jnp.where(s == 0, 0.0, t[:, w * blk : (w + 1) * blk] + s).astype(BF16)
-                    res[at : at + blk, (c + w) * blk : (c + w + 1) * blk] = two
-                    twos.append(two)
-                part = dot(jnp.concatenate(twos, 1), v, NN)
-                total = part if total is None else total + part
-            rows = slice(q * blk, (q + 1) * blk)
-            grads[i, rows, :] = total.astype(grads.dtype)
+                    two = jnp.where(s == 0, 0.0, t[g : g + blk, w * blk : (w + 1) * blk] + s)
+                    res[at + g : at + g + blk, (c + w) * blk : (c + w + 1) * blk] = two.astype(BF16)
+            part = dot(res[at : at + tall, c * blk : (c + wide) * blk], v, NN)
+            total = part if total is None else total + part
+        grads[at // own : (at + tall) // own] = total.astype(grads.dtype).reshape(-1, own, lvl.shape[1])
 
 
 def add_body(mine, other, *sums):
@@ -122,17 +122,10 @@
 def level_body(n, *refs):
     res, stu, (keep, send, acc) = refs[:n], refs[n : 2 * n], refs[2 * n :]
     me, half = lax.axis_index("stu"), keep.shape[0]
-    width = acc.shape[0] // 4
-
-    def step(i, _):
-        at = pl.ds(pl.multiple_of(i * width, width), width)
-        total = dot(res[0][:, at], stu[0][...], TN)
-        for i in range(1, n):
-            total += dot(res[i][:, at], stu[i][...], TN)
-        acc[at, :] = total
-        return 0
-
-    lax.fori_loop(0, 4, step, 0)
+    total = dot(res[0][...], stu[0][...], TN)
+    for i in range(1, n):
+        total += dot(res[i][...], stu[i][...], TN)
+    acc[...] = total
     keep[...] = window(acc, me, half)
     send[...] = window(acc, me ^ 1, half).astype(BF16)
 
@@ -160,7 +153,7 @@
     (sign,) = call(
         sign_body,
         [sds((blocks, blk, blk), BF16)],
-        (block_position.reshape(-1), block_count.reshape(-1)),
+        (block_position.reshape(-1), block_count),
         (outcome.reshape(slots, blk, blk),),
     )
     for step in range(ITERS):

time: 63.2 us -> 61.9 us (0.979)
  Pallas kernels: 11.8 us -> 8.47 us
  waiting for transfers between devices: 13.4 us -> 14.9 us
    pallas_call x17, Pallas kernels: 11.8 us -> 8.47 us  [call(): pl.pallas_call(body, out_shape=tuple(out_shape), in_specs=[smem()] * len(...]
    ppermute x26, waiting for transfers between devices: 13.4 us -> 14.9 us  [swap(): return lax.ppermute(x, axis, [(i, i ^ k) for i in range(n)])]
  transfers between devices with their start and end apart: 26 -> 26, of which waited for: 11 -> 10; matrix products, arithmetic and copies ran while one was open for 0% -> 0% of each run, Pallas kernels for 18% -> 13%
where the time goes in v4:
time: 61.9 us; the launch traced here: 61.7 us
  starting transfers between devices  35.9 us (58%)
  waiting for transfers between devices  14.9 us (24%)
  Pallas kernels  8.47 us (14%)
  between operations  1.5 us (2%)
  local copies, waits for them, and re-layouts  0.98 us (2%)
    ppermute x26, starting transfers between devices, swap(): return lax.ppermute(x, axis, [(i, i ^ k) for i in range(n)])  35.9 us
    ppermute x26, waiting for transfers between devices, swap(): return lax.ppermute(x, axis, [(i, i ^ k) for i in range(n)])  14.9 us
    pallas_call x17, Pallas kernels, call(): pl.pallas_call(body, out_shape=tuple(out_shape), in_specs=[smem()] * len(...  8.47 us
  transfers between devices with their start and end apart: 26, of which 10 were waited for; matrix products, arithmetic and copies ran while one was open for 0% of the time, Pallas kernels for 13%

profile of v4, /device:TPU:0, one launch (start us, length us, event | category | flops | bytes accessed | tf_op | source)
XLA Modules:
  0.0 61.7 jit_solution(2866300912073841040)
XLA Ops:
  0.7 1.0 %copy-done.2 = f32[128,256]{1,0:T(8,128)S(1)} copy-done((f32[128,256]{1,0:T(8,128)S(1)}, f32[128,256]{1,0:T(8,128)}, u32[]{:S(2)}) %copy-start.2) | copy-done | bytes 131096
  1.6 5.1 %collective-permute-start.7 = (bf16[128,256]{1,0:T(8,128)(2,1)S(1)}, bf16[128,256]{1,0:T(8,128)(2,1)S(1)}, u32[]{:S(2)}, u32[]{:S(2)}) collective-permute-start(bf16[128,256]{1,0:T(8,128)(2,1)S(1)} %shard_map.68.refs_1_), channel_id=1, source_target_pairs={{0,10},{2,8},{4,14},{6,12},{8,2},{10,0},{12,6},{14,4},{1,11},{3,9}... | collective-permute-start | bytes 196616 | tf_op jit(solution)/shard_map/ppermute | solution.py:56
  6.7 1.3 %collective-permute-start.6 = (bf16[128,256]{1,0:T(8,128)(2,1)S(1)}, bf16[128,256]{1,0:T(8,128)(2,1)S(1)}, u32[]{:S(2)}, u32[]{:S(2)}) collective-permute-start(bf16[128,256]{1,0:T(8,128)(2,1)S(1)} %shard_map.68.refs_1_), channel_id=1, source_target_pairs={{0,14},{2,12},{4,10},{6,8},{8,6},{10,4},{12,2},{14,0},{1,15},{3,13... | collective-permute-start | bytes 196616 | tf_op jit(solution)/shard_map/ppermute | solution.py:56
  8.0 1.5 %collective-permute-start.5 = (bf16[128,256]{1,0:T(8,128)(2,1)S(1)}, bf16[128,256]{1,0:T(8,128)(2,1)S(1)}, u32[]{:S(2)}, u32[]{:S(2)}) collective-permute-start(bf16[128,256]{1,0:T(8,128)(2,1)S(1)} %shard_map.68.refs_1_), channel_id=1, source_target_pairs={{0,2},{2,0},{4,6},{6,4},{8,10},{10,8},{12,14},{14,12},{1,3},{3,1},... | collective-permute-start | bytes 196616 | tf_op jit(solution)/shard_map/ppermute | solution.py:56
  10.5 0.9 %shard_map.71.refs_5_ = bf16[64,128,128]{2,1,0:T(8,128)(2,1)S(1)} custom-call(s32[24]{0:T(128)S(1)} %bitcast.3, s32[1,1]{1,0:T(1,128)S(6)} %copy.7.count, s32[24,128,128]{2,1,0:T(8,128)S(1)} %bitcast.2), custom_call_target="tpu_custom_call" | custom-call | flops 10000000000 | tf_op jit(solution)/shard_map/pallas_call | solution.py:44
  11.4 2.8 %collective-permute-start.2 = (bf16[128,256]{1,0:T(8,128)(2,1)S(1)}, bf16[128,256]{1,0:T(8,128)(2,1)S(1)}, u32[]{:S(2)}, u32[]{:S(2)}) collective-permute-start(bf16[128,256]{1,0:T(8,128)(2,1)S(1)} %shard_map.68.refs_1_), channel_id=1, source_target_pairs={{0,8},{2,10},{4,12},{6,14},{8,0},{10,2},{12,4},{14,6},{1,9},{3,11}... | collective-permute-start | bytes 196616 | tf_op jit(solution)/shard_map/ppermute | solution.py:56
  14.2 1.7 %collective-permute-start.1 = (bf16[128,256]{1,0:T(8,128)(2,1)S(1)}, bf16[128,256]{1,0:T(8,128)(2,1)S(1)}, u32[]{:S(2)}, u32[]{:S(2)}) collective-permute-start(bf16[128,256]{1,0:T(8,128)(2,1)S(1)} %shard_map.68.refs_1_), channel_id=1, source_target_pairs={{0,12},{2,14},{4,8},{6,10},{8,4},{10,6},{12,0},{14,2},{1,13},{3,15... | collective-permute-start | bytes 196616 | tf_op jit(solution)/shard_map/ppermute | solution.py:56
  16.0 1.0 %shard_map.73 = (bf16[512,1024]{1,0:T(8,128)(2,1)S(1)}, bf16[512,256]{1,0:T(8,128)(2,1)S(1)}, bf16[4,128,256]{2,1,0:T(8,128)(2,1)S(1)}) custom-call(bf16[128,256]{1,0:T(8,128)(2,1)S(1)} %collective-permute-done.4.refs_0_, bf16[128,256]{1,0:T(8,128)(2,1)S(1)} %collective-permute-done.5.refs_1_, bf16[128,256]{1,0:T(8,128)(2,1)S(1)} %collective-permute-done.6.refs_2_, ...), custom_call_target="tpu_custom_call" | custom-call | flops 10000000000 | tf_op jit(solution)/shard_map/pallas_call | solution.py:44
  17.0 1.5 %collective-permute-start.8 = (bf16[4,128,256]{2,1,0:T(8,128)(2,1)S(1)}, bf16[4,128,256]{2,1,0:T(8,128)(2,1)S(1)}, u32[]{:S(2)}, u32[]{:S(2)}) collective-permute-start(bf16[4,128,256]{2,1,0:T(8,128)(2,1)S(1)} %get-tuple-element.33), channel_id=1, source_target_pairs={{0,2},{2,0},{4,6},{6,4},{8,10},{10,8},{12,14},{14,12},{1,3},{3,1},... | collective-permute-start | bytes 786440 | tf_op jit(solution)/shard_map/ppermute | solution.py:56
  18.7 2.4 %collective-permute-done.1.refs_2_ = bf16[128,256]{1,0:T(8,128)(2,1)S(1)} collective-permute-done((bf16[128,256]{1,0:T(8,128)(2,1)S(1)}, bf16[128,256]{1,0:T(8,128)(2,1)S(1)}, u32[]{:S(2)}, u32[]{:S(2)}) %collective-permute-start.1) | collective-permute-done | bytes 65568 | tf_op jit(solution)/shard_map/ppermute | solution.py:56
  21.3 1.0 %shard_map.72 = (bf16[512,1024]{1,0:T(8,128)(2,1)S(1)}, bf16[512,256]{1,0:T(8,128)(2,1)S(1)}, f32[4,128,256]{2,1,0:T(8,128)S(1)}) custom-call(bf16[128,256]{1,0:T(8,128)(2,1)S(1)} %collective-permute-done.refs_0_, bf16[128,256]{1,0:T(8,128)(2,1)S(1)} %shard_map.68.refs_1_, bf16[128,256]{1,0:T(8,128)(2,1)S(1)} %collective-permute-done.1.refs_2_, ...), custom_call_target="tpu_custom_call" | custom-call | flops 10000000000 | tf_op jit(solution)/shard_map/pallas_call | solution.py:44
  23.2 1.8 %collective-permute-done.8.other = bf16[4,128,256]{2,1,0:T(8,128)(2,1)S(1)} collective-permute-done((bf16[4,128,256]{2,1,0:T(8,128)(2,1)S(1)}, bf16[4,128,256]{2,1,0:T(8,128)(2,1)S(1)}, u32[]{:S(2)}, u32[]{:S(2)}) %collective-permute-start.8) | collective-permute-done | bytes 262176 | tf_op jit(solution)/shard_map/ppermute | solution.py:56
  25.1 2.5 %collective-permute-start.9 = (bf16[128,256]{1,0:T(8,128)(2,1)S(1)}, bf16[128,256]{1,0:T(8,128)(2,1)S(1)}, u32[]{:S(2)}, u32[]{:S(2)}) collective-permute-start(bf16[128,256]{1,0:T(8,128)(2,1)S(1)} %get-tuple-element.34), channel_id=1, source_target_pairs={{0,12},{2,14},{4,8},{6,10},{8,4},{10,6},{12,0},{14,2},{1,13},{3,15... | collective-permute-start | bytes 196616 | tf_op jit(solution)/shard_map/ppermute | solution.py:56
  28.3 1.2 %collective-permute-start.11 = (bf16[128,256]{1,0:T(8,128)(2,1)S(1)}, bf16[128,256]{1,0:T(8,128)(2,1)S(1)}, u32[]{:S(2)}, u32[]{:S(2)}) collective-permute-start(bf16[128,256]{1,0:T(8,128)(2,1)S(1)} %get-tuple-element.36), channel_id=1, source_target_pairs={{0,4},{2,6},{4,0},{6,2},{8,12},{10,14},{12,8},{14,10},{1,5},{3,7},... | collective-permute-start | bytes 196616 | tf_op jit(solution)/shard_map/ppermute | solution.py:56
  29.8 1.9 %collective-permute-done.9.refs_0_ = bf16[128,256]{1,0:T(8,128)(2,1)S(1)} collective-permute-done((bf16[128,256]{1,0:T(8,128)(2,1)S(1)}, bf16[128,256]{1,0:T(8,128)(2,1)S(1)}, u32[]{:S(2)}, u32[]{:S(2)}) %collective-permute-start.9) | collective-permute-done | bytes 65568 | tf_op jit(solution)/shard_map/ppermute | solution.py:56
  31.7 2.4 %collective-permute-done.10.refs_1_ = bf16[128,256]{1,0:T(8,128)(2,1)S(1)} collective-permute-done((bf16[128,256]{1,0:T(8,128)(2,1)S(1)}, bf16[128,256]{1,0:T(8,128)(2,1)S(1)}, u32[]{:S(2)}, u32[]{:S(2)}) %collective-permute-start.10) | collective-permute-done | bytes 65568 | tf_op jit(solution)/shard_map/ppermute | solution.py:56
  34.2 1.7 %collective-permute-start.20 = (bf16[128,256]{1,0:T(8,128)(2,1)S(1)}, bf16[128,256]{1,0:T(8,128)(2,1)S(1)}, u32[]{:S(2)}, u32[]{:S(2)}) collective-permute-start(bf16[128,256]{1,0:T(8,128)(2,1)S(1)} %get-tuple-element.39.refs_1_), channel_id=1, source_target_pairs={{0,10},{2,8},{4,14},{6,12},{8,2},{10,0},{12,6},{14,4},{1,11},{3,9}... | collective-permute-start | bytes 196616 | tf_op jit(solution)/shard_map/ppermute | solution.py:56
  35.9 1.4 %collective-permute-start.19 = (bf16[128,256]{1,0:T(8,128)(2,1)S(1)}, bf16[128,256]{1,0:T(8,128)(2,1)S(1)}, u32[]{:S(2)}, u32[]{:S(2)}) collective-permute-start(bf16[128,256]{1,0:T(8,128)(2,1)S(1)} %get-tuple-element.39.refs_1_), channel_id=1, source_target_pairs={{0,14},{2,12},{4,10},{6,8},{8,6},{10,4},{12,2},{14,0},{1,15},{3,13... | collective-permute-start | bytes 196616 | tf_op jit(solution)/shard_map/ppermute | solution.py:56
  37.3 1.5 %collective-permute-start.18 = (bf16[128,256]{1,0:T(8,128)(2,1)S(1)}, bf16[128,256]{1,0:T(8,128)(2,1)S(1)}, u32[]{:S(2)}, u32[]{:S(2)}) collective-permute-start(bf16[128,256]{1,0:T(8,128)(2,1)S(1)} %get-tuple-element.39.refs_1_), channel_id=1, source_target_pairs={{0,2},{2,0},{4,6},{6,4},{8,10},{10,8},{12,14},{14,12},{1,3},{3,1},... | collective-permute-start | bytes 196616 | tf_op jit(solution)/shard_map/ppermute | solution.py:56
  38.8 1.3 %collective-permute-start.17 = (bf16[128,256]{1,0:T(8,128)(2,1)S(1)}, bf16[128,256]{1,0:T(8,128)(2,1)S(1)}, u32[]{:S(2)}, u32[]{:S(2)}) collective-permute-start(bf16[128,256]{1,0:T(8,128)(2,1)S(1)} %get-tuple-element.39.refs_1_), channel_id=1, source_target_pairs={{0,6},{2,4},{4,2},{6,0},{8,14},{10,12},{12,10},{14,8},{1,7},{3,5},... | collective-permute-start | bytes 196616 | tf_op jit(solution)/shard_map/ppermute | solution.py:56
  40.1 1.6 %collective-permute-start.14 = (bf16[128,256]{1,0:T(8,128)(2,1)S(1)}, bf16[128,256]{1,0:T(8,128)(2,1)S(1)}, u32[]{:S(2)}, u32[]{:S(2)}) collective-permute-start(bf16[128,256]{1,0:T(8,128)(2,1)S(1)} %get-tuple-element.39.refs_1_), channel_id=1, source_target_pairs={{0,8},{2,10},{4,12},{6,14},{8,0},{10,2},{12,4},{14,6},{1,9},{3,11}... | collective-permute-start | bytes 196616 | tf_op jit(solution)/shard_map/ppermute | solution.py:56
  41.8 2.6 %collective-permute-start.13 = (bf16[128,256]{1,0:T(8,128)(2,1)S(1)}, bf16[128,256]{1,0:T(8,128)(2,1)S(1)}, u32[]{:S(2)}, u32[]{:S(2)}) collective-permute-start(bf16[128,256]{1,0:T(8,128)(2,1)S(1)} %get-tuple-element.39.refs_1_), channel_id=1, source_target_pairs={{0,12},{2,14},{4,8},{6,10},{8,4},{10,6},{12,0},{14,2},{1,13},{3,15... | collective-permute-start | bytes 196616 | tf_op jit(solution)/shard_map/ppermute | solution.py:56
  44.4 1.2 %collective-permute-done.17.refs_0_ = bf16[128,256]{1,0:T(8,128)(2,1)S(1)} collective-permute-done((bf16[128,256]{1,0:T(8,128)(2,1)S(1)}, bf16[128,256]{1,0:T(8,128)(2,1)S(1)}, u32[]{:S(2)}, u32[]{:S(2)}) %collective-permute-start.17) | collective-permute-done | bytes 65568 | tf_op jit(solution)/shard_map/ppermute | solution.py:56
  45.6 1.0 %shard_map.80 = (bf16[512,1024]{1,0:T(8,128)(2,1)S(1)}, bf16[512,256]{1,0:T(8,128)(2,1)S(1)}, bf16[4,128,256]{2,1,0:T(8,128)(2,1)S(1)}) custom-call(bf16[128,256]{1,0:T(8,128)(2,1)S(1)} %collective-permute-done.17.refs_0_, bf16[128,256]{1,0:T(8,128)(2,1)S(1)} %collective-permute-done.18.refs_1_, bf16[128,256]{1,0:T(8,128)(2,1)S(1)} %collective-permute-done.19.refs_2_, ...), custom_call_target="tpu_custom_call" | custom-call | flops 10000000000 | tf_op jit(solution)/shard_map/pallas_call | solution.py:44
  46.6 2.5 %collective-permute-start.21 = (bf16[4,128,256]{2,1,0:T(8,128)(2,1)S(1)}, bf16[4,128,256]{2,1,0:T(8,128)(2,1)S(1)}, u32[]{:S(2)}, u32[]{:S(2)}) collective-permute-start(bf16[4,128,256]{2,1,0:T(8,128)(2,1)S(1)} %get-tuple-element.48), channel_id=1, source_target_pairs={{0,2},{2,0},{4,6},{6,4},{8,10},{10,8},{12,14},{14,12},{1,3},{3,1},... | collective-permute-start | bytes 786440 | tf_op jit(solution)/shard_map/ppermute | solution.py:56
  49.1 1.0 %shard_map.79 = (bf16[512,1024]{1,0:T(8,128)(2,1)S(1)}, bf16[512,256]{1,0:T(8,128)(2,1)S(1)}, f32[4,128,256]{2,1,0:T(8,128)S(1)}) custom-call(bf16[128,256]{1,0:T(8,128)(2,1)S(1)} %collective-permute-done.12.refs_0_, bf16[128,256]{1,0:T(8,128)(2,1)S(1)} %get-tuple-element.39.refs_1_, bf16[128,256]{1,0:T(8,128)(2,1)S(1)} %collective-permute-done.13.refs_2_, ...), custom_call_target="tpu_custom_call" | custom-call | flops 10000000000 | tf_op jit(solution)/shard_map/pallas_call | solution.py:44
  50.0 0.9 %shard_map.83 = (f32[512,256]{1,0:T(8,128)S(1)}, bf16[512,256]{1,0:T(8,128)(2,1)S(1)}) custom-call(bf16[512,1024]{1,0:T(8,128)(2,1)S(1)} %get-tuple-element.54.refs_0_, bf16[512,1024]{1,0:T(8,128)(2,1)S(1)} %get-tuple-element.55.refs_1_, bf16[512,256]{1,0:T(8,128)(2,1)S(1)} %get-tuple-element.56.refs_2_, bf16[512,256]{1,0:T(8,128)(2,1)S(1)} %get-tuple-element.57.refs_3_), custom_call_target="tpu_custom_call" | custom-call | flops 10000000000 | tf_op jit(solution)/shard_map/pallas_call | solution.py:44
  51.0 2.4 %collective-permute-done.21.other = bf16[4,128,256]{2,1,0:T(8,128)(2,1)S(1)} collective-permute-done((bf16[4,128,256]{2,1,0:T(8,128)(2,1)S(1)}, bf16[4,128,256]{2,1,0:T(8,128)(2,1)S(1)}, u32[]{:S(2)}, u32[]{:S(2)}) %collective-permute-start.21) | collective-permute-done | bytes 262176 | tf_op jit(solution)/shard_map/ppermute | solution.py:56
  53.5 2.2 %collective-permute-start.22 = (bf16[128,256]{1,0:T(8,128)(2,1)S(1)}, bf16[128,256]{1,0:T(8,128)(2,1)S(1)}, u32[]{:S(2)}, u32[]{:S(2)}) collective-permute-start(bf16[128,256]{1,0:T(8,128)(2,1)S(1)} %get-tuple-element.49), channel_id=1, source_target_pairs={{0,12},{2,14},{4,8},{6,10},{8,4},{10,6},{12,0},{14,2},{1,13},{3,15... | collective-permute-start | bytes 196616 | tf_op jit(solution)/shard_map/ppermute | solution.py:56
  55.6 2.3 %collective-permute-start.24 = (bf16[128,256]{1,0:T(8,128)(2,1)S(1)}, bf16[128,256]{1,0:T(8,128)(2,1)S(1)}, u32[]{:S(2)}, u32[]{:S(2)}) collective-permute-start(bf16[128,256]{1,0:T(8,128)(2,1)S(1)} %get-tuple-element.51), channel_id=1, source_target_pairs={{0,4},{2,6},{4,0},{6,2},{8,12},{10,14},{12,8},{14,10},{1,5},{3,7},... | collective-permute-start | bytes 196616 | tf_op jit(solution)/shard_map/ppermute | solution.py:56
  57.9 0.9 %shard_map.84 = f32[512,256]{1,0:T(8,128)} custom-call(f32[512,256]{1,0:T(8,128)S(1)} %get-tuple-element.53.own, f32[512,256]{1,0:T(8,128)S(1)} %get-tuple-element.58.refs_0_, bf16[512,256]{1,0:T(8,128)(2,1)S(1)} %collective-permute-done.25.refs_1_), custom_call_target="tpu_custom_call" | custom-call | flops 10000000000 | tf_op jit(solution)/shard_map/pallas_call | solution.py:44
  59.6 1.4 %collective-permute-done.23.refs_1_ = bf16[128,256]{1,0:T(8,128)(2,1)S(1)} collective-permute-done((bf16[128,256]{1,0:T(8,128)(2,1)S(1)}, bf16[128,256]{1,0:T(8,128)(2,1)S(1)}, u32[]{:S(2)}, u32[]{:S(2)}) %collective-permute-start.23) | collective-permute-done | bytes 65568 | tf_op jit(solution)/shard_map/ppermute | solution.py:56
  (47 shorter events, 4.6 us)
Async XLA Ops:
  0.6 9.1 %copy-start.1 = (f32[512,256]{1,0:T(8,128)S(1)}, f32[512,256]{1,0:T(8,128)}, u32[]{:S(2)}) copy-start(f32[512,256]{1,0:T(8,128)} %own.3) | copy-start | bytes 1572868
  0.6 1.0 %copy-start.2 = (f32[128,256]{1,0:T(8,128)S(1)}, f32[128,256]{1,0:T(8,128)}, u32[]{:S(2)}) copy-start(f32[128,256]{1,0:T(8,128)} %own.2) | copy-start | bytes 393220
  1.6 8.9 %copy-start = (s32[1,1,24,128,128]{4,3,2,1,0:T(8,128)S(1)}, s32[1,1,24,128,128]{4,3,2,1,0:T(8,128)}, u32[]{:S(2)}) copy-start(s32[1,1,24,128,128]{4,3,2,1,0:T(8,128)} %param.9) | copy-start | bytes 4718596
  1.6 8.9 %copy-start.4 = (s32[1,1,24]{2,1,0:T(1,128)S(1)}, s32[1,1,24]{2,1,0:T(1,128)}, u32[]{:S(2)}) copy-start(s32[1,1,24]{2,1,0:T(1,128)} %param.7) | copy-start | bytes 292
  1.6 12.6 %collective-permute-start.7 = (bf16[128,256]{1,0:T(8,128)(2,1)S(1)}, bf16[128,256]{1,0:T(8,128)(2,1)S(1)}, u32[]{:S(2)}, u32[]{:S(2)}) collective-permute-start(bf16[128,256]{1,0:T(8,128)(2,1)S(1)} %shard_map.68.refs_1_), channel_id=1, source_target_pairs={{0,10},{2,8},{4,14},{6,12},{8,2},{10,0},{12,6},{14,4},{1,11},{3,9}... | collective-permute-start | bytes 196616 | tf_op jit(solution)/shard_map/ppermute | solution.py:56
  6.7 9.3 %collective-permute-start.6 = (bf16[128,256]{1,0:T(8,128)(2,1)S(1)}, bf16[128,256]{1,0:T(8,128)(2,1)S(1)}, u32[]{:S(2)}, u32[]{:S(2)}) collective-permute-start(bf16[128,256]{1,0:T(8,128)(2,1)S(1)} %shard_map.68.refs_1_), channel_id=1, source_target_pairs={{0,14},{2,12},{4,10},{6,8},{8,6},{10,4},{12,2},{14,0},{1,15},{3,13... | collective-permute-start | bytes 196616 | tf_op jit(solution)/shard_map/ppermute | solution.py:56
  8.0 8.0 %collective-permute-start.5 = (bf16[128,256]{1,0:T(8,128)(2,1)S(1)}, bf16[128,256]{1,0:T(8,128)(2,1)S(1)}, u32[]{:S(2)}, u32[]{:S(2)}) collective-permute-start(bf16[128,256]{1,0:T(8,128)(2,1)S(1)} %shard_map.68.refs_1_), channel_id=1, source_target_pairs={{0,2},{2,0},{4,6},{6,4},{8,10},{10,8},{12,14},{14,12},{1,3},{3,1},... | collective-permute-start | bytes 196616 | tf_op jit(solution)/shard_map/ppermute | solution.py:56
  9.5 6.5 %collective-permute-start.4 = (bf16[128,256]{1,0:T(8,128)(2,1)S(1)}, bf16[128,256]{1,0:T(8,128)(2,1)S(1)}, u32[]{:S(2)}, u32[]{:S(2)}) collective-permute-start(bf16[128,256]{1,0:T(8,128)(2,1)S(1)} %shard_map.68.refs_1_), channel_id=1, source_target_pairs={{0,6},{2,4},{4,2},{6,0},{8,14},{10,12},{12,10},{14,8},{1,7},{3,5},... | collective-permute-start | bytes 196616 | tf_op jit(solution)/shard_map/ppermute | solution.py:56
  9.8 1.6 %collective-permute-start.3 = (bf16[512,256]{1,0:T(8,128)(2,1)S(1)}, bf16[512,256]{1,0:T(8,128)(2,1)S(1)}, u32[]{:S(2)}, u32[]{:S(2)}) collective-permute-start(bf16[512,256]{1,0:T(8,128)(2,1)S(1)} %shard_map.69.mine), channel_id=1, source_target_pairs={{0,1},{1,0},{2,3},{3,2},{4,5},{5,4},{6,7},{7,6},{8,9},{9,8},{10,11... | collective-permute-start | bytes 786440 | tf_op jit(solution)/shard_map/ppermute | solution.py:56
  11.4 7.2 %collective-permute-start.2 = (bf16[128,256]{1,0:T(8,128)(2,1)S(1)}, bf16[128,256]{1,0:T(8,128)(2,1)S(1)}, u32[]{:S(2)}, u32[]{:S(2)}) collective-permute-start(bf16[128,256]{1,0:T(8,128)(2,1)S(1)} %shard_map.68.refs_1_), channel_id=1, source_target_pairs={{0,8},{2,10},{4,12},{6,14},{8,0},{10,2},{12,4},{14,6},{1,9},{3,11}... | collective-permute-start | bytes 196616 | tf_op jit(solution)/shard_map/ppermute | solution.py:56
  14.2 6.8 %collective-permute-start.1 = (bf16[128,256]{1,0:T(8,128)(2,1)S(1)}, bf16[128,256]{1,0:T(8,128)(2,1)S(1)}, u32[]{:S(2)}, u32[]{:S(2)}) collective-permute-start(bf16[128,256]{1,0:T(8,128)(2,1)S(1)} %shard_map.68.refs_1_), channel_id=1, source_target_pairs={{0,12},{2,14},{4,8},{6,10},{8,4},{10,6},{12,0},{14,2},{1,13},{3,15... | collective-permute-start | bytes 196616 | tf_op jit(solution)/shard_map/ppermute | solution.py:56
  16.0 5.4 %collective-permute-start = (bf16[128,256]{1,0:T(8,128)(2,1)S(1)}, bf16[128,256]{1,0:T(8,128)(2,1)S(1)}, u32[]{:S(2)}, u32[]{:S(2)}) collective-permute-start(bf16[128,256]{1,0:T(8,128)(2,1)S(1)} %shard_map.68.refs_1_), channel_id=1, source_target_pairs={{0,4},{2,6},{4,0},{6,2},{8,12},{10,14},{12,8},{14,10},{1,5},{3,7},... | collective-permute-start | bytes 196616 | tf_op jit(solution)/shard_map/ppermute | solution.py:56
  17.0 8.1 %collective-permute-start.8 = (bf16[4,128,256]{2,1,0:T(8,128)(2,1)S(1)}, bf16[4,128,256]{2,1,0:T(8,128)(2,1)S(1)}, u32[]{:S(2)}, u32[]{:S(2)}) collective-permute-start(bf16[4,128,256]{2,1,0:T(8,128)(2,1)S(1)} %get-tuple-element.33), channel_id=1, source_target_pairs={{0,2},{2,0},{4,6},{6,4},{8,10},{10,8},{12,14},{14,12},{1,3},{3,1},... | collective-permute-start | bytes 786440 | tf_op jit(solution)/shard_map/ppermute | solution.py:56
  23.1 6.4 %collective-permute-start.15 = (bf16[512,256]{1,0:T(8,128)(2,1)S(1)}, bf16[512,256]{1,0:T(8,128)(2,1)S(1)}, u32[]{:S(2)}, u32[]{:S(2)}) collective-permute-start(bf16[512,256]{1,0:T(8,128)(2,1)S(1)} %get-tuple-element.45), channel_id=1, source_target_pairs={{0,1},{1,0},{2,3},{3,2},{4,5},{5,4},{6,7},{7,6},{8,9},{9,8},{10,11... | collective-permute-start | bytes 786440 | tf_op jit(solution)/shard_map/ppermute | solution.py:56
  25.1 6.6 %collective-permute-start.9 = (bf16[128,256]{1,0:T(8,128)(2,1)S(1)}, bf16[128,256]{1,0:T(8,128)(2,1)S(1)}, u32[]{:S(2)}, u32[]{:S(2)}) collective-permute-start(bf16[128,256]{1,0:T(8,128)(2,1)S(1)} %get-tuple-element.34), channel_id=1, source_target_pairs={{0,12},{2,14},{4,8},{6,10},{8,4},{10,6},{12,0},{14,2},{1,13},{3,15... | collective-permute-start | bytes 196616 | tf_op jit(solution)/shard_map/ppermute | solution.py:56
  27.6 6.5 %collective-permute-start.10 = (bf16[128,256]{1,0:T(8,128)(2,1)S(1)}, bf16[128,256]{1,0:T(8,128)(2,1)S(1)}, u32[]{:S(2)}, u32[]{:S(2)}) collective-permute-start(bf16[128,256]{1,0:T(8,128)(2,1)S(1)} %get-tuple-element.35), channel_id=1, source_target_pairs={{0,8},{2,10},{4,12},{6,14},{8,0},{10,2},{12,4},{14,6},{1,9},{3,11}... | collective-permute-start | bytes 196616 | tf_op jit(solution)/shard_map/ppermute | solution.py:56
  28.3 5.8 %collective-permute-start.11 = (bf16[128,256]{1,0:T(8,128)(2,1)S(1)}, bf16[128,256]{1,0:T(8,128)(2,1)S(1)}, u32[]{:S(2)}, u32[]{:S(2)}) collective-permute-start(bf16[128,256]{1,0:T(8,128)(2,1)S(1)} %get-tuple-element.36), channel_id=1, source_target_pairs={{0,4},{2,6},{4,0},{6,2},{8,12},{10,14},{12,8},{14,10},{1,5},{3,7},... | collective-permute-start | bytes 196616 | tf_op jit(solution)/shard_map/ppermute | solution.py:56
  29.5 4.6 %copy-start.3 = (f32[128,256]{1,0:T(8,128)S(1)}, f32[128,256]{1,0:T(8,128)}, u32[]{:S(2)}) copy-start(f32[128,256]{1,0:T(8,128)} %own.2) | copy-start | bytes 393220
  29.7 10.4 %collective-permute-start.16 = (bf16[512,256]{1,0:T(8,128)(2,1)S(1)}, bf16[512,256]{1,0:T(8,128)(2,1)S(1)}, u32[]{:S(2)}, u32[]{:S(2)}) collective-permute-start(bf16[512,256]{1,0:T(8,128)(2,1)S(1)} %get-tuple-element.46.mine), channel_id=1, source_target_pairs={{0,1},{1,0},{2,3},{3,2},{4,5},{5,4},{6,7},{7,6},{8,9},{9,8},{10,11... | collective-permute-start | bytes 786440 | tf_op jit(solution)/shard_map/ppermute | solution.py:56
  34.2 7.6 %collective-permute-start.20 = (bf16[128,256]{1,0:T(8,128)(2,1)S(1)}, bf16[128,256]{1,0:T(8,128)(2,1)S(1)}, u32[]{:S(2)}, u32[]{:S(2)}) collective-permute-start(bf16[128,256]{1,0:T(8,128)(2,1)S(1)} %get-tuple-element.39.refs_1_), channel_id=1, source_target_pairs={{0,10},{2,8},{4,14},{6,12},{8,2},{10,0},{12,6},{14,4},{1,11},{3,9}... | collective-permute-start | bytes 196616 | tf_op jit(solution)/shard_map/ppermute | solution.py:56
  35.9 8.5 %collective-permute-start.19 = (bf16[128,256]{1,0:T(8,128)(2,1)S(1)}, bf16[128,256]{1,0:T(8,128)(2,1)S(1)}, u32[]{:S(2)}, u32[]{:S(2)}) collective-permute-start(bf16[128,256]{1,0:T(8,128)(2,1)S(1)} %get-tuple-element.39.refs_1_), channel_id=1, source_target_pairs={{0,14},{2,12},{4,10},{6,8},{8,6},{10,4},{12,2},{14,0},{1,15},{3,13... | collective-permute-start | bytes 196616 | tf_op jit(solution)/shard_map/ppermute | solution.py:56
  37.3 7.1 %collective-permute-start.18 = (bf16[128,256]{1,0:T(8,128)(2,1)S(1)}, bf16[128,256]{1,0:T(8,128)(2,1)S(1)}, u32[]{:S(2)}, u32[]{:S(2)}) collective-permute-start(bf16[128,256]{1,0:T(8,128)(2,1)S(1)} %get-tuple-element.39.refs_1_), channel_id=1, source_target_pairs={{0,2},{2,0},{4,6},{6,4},{8,10},{10,8},{12,14},{14,12},{1,3},{3,1},... | collective-permute-start | bytes 196616 | tf_op jit(solution)/shard_map/ppermute | solution.py:56
  38.8 6.8 %collective-permute-start.17 = (bf16[128,256]{1,0:T(8,128)(2,1)S(1)}, bf16[128,256]{1,0:T(8,128)(2,1)S(1)}, u32[]{:S(2)}, u32[]{:S(2)}) collective-permute-start(bf16[128,256]{1,0:T(8,128)(2,1)S(1)} %get-tuple-element.39.refs_1_), channel_id=1, source_target_pairs={{0,6},{2,4},{4,2},{6,0},{8,14},{10,12},{12,10},{14,8},{1,7},{3,5},... | collective-permute-start | bytes 196616 | tf_op jit(solution)/shard_map/ppermute | solution.py:56
  40.1 9.0 %collective-permute-start.14 = (bf16[128,256]{1,0:T(8,128)(2,1)S(1)}, bf16[128,256]{1,0:T(8,128)(2,1)S(1)}, u32[]{:S(2)}, u32[]{:S(2)}) collective-permute-start(bf16[128,256]{1,0:T(8,128)(2,1)S(1)} %get-tuple-element.39.refs_1_), channel_id=1, source_target_pairs={{0,8},{2,10},{4,12},{6,14},{8,0},{10,2},{12,4},{14,6},{1,9},{3,11}... | collective-permute-start | bytes 196616 | tf_op jit(solution)/shard_map/ppermute | solution.py:56
  41.8 7.3 %collective-permute-start.13 = (bf16[128,256]{1,0:T(8,128)(2,1)S(1)}, bf16[128,256]{1,0:T(8,128)(2,1)S(1)}, u32[]{:S(2)}, u32[]{:S(2)}) collective-permute-start(bf16[128,256]{1,0:T(8,128)(2,1)S(1)} %get-tuple-element.39.refs_1_), channel_id=1, source_target_pairs={{0,12},{2,14},{4,8},{6,10},{8,4},{10,6},{12,0},{14,2},{1,13},{3,15... | collective-permute-start | bytes 196616 | tf_op jit(solution)/shard_map/ppermute | solution.py:56
  44.4 4.7 %collective-permute-start.12 = (bf16[128,256]{1,0:T(8,128)(2,1)S(1)}, bf16[128,256]{1,0:T(8,128)(2,1)S(1)}, u32[]{:S(2)}, u32[]{:S(2)}) collective-permute-start(bf16[128,256]{1,0:T(8,128)(2,1)S(1)} %get-tuple-element.39.refs_1_), channel_id=1, source_target_pairs={{0,4},{2,6},{4,0},{6,2},{8,12},{10,14},{12,8},{14,10},{1,5},{3,7},... | collective-permute-start | bytes 196616 | tf_op jit(solution)/shard_map/ppermute | solution.py:56
  46.6 6.8 %collective-permute-start.21 = (bf16[4,128,256]{2,1,0:T(8,128)(2,1)S(1)}, bf16[4,128,256]{2,1,0:T(8,128)(2,1)S(1)}, u32[]{:S(2)}, u32[]{:S(2)}) collective-permute-start(bf16[4,128,256]{2,1,0:T(8,128)(2,1)S(1)} %get-tuple-element.48), channel_id=1, source_target_pairs={{0,2},{2,0},{4,6},{6,4},{8,10},{10,8},{12,14},{14,12},{1,3},{3,1},... | collective-permute-start | bytes 786440 | tf_op jit(solution)/shard_map/ppermute | solution.py:56
  50.9 7.0 %collective-permute-start.25 = (bf16[512,256]{1,0:T(8,128)(2,1)S(1)}, bf16[512,256]{1,0:T(8,128)(2,1)S(1)}, u32[]{:S(2)}, u32[]{:S(2)}) collective-permute-start(bf16[512,256]{1,0:T(8,128)(2,1)S(1)} %get-tuple-element.59), channel_id=1, source_target_pairs={{0,1},{1,0},{2,3},{3,2},{4,5},{5,4},{6,7},{7,6},{8,9},{9,8},{10,11... | collective-permute-start | bytes 786440 | tf_op jit(solution)/shard_map/ppermute | solution.py:56
  53.5 6.1 %collective-permute-start.22 = (bf16[128,256]{1,0:T(8,128)(2,1)S(1)}, bf16[128,256]{1,0:T(8,128)(2,1)S(1)}, u32[]{:S(2)}, u32[]{:S(2)}) collective-permute-start(bf16[128,256]{1,0:T(8,128)(2,1)S(1)} %get-tuple-element.49), channel_id=1, source_target_pairs={{0,12},{2,14},{4,8},{6,10},{8,4},{10,6},{12,0},{14,2},{1,13},{3,15... | collective-permute-start | bytes 196616 | tf_op jit(solution)/shard_map/ppermute | solution.py:56
  55.6 5.4 %collective-permute-start.23 = (bf16[128,256]{1,0:T(8,128)(2,1)S(1)}, bf16[128,256]{1,0:T(8,128)(2,1)S(1)}, u32[]{:S(2)}, u32[]{:S(2)}) collective-permute-start(bf16[128,256]{1,0:T(8,128)(2,1)S(1)} %get-tuple-element.50), channel_id=1, source_target_pairs={{0,8},{2,10},{4,12},{6,14},{8,0},{10,2},{12,4},{14,6},{1,9},{3,11}... | collective-permute-start | bytes 196616 | tf_op jit(solution)/shard_map/ppermute | solution.py:56
  55.6 5.4 %collective-permute-start.24 = (bf16[128,256]{1,0:T(8,128)(2,1)S(1)}, bf16[128,256]{1,0:T(8,128)(2,1)S(1)}, u32[]{:S(2)}, u32[]{:S(2)}) collective-permute-start(bf16[128,256]{1,0:T(8,128)(2,1)S(1)} %get-tuple-element.51), channel_id=1, source_target_pairs={{0,4},{2,6},{4,0},{6,2},{8,12},{10,14},{12,8},{14,10},{1,5},{3,7},... | collective-permute-start | bytes 196616 | tf_op jit(solution)/shard_map/ppermute | solution.py:56

commit v5 on v4

--- a/solution.py
+++ b/solution.py
@@ -80,8 +80,9 @@
     panel[pl.ds(pl.multiple_of((me ^ 1) * half, half), half), :] = other[...]
 
 
-def turned(n):
-    return [*range(n // 2, n), *range(n // 2)]
+def turned(n, back=False):
+    far = range(n // 2)
+    return [*range(n // 2, n), *(reversed(far) if back else far)]
 
 
 def rows_body(partners, blk, *refs):
@@ -92,7 +93,7 @@
     owned, across = own // blk, lvl.shape[0] // blk
     wide = 2 if across % 2 == 0 else 1
     me = lax.axis_index("lvl")
-    for part, i in zip(parts, turned(n)):
+    for part, i in zip(parts, turned(n, 0 in partners)):
         stu[i * own : (i + 1) * own, :] = part[...]
     rows = n * own
     tall = min(TALL * blk, rows)
@@ -167,6 +168,7 @@
             (lvl_low, swap(lvl_low, "stu", n_stu, 1)),
         )
         back, res, stu = [], [], []
+        n = n_lvl // 2
         for evens in groups:
             made = []
             for partners, kind in (([k ^ 1 for k in evens], BF16), (evens, F32)):
@@ -179,7 +181,7 @@
                         sds((len(partners), own, rank), kind),
                     ),
                     (),
-                    (*(came[partners[i]] for i in turned(len(partners))), panel, sign),
+                    (*(came[partners[i]] for i in turned(len(partners), kind == F32)), panel, sign),
                 )
                 res.append(panels[0])
                 stu.append(panels[1])
@@ -209,7 +211,7 @@
             functools.partial(settle_body, len(kinds)),
             [sds((own, rank), kind) for kind in kinds],
             (),
-            (stu_own, *back),
+            (stu_own, *(back[i] for i in (n - 1, *reversed(range(n // 2)), *range(n // 2, n - 1)))),
         )
         stu_low = lows[0] if lows else None
     return (stu_own, lvl_own)

time: 61.9 us -> 61 us (0.985)
  starting transfers between devices: 35.9 us -> 32.1 us
  waiting for transfers between devices: 14.9 us -> 17.8 us
    ppermute x26, starting transfers between devices: 35.9 us -> 32.1 us  [swap(): return lax.ppermute(x, axis, [(i, i ^ k) for i in range(n)])]
    ppermute x26, waiting for transfers between devices: 14.9 us -> 17.8 us  [swap(): return lax.ppermute(x, axis, [(i, i ^ k) for i in range(n)])]
  transfers between devices with their start and end apart: 26 -> 26, of which waited for: 10 -> 13; matrix products, arithmetic and copies ran while one was open for 0% -> 0% of each run, Pallas kernels for 13% -> 13%
where the time goes in v5:
time: 61 us; the launch traced here: 60.9 us
  starting transfers between devices  32.1 us (53%)
  waiting for transfers between devices  17.8 us (29%)
  Pallas kernels  8.48 us (14%)
  between operations  1.49 us (2%)
  local copies, waits for them, and re-layouts  0.98 us (2%)
    ppermute x26, starting transfers between devices, swap(): return lax.ppermute(x, axis, [(i, i ^ k) for i in range(n)])  32.1 us
    ppermute x26, waiting for transfers between devices, swap(): return lax.ppermute(x, axis, [(i, i ^ k) for i in range(n)])  17.8 us
    pallas_call x17, Pallas kernels, call(): pl.pallas_call(body, out_shape=tuple(out_shape), in_specs=[smem()] * len(...  8.48 us
  transfers between devices with their start and end apart: 26, of which 13 were waited for; matrix products, arithmetic and copies ran while one was open for 0% of the time, Pallas kernels for 13%

profile of v5, /device:TPU:0, one launch (start us, length us, event | category | flops | bytes accessed | tf_op | source)
XLA Modules:
  0.0 60.9 jit_solution(17530319337963735371)
XLA Ops:
  0.7 1.0 %copy-done.2 = f32[128,256]{1,0:T(8,128)S(1)} copy-done((f32[128,256]{1,0:T(8,128)S(1)}, f32[128,256]{1,0:T(8,128)}, u32[]{:S(2)}) %copy-start.2) | copy-done | bytes 131096
  1.6 5.1 %collective-permute-start.7 = (bf16[128,256]{1,0:T(8,128)(2,1)S(1)}, bf16[128,256]{1,0:T(8,128)(2,1)S(1)}, u32[]{:S(2)}, u32[]{:S(2)}) collective-permute-start(bf16[128,256]{1,0:T(8,128)(2,1)S(1)} %shard_map.68.refs_1_), channel_id=1, source_target_pairs={{0,10},{2,8},{4,14},{6,12},{8,2},{10,0},{12,6},{14,4},{1,11},{3,9}... | collective-permute-start | bytes 196616 | tf_op jit(solution)/shard_map/ppermute | solution.py:56
  6.7 1.3 %collective-permute-start.6 = (bf16[128,256]{1,0:T(8,128)(2,1)S(1)}, bf16[128,256]{1,0:T(8,128)(2,1)S(1)}, u32[]{:S(2)}, u32[]{:S(2)}) collective-permute-start(bf16[128,256]{1,0:T(8,128)(2,1)S(1)} %shard_map.68.refs_1_), channel_id=1, source_target_pairs={{0,14},{2,12},{4,10},{6,8},{8,6},{10,4},{12,2},{14,0},{1,15},{3,13... | collective-permute-start | bytes 196616 | tf_op jit(solution)/shard_map/ppermute | solution.py:56
  8.0 1.5 %collective-permute-start.5 = (bf16[128,256]{1,0:T(8,128)(2,1)S(1)}, bf16[128,256]{1,0:T(8,128)(2,1)S(1)}, u32[]{:S(2)}, u32[]{:S(2)}) collective-permute-start(bf16[128,256]{1,0:T(8,128)(2,1)S(1)} %shard_map.68.refs_1_), channel_id=1, source_target_pairs={{0,2},{2,0},{4,6},{6,4},{8,10},{10,8},{12,14},{14,12},{1,3},{3,1},... | collective-permute-start | bytes 196616 | tf_op jit(solution)/shard_map/ppermute | solution.py:56
  10.5 0.9 %shard_map.71.refs_5_ = bf16[64,128,128]{2,1,0:T(8,128)(2,1)S(1)} custom-call(s32[24]{0:T(128)S(1)} %bitcast.3, s32[1,1]{1,0:T(1,128)S(6)} %copy.7.count, s32[24,128,128]{2,1,0:T(8,128)S(1)} %bitcast.2), custom_call_target="tpu_custom_call" | custom-call | flops 10000000000 | tf_op jit(solution)/shard_map/pallas_call | solution.py:44
  11.4 2.9 %collective-permute-start.2 = (bf16[128,256]{1,0:T(8,128)(2,1)S(1)}, bf16[128,256]{1,0:T(8,128)(2,1)S(1)}, u32[]{:S(2)}, u32[]{:S(2)}) collective-permute-start(bf16[128,256]{1,0:T(8,128)(2,1)S(1)} %shard_map.68.refs_1_), channel_id=1, source_target_pairs={{0,12},{2,14},{4,8},{6,10},{8,4},{10,6},{12,0},{14,2},{1,13},{3,15... | collective-permute-start | bytes 196616 | tf_op jit(solution)/shard_map/ppermute | solution.py:56
  14.8 1.3 %collective-permute-start = (bf16[128,256]{1,0:T(8,128)(2,1)S(1)}, bf16[128,256]{1,0:T(8,128)(2,1)S(1)}, u32[]{:S(2)}, u32[]{:S(2)}) collective-permute-start(bf16[128,256]{1,0:T(8,128)(2,1)S(1)} %shard_map.68.refs_1_), channel_id=1, source_target_pairs={{0,4},{2,6},{4,0},{6,2},{8,12},{10,14},{12,8},{14,10},{1,5},{3,7},... | collective-permute-start | bytes 196616 | tf_op jit(solution)/shard_map/ppermute | solution.py:56
  16.1 1.0 %shard_map.73 = (bf16[512,1024]{1,0:T(8,128)(2,1)S(1)}, bf16[512,256]{1,0:T(8,128)(2,1)S(1)}, bf16[4,128,256]{2,1,0:T(8,128)(2,1)S(1)}) custom-call(bf16[128,256]{1,0:T(8,128)(2,1)S(1)} %collective-permute-done.4.refs_0_, bf16[128,256]{1,0:T(8,128)(2,1)S(1)} %collective-permute-done.5.refs_1_, bf16[128,256]{1,0:T(8,128)(2,1)S(1)} %collective-permute-done.6.refs_2_, ...), custom_call_target="tpu_custom_call" | custom-call | flops 10000000000 | tf_op jit(solution)/shard_map/pallas_call | solution.py:44
  17.1 1.6 %collective-permute-start.8 = (bf16[4,128,256]{2,1,0:T(8,128)(2,1)S(1)}, bf16[4,128,256]{2,1,0:T(8,128)(2,1)S(1)}, u32[]{:S(2)}, u32[]{:S(2)}) collective-permute-start(bf16[4,128,256]{2,1,0:T(8,128)(2,1)S(1)} %get-tuple-element.33), channel_id=1, source_target_pairs={{0,2},{2,0},{4,6},{6,4},{8,10},{10,8},{12,14},{14,12},{1,3},{3,1},... | collective-permute-start | bytes 786440 | tf_op jit(solution)/shard_map/ppermute | solution.py:56
  18.7 2.9 %collective-permute-done.1.refs_2_ = bf16[128,256]{1,0:T(8,128)(2,1)S(1)} collective-permute-done((bf16[128,256]{1,0:T(8,128)(2,1)S(1)}, bf16[128,256]{1,0:T(8,128)(2,1)S(1)}, u32[]{:S(2)}, u32[]{:S(2)}) %collective-permute-start.1) | collective-permute-done | bytes 65568 | tf_op jit(solution)/shard_map/ppermute | solution.py:56
  21.5 1.0 %shard_map.72 = (bf16[512,1024]{1,0:T(8,128)(2,1)S(1)}, bf16[512,256]{1,0:T(8,128)(2,1)S(1)}, f32[4,128,256]{2,1,0:T(8,128)S(1)}) custom-call(bf16[128,256]{1,0:T(8,128)(2,1)S(1)} %collective-permute-done.refs_0_, bf16[128,256]{1,0:T(8,128)(2,1)S(1)} %shard_map.68.refs_1_, bf16[128,256]{1,0:T(8,128)(2,1)S(1)} %collective-permute-done.1.refs_2_, ...), custom_call_target="tpu_custom_call" | custom-call | flops 10000000000 | tf_op jit(solution)/shard_map/pallas_call | solution.py:44
  23.5 1.6 %collective-permute-done.8.other = bf16[4,128,256]{2,1,0:T(8,128)(2,1)S(1)} collective-permute-done((bf16[4,128,256]{2,1,0:T(8,128)(2,1)S(1)}, bf16[4,128,256]{2,1,0:T(8,128)(2,1)S(1)}, u32[]{:S(2)}, u32[]{:S(2)}) %collective-permute-start.8) | collective-permute-done | bytes 262176 | tf_op jit(solution)/shard_map/ppermute | solution.py:56
  25.1 1.8 %collective-permute-start.9 = (bf16[128,256]{1,0:T(8,128)(2,1)S(1)}, bf16[128,256]{1,0:T(8,128)(2,1)S(1)}, u32[]{:S(2)}, u32[]{:S(2)}) collective-permute-start(bf16[128,256]{1,0:T(8,128)(2,1)S(1)} %get-tuple-element.35), channel_id=1, source_target_pairs={{0,8},{2,10},{4,12},{6,14},{8,0},{10,2},{12,4},{14,6},{1,9},{3,11}... | collective-permute-start | bytes 196616 | tf_op jit(solution)/shard_map/ppermute | solution.py:56
  26.9 1.5 %collective-permute-start.10 = (bf16[128,256]{1,0:T(8,128)(2,1)S(1)}, bf16[128,256]{1,0:T(8,128)(2,1)S(1)}, u32[]{:S(2)}, u32[]{:S(2)}) collective-permute-start(bf16[128,256]{1,0:T(8,128)(2,1)S(1)} %get-tuple-element.36), channel_id=1, source_target_pairs={{0,12},{2,14},{4,8},{6,10},{8,4},{10,6},{12,0},{14,2},{1,13},{3,15... | collective-permute-start | bytes 196616 | tf_op jit(solution)/shard_map/ppermute | solution.py:56
  28.9 2.9 %collective-permute-done.9.refs_1_ = bf16[128,256]{1,0:T(8,128)(2,1)S(1)} collective-permute-done((bf16[128,256]{1,0:T(8,128)(2,1)S(1)}, bf16[128,256]{1,0:T(8,128)(2,1)S(1)}, u32[]{:S(2)}, u32[]{:S(2)}) %collective-permute-start.9) | collective-permute-done | bytes 65568 | tf_op jit(solution)/shard_map/ppermute | solution.py:56
  31.8 1.3 %collective-permute-done.10.refs_2_ = bf16[128,256]{1,0:T(8,128)(2,1)S(1)} collective-permute-done((bf16[128,256]{1,0:T(8,128)(2,1)S(1)}, bf16[128,256]{1,0:T(8,128)(2,1)S(1)}, u32[]{:S(2)}, u32[]{:S(2)}) %collective-permute-start.10) | collective-permute-done | bytes 65568 | tf_op jit(solution)/shard_map/ppermute | solution.py:56
  33.4 2.5 %collective-permute-start.20 = (bf16[128,256]{1,0:T(8,128)(2,1)S(1)}, bf16[128,256]{1,0:T(8,128)(2,1)S(1)}, u32[]{:S(2)}, u32[]{:S(2)}) collective-permute-start(bf16[128,256]{1,0:T(8,128)(2,1)S(1)} %get-tuple-element.39.refs_1_), channel_id=1, source_target_pairs={{0,10},{2,8},{4,14},{6,12},{8,2},{10,0},{12,6},{14,4},{1,11},{3,9}... | collective-permute-start | bytes 196616 | tf_op jit(solution)/shard_map/ppermute | solution.py:56
  35.9 1.2 %collective-permute-start.19 = (bf16[128,256]{1,0:T(8,128)(2,1)S(1)}, bf16[128,256]{1,0:T(8,128)(2,1)S(1)}, u32[]{:S(2)}, u32[]{:S(2)}) collective-permute-start(bf16[128,256]{1,0:T(8,128)(2,1)S(1)} %get-tuple-element.39.refs_1_), channel_id=1, source_target_pairs={{0,14},{2,12},{4,10},{6,8},{8,6},{10,4},{12,2},{14,0},{1,15},{3,13... | collective-permute-start | bytes 196616 | tf_op jit(solution)/shard_map/ppermute | solution.py:56
  37.1 1.0 %collective-permute-start.18 = (bf16[128,256]{1,0:T(8,128)(2,1)S(1)}, bf16[128,256]{1,0:T(8,128)(2,1)S(1)}, u32[]{:S(2)}, u32[]{:S(2)}) collective-permute-start(bf16[128,256]{1,0:T(8,128)(2,1)S(1)} %get-tuple-element.39.refs_1_), channel_id=1, source_target_pairs={{0,2},{2,0},{4,6},{6,4},{8,10},{10,8},{12,14},{14,12},{1,3},{3,1},... | collective-permute-start | bytes 196616 | tf_op jit(solution)/shard_map/ppermute | solution.py:56
  38.2 1.2 %collective-permute-start.17 = (bf16[128,256]{1,0:T(8,128)(2,1)S(1)}, bf16[128,256]{1,0:T(8,128)(2,1)S(1)}, u32[]{:S(2)}, u32[]{:S(2)}) collective-permute-start(bf16[128,256]{1,0:T(8,128)(2,1)S(1)} %get-tuple-element.39.refs_1_), channel_id=1, source_target_pairs={{0,6},{2,4},{4,2},{6,0},{8,14},{10,12},{12,10},{14,8},{1,7},{3,5},... | collective-permute-start | bytes 196616 | tf_op jit(solution)/shard_map/ppermute | solution.py:56
  39.4 2.1 %collective-permute-start.14 = (bf16[128,256]{1,0:T(8,128)(2,1)S(1)}, bf16[128,256]{1,0:T(8,128)(2,1)S(1)}, u32[]{:S(2)}, u32[]{:S(2)}) collective-permute-start(bf16[128,256]{1,0:T(8,128)(2,1)S(1)} %get-tuple-element.39.refs_1_), channel_id=1, source_target_pairs={{0,12},{2,14},{4,8},{6,10},{8,4},{10,6},{12,0},{14,2},{1,13},{3,15... | collective-permute-start | bytes 196616 | tf_op jit(solution)/shard_map/ppermute | solution.py:56
  43.1 1.0 %collective-permute-start.12 = (bf16[128,256]{1,0:T(8,128)(2,1)S(1)}, bf16[128,256]{1,0:T(8,128)(2,1)S(1)}, u32[]{:S(2)}, u32[]{:S(2)}) collective-permute-start(bf16[128,256]{1,0:T(8,128)(2,1)S(1)} %get-tuple-element.39.refs_1_), channel_id=1, source_target_pairs={{0,4},{2,6},{4,0},{6,2},{8,12},{10,14},{12,8},{14,10},{1,5},{3,7},... | collective-permute-start | bytes 196616 | tf_op jit(solution)/shard_map/ppermute | solution.py:56
  44.6 1.0 %shard_map.80 = (bf16[512,1024]{1,0:T(8,128)(2,1)S(1)}, bf16[512,256]{1,0:T(8,128)(2,1)S(1)}, bf16[4,128,256]{2,1,0:T(8,128)(2,1)S(1)}) custom-call(bf16[128,256]{1,0:T(8,128)(2,1)S(1)} %collective-permute-done.17.refs_0_, bf16[128,256]{1,0:T(8,128)(2,1)S(1)} %collective-permute-done.18.refs_1_, bf16[128,256]{1,0:T(8,128)(2,1)S(1)} %collective-permute-done.19.refs_2_, ...), custom_call_target="tpu_custom_call" | custom-call | flops 10000000000 | tf_op jit(solution)/shard_map/pallas_call | solution.py:44
  46.3 1.2 %collective-permute-done.13.refs_2_ = bf16[128,256]{1,0:T(8,128)(2,1)S(1)} collective-permute-done((bf16[128,256]{1,0:T(8,128)(2,1)S(1)}, bf16[128,256]{1,0:T(8,128)(2,1)S(1)}, u32[]{:S(2)}, u32[]{:S(2)}) %collective-permute-start.13) | collective-permute-done | bytes 65568 | tf_op jit(solution)/shard_map/ppermute | solution.py:56
  47.9 1.0 %shard_map.79 = (bf16[512,1024]{1,0:T(8,128)(2,1)S(1)}, bf16[512,256]{1,0:T(8,128)(2,1)S(1)}, f32[4,128,256]{2,1,0:T(8,128)S(1)}) custom-call(bf16[128,256]{1,0:T(8,128)(2,1)S(1)} %collective-permute-done.12.refs_0_, bf16[128,256]{1,0:T(8,128)(2,1)S(1)} %get-tuple-element.39.refs_1_, bf16[128,256]{1,0:T(8,128)(2,1)S(1)} %collective-permute-done.13.refs_2_, ...), custom_call_target="tpu_custom_call" | custom-call | flops 10000000000 | tf_op jit(solution)/shard_map/pallas_call | solution.py:44
  48.9 0.9 %shard_map.83 = (f32[512,256]{1,0:T(8,128)S(1)}, bf16[512,256]{1,0:T(8,128)(2,1)S(1)}) custom-call(bf16[512,1024]{1,0:T(8,128)(2,1)S(1)} %get-tuple-element.54.refs_0_, bf16[512,1024]{1,0:T(8,128)(2,1)S(1)} %get-tuple-element.55.refs_1_, bf16[512,256]{1,0:T(8,128)(2,1)S(1)} %get-tuple-element.56.refs_2_, bf16[512,256]{1,0:T(8,128)(2,1)S(1)} %get-tuple-element.57.refs_3_), custom_call_target="tpu_custom_call" | custom-call | flops 10000000000 | tf_op jit(solution)/shard_map/pallas_call | solution.py:44
  49.8 2.2 %collective-permute-done.21.other = bf16[4,128,256]{2,1,0:T(8,128)(2,1)S(1)} collective-permute-done((bf16[4,128,256]{2,1,0:T(8,128)(2,1)S(1)}, bf16[4,128,256]{2,1,0:T(8,128)(2,1)S(1)}, u32[]{:S(2)}, u32[]{:S(2)}) %collective-permute-start.21) | collective-permute-done | bytes 262176 | tf_op jit(solution)/shard_map/ppermute | solution.py:56
  52.1 1.4 %collective-permute-start.22 = (bf16[128,256]{1,0:T(8,128)(2,1)S(1)}, bf16[128,256]{1,0:T(8,128)(2,1)S(1)}, u32[]{:S(2)}, u32[]{:S(2)}) collective-permute-start(bf16[128,256]{1,0:T(8,128)(2,1)S(1)} %get-tuple-element.50), channel_id=1, source_target_pairs={{0,8},{2,10},{4,12},{6,14},{8,0},{10,2},{12,4},{14,6},{1,9},{3,11}... | collective-permute-start | bytes 196616 | tf_op jit(solution)/shard_map/ppermute | solution.py:56
  53.5 1.7 %collective-permute-start.23 = (bf16[128,256]{1,0:T(8,128)(2,1)S(1)}, bf16[128,256]{1,0:T(8,128)(2,1)S(1)}, u32[]{:S(2)}, u32[]{:S(2)}) collective-permute-start(bf16[128,256]{1,0:T(8,128)(2,1)S(1)} %get-tuple-element.51), channel_id=1, source_target_pairs={{0,12},{2,14},{4,8},{6,10},{8,4},{10,6},{12,0},{14,2},{1,13},{3,15... | collective-permute-start | bytes 196616 | tf_op jit(solution)/shard_map/ppermute | solution.py:56
  55.7 0.9 %shard_map.84 = f32[512,256]{1,0:T(8,128)} custom-call(f32[512,256]{1,0:T(8,128)S(1)} %get-tuple-element.53.own, f32[512,256]{1,0:T(8,128)S(1)} %get-tuple-element.58.refs_0_, bf16[512,256]{1,0:T(8,128)(2,1)S(1)} %collective-permute-done.25.refs_1_), custom_call_target="tpu_custom_call" | custom-call | flops 10000000000 | tf_op jit(solution)/shard_map/pallas_call | solution.py:44
  56.6 1.4 %collective-permute-done.22.refs_1_ = bf16[128,256]{1,0:T(8,128)(2,1)S(1)} collective-permute-done((bf16[128,256]{1,0:T(8,128)(2,1)S(1)}, bf16[128,256]{1,0:T(8,128)(2,1)S(1)}, u32[]{:S(2)}, u32[]{:S(2)}) %collective-permute-start.22) | collective-permute-done | bytes 65568 | tf_op jit(solution)/shard_map/ppermute | solution.py:56
  58.0 1.7 %collective-permute-done.23.refs_2_ = bf16[128,256]{1,0:T(8,128)(2,1)S(1)} collective-permute-done((bf16[128,256]{1,0:T(8,128)(2,1)S(1)}, bf16[128,256]{1,0:T(8,128)(2,1)S(1)}, u32[]{:S(2)}, u32[]{:S(2)}) %collective-permute-start.23) | collective-permute-done | bytes 65568 | tf_op jit(solution)/shard_map/ppermute | solution.py:56
  (47 shorter events, 7.6 us)
Async XLA Ops:
  0.6 9.1 %copy-start.1 = (f32[512,256]{1,0:T(8,128)S(1)}, f32[512,256]{1,0:T(8,128)}, u32[]{:S(2)}) copy-start(f32[512,256]{1,0:T(8,128)} %own.3) | copy-start | bytes 1572868
  0.6 1.0 %copy-start.2 = (f32[128,256]{1,0:T(8,128)S(1)}, f32[128,256]{1,0:T(8,128)}, u32[]{:S(2)}) copy-start(f32[128,256]{1,0:T(8,128)} %own.2) | copy-start | bytes 393220
  1.6 8.9 %copy-start = (s32[1,1,24,128,128]{4,3,2,1,0:T(8,128)S(1)}, s32[1,1,24,128,128]{4,3,2,1,0:T(8,128)}, u32[]{:S(2)}) copy-start(s32[1,1,24,128,128]{4,3,2,1,0:T(8,128)} %param.9) | copy-start | bytes 4718596
  1.6 8.9 %copy-start.4 = (s32[1,1,24]{2,1,0:T(1,128)S(1)}, s32[1,1,24]{2,1,0:T(1,128)}, u32[]{:S(2)}) copy-start(s32[1,1,24]{2,1,0:T(1,128)} %param.7) | copy-start | bytes 292
  1.6 12.7 %collective-permute-start.7 = (bf16[128,256]{1,0:T(8,128)(2,1)S(1)}, bf16[128,256]{1,0:T(8,128)(2,1)S(1)}, u32[]{:S(2)}, u32[]{:S(2)}) collective-permute-start(bf16[128,256]{1,0:T(8,128)(2,1)S(1)} %shard_map.68.refs_1_), channel_id=1, source_target_pairs={{0,10},{2,8},{4,14},{6,12},{8,2},{10,0},{12,6},{14,4},{1,11},{3,9}... | collective-permute-start | bytes 196616 | tf_op jit(solution)/shard_map/ppermute | solution.py:56
  6.7 8.1 %collective-permute-start.6 = (bf16[128,256]{1,0:T(8,128)(2,1)S(1)}, bf16[128,256]{1,0:T(8,128)(2,1)S(1)}, u32[]{:S(2)}, u32[]{:S(2)}) collective-permute-start(bf16[128,256]{1,0:T(8,128)(2,1)S(1)} %shard_map.68.refs_1_), channel_id=1, source_target_pairs={{0,14},{2,12},{4,10},{6,8},{8,6},{10,4},{12,2},{14,0},{1,15},{3,13... | collective-permute-start | bytes 196616 | tf_op jit(solution)/shard_map/ppermute | solution.py:56
  8.0 8.2 %collective-permute-start.5 = (bf16[128,256]{1,0:T(8,128)(2,1)S(1)}, bf16[128,256]{1,0:T(8,128)(2,1)S(1)}, u32[]{:S(2)}, u32[]{:S(2)}) collective-permute-start(bf16[128,256]{1,0:T(8,128)(2,1)S(1)} %shard_map.68.refs_1_), channel_id=1, source_target_pairs={{0,2},{2,0},{4,6},{6,4},{8,10},{10,8},{12,14},{14,12},{1,3},{3,1},... | collective-permute-start | bytes 196616 | tf_op jit(solution)/shard_map/ppermute | solution.py:56
  9.5 6.6 %collective-permute-start.4 = (bf16[128,256]{1,0:T(8,128)(2,1)S(1)}, bf16[128,256]{1,0:T(8,128)(2,1)S(1)}, u32[]{:S(2)}, u32[]{:S(2)}) collective-permute-start(bf16[128,256]{1,0:T(8,128)(2,1)S(1)} %shard_map.68.refs_1_), channel_id=1, source_target_pairs={{0,6},{2,4},{4,2},{6,0},{8,14},{10,12},{12,10},{14,8},{1,7},{3,5},... | collective-permute-start | bytes 196616 | tf_op jit(solution)/shard_map/ppermute | solution.py:56
  9.8 1.6 %collective-permute-start.3 = (bf16[512,256]{1,0:T(8,128)(2,1)S(1)}, bf16[512,256]{1,0:T(8,128)(2,1)S(1)}, u32[]{:S(2)}, u32[]{:S(2)}) collective-permute-start(bf16[512,256]{1,0:T(8,128)(2,1)S(1)} %shard_map.69.mine), channel_id=1, source_target_pairs={{0,1},{1,0},{2,3},{3,2},{4,5},{5,4},{6,7},{7,6},{8,9},{9,8},{10,11... | collective-permute-start | bytes 786440 | tf_op jit(solution)/shard_map/ppermute | solution.py:56
  11.4 7.3 %collective-permute-start.2 = (bf16[128,256]{1,0:T(8,128)(2,1)S(1)}, bf16[128,256]{1,0:T(8,128)(2,1)S(1)}, u32[]{:S(2)}, u32[]{:S(2)}) collective-permute-start(bf16[128,256]{1,0:T(8,128)(2,1)S(1)} %shard_map.68.refs_1_), channel_id=1, source_target_pairs={{0,12},{2,14},{4,8},{6,10},{8,4},{10,6},{12,0},{14,2},{1,13},{3,15... | collective-permute-start | bytes 196616 | tf_op jit(solution)/shard_map/ppermute | solution.py:56
  14.3 7.2 %collective-permute-start.1 = (bf16[128,256]{1,0:T(8,128)(2,1)S(1)}, bf16[128,256]{1,0:T(8,128)(2,1)S(1)}, u32[]{:S(2)}, u32[]{:S(2)}) collective-permute-start(bf16[128,256]{1,0:T(8,128)(2,1)S(1)} %shard_map.68.refs_1_), channel_id=1, source_target_pairs={{0,8},{2,10},{4,12},{6,14},{8,0},{10,2},{12,4},{14,6},{1,9},{3,11}... | collective-permute-start | bytes 196616 | tf_op jit(solution)/shard_map/ppermute | solution.py:56
  14.8 6.7 %collective-permute-start = (bf16[128,256]{1,0:T(8,128)(2,1)S(1)}, bf16[128,256]{1,0:T(8,128)(2,1)S(1)}, u32[]{:S(2)}, u32[]{:S(2)}) collective-permute-start(bf16[128,256]{1,0:T(8,128)(2,1)S(1)} %shard_map.68.refs_1_), channel_id=1, source_target_pairs={{0,4},{2,6},{4,0},{6,2},{8,12},{10,14},{12,8},{14,10},{1,5},{3,7},... | collective-permute-start | bytes 196616 | tf_op jit(solution)/shard_map/ppermute | solution.py:56
  17.1 7.9 %collective-permute-start.8 = (bf16[4,128,256]{2,1,0:T(8,128)(2,1)S(1)}, bf16[4,128,256]{2,1,0:T(8,128)(2,1)S(1)}, u32[]{:S(2)}, u32[]{:S(2)}) collective-permute-start(bf16[4,128,256]{2,1,0:T(8,128)(2,1)S(1)} %get-tuple-element.33), channel_id=1, source_target_pairs={{0,2},{2,0},{4,6},{6,4},{8,10},{10,8},{12,14},{14,12},{1,3},{3,1},... | collective-permute-start | bytes 786440 | tf_op jit(solution)/shard_map/ppermute | solution.py:56
  23.4 5.3 %collective-permute-start.15 = (bf16[512,256]{1,0:T(8,128)(2,1)S(1)}, bf16[512,256]{1,0:T(8,128)(2,1)S(1)}, u32[]{:S(2)}, u32[]{:S(2)}) collective-permute-start(bf16[512,256]{1,0:T(8,128)(2,1)S(1)} %get-tuple-element.45), channel_id=1, source_target_pairs={{0,1},{1,0},{2,3},{3,2},{4,5},{5,4},{6,7},{7,6},{8,9},{9,8},{10,11... | collective-permute-start | bytes 786440 | tf_op jit(solution)/shard_map/ppermute | solution.py:56
  25.1 6.7 %collective-permute-start.9 = (bf16[128,256]{1,0:T(8,128)(2,1)S(1)}, bf16[128,256]{1,0:T(8,128)(2,1)S(1)}, u32[]{:S(2)}, u32[]{:S(2)}) collective-permute-start(bf16[128,256]{1,0:T(8,128)(2,1)S(1)} %get-tuple-element.35), channel_id=1, source_target_pairs={{0,8},{2,10},{4,12},{6,14},{8,0},{10,2},{12,4},{14,6},{1,9},{3,11}... | collective-permute-start | bytes 196616 | tf_op jit(solution)/shard_map/ppermute | solution.py:56
  26.9 6.2 %collective-permute-start.10 = (bf16[128,256]{1,0:T(8,128)(2,1)S(1)}, bf16[128,256]{1,0:T(8,128)(2,1)S(1)}, u32[]{:S(2)}, u32[]{:S(2)}) collective-permute-start(bf16[128,256]{1,0:T(8,128)(2,1)S(1)} %get-tuple-element.36), channel_id=1, source_target_pairs={{0,12},{2,14},{4,8},{6,10},{8,4},{10,6},{12,0},{14,2},{1,13},{3,15... | collective-permute-start | bytes 196616 | tf_op jit(solution)/shard_map/ppermute | solution.py:56
  28.4 5.0 %collective-permute-start.11 = (bf16[128,256]{1,0:T(8,128)(2,1)S(1)}, bf16[128,256]{1,0:T(8,128)(2,1)S(1)}, u32[]{:S(2)}, u32[]{:S(2)}) collective-permute-start(bf16[128,256]{1,0:T(8,128)(2,1)S(1)} %get-tuple-element.37), channel_id=1, source_target_pairs={{0,4},{2,6},{4,0},{6,2},{8,12},{10,14},{12,8},{14,10},{1,5},{3,7},... | collective-permute-start | bytes 196616 | tf_op jit(solution)/shard_map/ppermute | solution.py:56
  28.6 4.7 %copy-start.3 = (f32[128,256]{1,0:T(8,128)S(1)}, f32[128,256]{1,0:T(8,128)}, u32[]{:S(2)}) copy-start(f32[128,256]{1,0:T(8,128)} %own.2) | copy-start | bytes 393220
  28.8 10.6 %collective-permute-start.16 = (bf16[512,256]{1,0:T(8,128)(2,1)S(1)}, bf16[512,256]{1,0:T(8,128)(2,1)S(1)}, u32[]{:S(2)}, u32[]{:S(2)}) collective-permute-start(bf16[512,256]{1,0:T(8,128)(2,1)S(1)} %get-tuple-element.46.mine), channel_id=1, source_target_pairs={{0,1},{1,0},{2,3},{3,2},{4,5},{5,4},{6,7},{7,6},{8,9},{9,8},{10,11... | collective-permute-start | bytes 786440 | tf_op jit(solution)/shard_map/ppermute | solution.py:56
  33.4 8.1 %collective-permute-start.20 = (bf16[128,256]{1,0:T(8,128)(2,1)S(1)}, bf16[128,256]{1,0:T(8,128)(2,1)S(1)}, u32[]{:S(2)}, u32[]{:S(2)}) collective-permute-start(bf16[128,256]{1,0:T(8,128)(2,1)S(1)} %get-tuple-element.39.refs_1_), channel_id=1, source_target_pairs={{0,10},{2,8},{4,14},{6,12},{8,2},{10,0},{12,6},{14,4},{1,11},{3,9}... | collective-permute-start | bytes 196616 | tf_op jit(solution)/shard_map/ppermute | solution.py:56
  35.9 7.2 %collective-permute-start.19 = (bf16[128,256]{1,0:T(8,128)(2,1)S(1)}, bf16[128,256]{1,0:T(8,128)(2,1)S(1)}, u32[]{:S(2)}, u32[]{:S(2)}) collective-permute-start(bf16[128,256]{1,0:T(8,128)(2,1)S(1)} %get-tuple-element.39.refs_1_), channel_id=1, source_target_pairs={{0,14},{2,12},{4,10},{6,8},{8,6},{10,4},{12,2},{14,0},{1,15},{3,13... | collective-permute-start | bytes 196616 | tf_op jit(solution)/shard_map/ppermute | solution.py:56
  37.1 6.9 %collective-permute-start.18 = (bf16[128,256]{1,0:T(8,128)(2,1)S(1)}, bf16[128,256]{1,0:T(8,128)(2,1)S(1)}, u32[]{:S(2)}, u32[]{:S(2)}) collective-permute-start(bf16[128,256]{1,0:T(8,128)(2,1)S(1)} %get-tuple-element.39.refs_1_), channel_id=1, source_target_pairs={{0,2},{2,0},{4,6},{6,4},{8,10},{10,8},{12,14},{14,12},{1,3},{3,1},... | collective-permute-start | bytes 196616 | tf_op jit(solution)/shard_map/ppermute | solution.py:56
  38.2 6.5 %collective-permute-start.17 = (bf16[128,256]{1,0:T(8,128)(2,1)S(1)}, bf16[128,256]{1,0:T(8,128)(2,1)S(1)}, u32[]{:S(2)}, u32[]{:S(2)}) collective-permute-start(bf16[128,256]{1,0:T(8,128)(2,1)S(1)} %get-tuple-element.39.refs_1_), channel_id=1, source_target_pairs={{0,6},{2,4},{4,2},{6,0},{8,14},{10,12},{12,10},{14,8},{1,7},{3,5},... | collective-permute-start | bytes 196616 | tf_op jit(solution)/shard_map/ppermute | solution.py:56
  39.4 7.0 %collective-permute-start.14 = (bf16[128,256]{1,0:T(8,128)(2,1)S(1)}, bf16[128,256]{1,0:T(8,128)(2,1)S(1)}, u32[]{:S(2)}, u32[]{:S(2)}) collective-permute-start(bf16[128,256]{1,0:T(8,128)(2,1)S(1)} %get-tuple-element.39.refs_1_), channel_id=1, source_target_pairs={{0,12},{2,14},{4,8},{6,10},{8,4},{10,6},{12,0},{14,2},{1,13},{3,15... | collective-permute-start | bytes 196616 | tf_op jit(solution)/shard_map/ppermute | solution.py:56
  41.5 6.0 %collective-permute-start.13 = (bf16[128,256]{1,0:T(8,128)(2,1)S(1)}, bf16[128,256]{1,0:T(8,128)(2,1)S(1)}, u32[]{:S(2)}, u32[]{:S(2)}) collective-permute-start(bf16[128,256]{1,0:T(8,128)(2,1)S(1)} %get-tuple-element.39.refs_1_), channel_id=1, source_target_pairs={{0,8},{2,10},{4,12},{6,14},{8,0},{10,2},{12,4},{14,6},{1,9},{3,11}... | collective-permute-start | bytes 196616 | tf_op jit(solution)/shard_map/ppermute | solution.py:56
  43.1 4.8 %collective-permute-start.12 = (bf16[128,256]{1,0:T(8,128)(2,1)S(1)}, bf16[128,256]{1,0:T(8,128)(2,1)S(1)}, u32[]{:S(2)}, u32[]{:S(2)}) collective-permute-start(bf16[128,256]{1,0:T(8,128)(2,1)S(1)} %get-tuple-element.39.refs_1_), channel_id=1, source_target_pairs={{0,4},{2,6},{4,0},{6,2},{8,12},{10,14},{12,8},{14,10},{1,5},{3,7},... | collective-permute-start | bytes 196616 | tf_op jit(solution)/shard_map/ppermute | solution.py:56
  45.6 6.4 %collective-permute-start.21 = (bf16[4,128,256]{2,1,0:T(8,128)(2,1)S(1)}, bf16[4,128,256]{2,1,0:T(8,128)(2,1)S(1)}, u32[]{:S(2)}, u32[]{:S(2)}) collective-permute-start(bf16[4,128,256]{2,1,0:T(8,128)(2,1)S(1)} %get-tuple-element.48), channel_id=1, source_target_pairs={{0,2},{2,0},{4,6},{6,4},{8,10},{10,8},{12,14},{14,12},{1,3},{3,1},... | collective-permute-start | bytes 786440 | tf_op jit(solution)/shard_map/ppermute | solution.py:56
  49.8 5.9 %collective-permute-start.25 = (bf16[512,256]{1,0:T(8,128)(2,1)S(1)}, bf16[512,256]{1,0:T(8,128)(2,1)S(1)}, u32[]{:S(2)}, u32[]{:S(2)}) collective-permute-start(bf16[512,256]{1,0:T(8,128)(2,1)S(1)} %get-tuple-element.59), channel_id=1, source_target_pairs={{0,1},{1,0},{2,3},{3,2},{4,5},{5,4},{6,7},{7,6},{8,9},{9,8},{10,11... | collective-permute-start | bytes 786440 | tf_op jit(solution)/shard_map/ppermute | solution.py:56
  52.1 5.9 %collective-permute-start.22 = (bf16[128,256]{1,0:T(8,128)(2,1)S(1)}, bf16[128,256]{1,0:T(8,128)(2,1)S(1)}, u32[]{:S(2)}, u32[]{:S(2)}) collective-permute-start(bf16[128,256]{1,0:T(8,128)(2,1)S(1)} %get-tuple-element.50), channel_id=1, source_target_pairs={{0,8},{2,10},{4,12},{6,14},{8,0},{10,2},{12,4},{14,6},{1,9},{3,11}... | collective-permute-start | bytes 196616 | tf_op jit(solution)/shard_map/ppermute | solution.py:56
  53.5 6.2 %collective-permute-start.23 = (bf16[128,256]{1,0:T(8,128)(2,1)S(1)}, bf16[128,256]{1,0:T(8,128)(2,1)S(1)}, u32[]{:S(2)}, u32[]{:S(2)}) collective-permute-start(bf16[128,256]{1,0:T(8,128)(2,1)S(1)} %get-tuple-element.51), channel_id=1, source_target_pairs={{0,12},{2,14},{4,8},{6,10},{8,4},{10,6},{12,0},{14,2},{1,13},{3,15... | collective-permute-start | bytes 196616 | tf_op jit(solution)/shard_map/ppermute | solution.py:56
  55.2 5.0 %collective-permute-start.24 = (bf16[128,256]{1,0:T(8,128)(2,1)S(1)}, bf16[128,256]{1,0:T(8,128)(2,1)S(1)}, u32[]{:S(2)}, u32[]{:S(2)}) collective-permute-start(bf16[128,256]{1,0:T(8,128)(2,1)S(1)} %get-tuple-element.52), channel_id=1, source_target_pairs={{0,4},{2,6},{4,0},{6,2},{8,12},{10,14},{12,8},{14,10},{1,5},{3,7},... | collective-permute-start | bytes 196616 | tf_op jit(solution)/shard_map/ppermute | solution.py:56

commit v6 on v5

--- a/solution.py
+++ b/solution.py
@@ -37,7 +37,7 @@
     return jax.ShapeDtypeStruct(tuple(shape), dtype)
 
 
-def call(body, out_shape, scalars, arrays, scratch=()):
+def call(body, out_shape, scalars, arrays, scratch=(), cost=COST):
     room = sum(
         math.prod(x.shape) * jnp.dtype(x.dtype).itemsize for x in (*out_shape, *arrays, *scratch)
     )
@@ -47,7 +47,7 @@
         in_specs=[smem()] * len(scalars) + [vmem()] * len(arrays),
         out_specs=(vmem(),) * len(out_shape),
         scratch_shapes=list(scratch),
-        cost_estimate=pl.CostEstimate(flops=COST, bytes_accessed=0, transcendentals=0),
+        cost_estimate=pl.CostEstimate(flops=cost, bytes_accessed=0, transcendentals=0),
         compiler_params=pltpu.CompilerParams(vmem_limit_bytes=room + 4 * 2**20),
     )(*scalars, *arrays)
 
@@ -60,8 +60,8 @@
     return ref[pl.ds(pl.multiple_of(place * size, size), size), :]
 
 
-def cast_body(rows, low):
-    low[...] = rows[...].astype(BF16)
+def cast_body(scale, rows, low):
+    low[...] = (scale * rows[...]).astype(BF16)
 
 
 def sign_body(position, count, outcome, sign):
@@ -102,7 +102,7 @@
         total = None
         for c in range(0, across, wide):
             v = lvl[c * blk : (c + wide) * blk, :]
-            t = jnp.tanh(0.5 * dot(u, v, NT))
+            t = jnp.tanh(dot(u, v, NT))
             for g in range(0, tall, blk):
                 i, q = divmod((at + g) // blk, owned)
                 first = ((me ^ partners[i]) * owned + q) * across
@@ -131,14 +131,14 @@
     send[...] = window(acc, me ^ 1, half).astype(BF16)
 
 
-def settle_body(n_out, own, *refs):
+def settle_body(n_out, times, scale, own, *refs):
     got, outs = refs[:-n_out], refs[-n_out:]
     grad = got[0][...].astype(F32)
     for other in got[1:]:
         grad += other[...].astype(F32)
-    value = own[...] - learn_rate * (0.5 * grad + decay_rate * own[...])
+    value = own[...] - learn_rate * (times * grad + decay_rate * own[...])
     for out in outs:
-        out[...] = value.astype(out.dtype)
+        out[...] = (value if out.dtype == F32 else scale * value).astype(out.dtype)
 
 
 def per_device(n_lvl, n_stu, groups, student_factor, level_factor, block_position, block_count, outcome):
@@ -148,9 +148,9 @@
     half = lvl_own.shape[0]
     lvl_rows = n_stu * half
     blocks = n_lvl * own // blk * (lvl_rows // blk)
-    (stu_low,) = call(cast_body, [sds((own, rank), BF16)], (), (stu_own,))
+    (stu_low,) = call(functools.partial(cast_body, 0.5), [sds((own, rank), BF16)], (), (stu_own,))
     later, _ = lax.optimization_barrier((lvl_own, stu_low))
-    (lvl_low,) = call(cast_body, [sds((half, rank), BF16)], (), (later,))
+    (lvl_low,) = call(functools.partial(cast_body, 1.0), [sds((half, rank), BF16)], (), (later,))
     (sign,) = call(
         sign_body,
         [sds((blocks, blk, blk), BF16)],
@@ -201,17 +201,18 @@
             (pltpu.VMEM((lvl_rows, rank), F32),),
         )
         lvl_own, *lows = call(
-            functools.partial(settle_body, len(kinds)),
+            functools.partial(settle_body, len(kinds), 1.0, 1.0),
             [sds((half, rank), kind) for kind in kinds],
             (),
             (lvl_own, keep, swap(send, "stu", n_stu, 1)),
         )
         lvl_low = lows[0] if lows else None
         stu_own, *lows = call(
-            functools.partial(settle_body, len(kinds)),
+            functools.partial(settle_body, len(kinds), 0.5, 0.5),
             [sds((own, rank), kind) for kind in kinds],
             (),
             (stu_own, *(back[i] for i in (n - 1, *reversed(range(n // 2)), *range(n // 2, n - 1)))),
+            cost=8 * COST,
         )
         stu_low = lows[0] if lows else None
     return (stu_own, lvl_own)

time: 61 us -> 60.9 us (level)
  waiting for transfers between devices: 17.8 us -> 16.5 us
  starting transfers between devices: 32.1 us -> 33.2 us
    ppermute x26, waiting for transfers between devices: 17.8 us -> 16.5 us  [swap(): return lax.ppermute(x, axis, [(i, i ^ k) for i in range(n)])]
    ppermute x26, starting transfers between devices: 32.1 us -> 33.2 us  [swap(): return lax.ppermute(x, axis, [(i, i ^ k) for i in range(n)])]
  transfers between devices with their start and end apart: 26 -> 26, of which waited for: 13 -> 12; matrix products, arithmetic and copies ran while one was open for 0% -> 0% of each run, Pallas kernels for 13% -> 13%
where the time goes in v6:
time: 60.9 us; the launch traced here: 60.7 us
  starting transfers between devices  33.2 us (55%)
  waiting for transfers between devices  16.5 us (27%)
  Pallas kernels  8.5 us (14%)
  between operations  1.49 us (2%)
  local copies, waits for them, and re-layouts  0.98 us (2%)
    ppermute x26, starting transfers between devices, swap(): return lax.ppermute(x, axis, [(i, i ^ k) for i in range(n)])  33.2 us
    ppermute x26, waiting for transfers between devices, swap(): return lax.ppermute(x, axis, [(i, i ^ k) for i in range(n)])  16.5 us
    pallas_call x17, Pallas kernels, call(): pl.pallas_call(body, out_shape=tuple(out_shape), in_specs=[smem()] * len(...  8.5 us
  transfers between devices with their start and end apart: 26, of which 12 were waited for; matrix products, arithmetic and copies ran while one was open for 0% of the time, Pallas kernels for 13%

profile of v6, /device:TPU:0, one launch (start us, length us, event | category | flops | bytes accessed | tf_op | source)
XLA Modules:
  0.0 60.7 jit_solution(9913589623272873539)
XLA Ops:
  0.7 1.0 %copy-done.2 = f32[128,256]{1,0:T(8,128)S(1)} copy-done((f32[128,256]{1,0:T(8,128)S(1)}, f32[128,256]{1,0:T(8,128)}, u32[]{:S(2)}) %copy-start.2) | copy-done | bytes 131096
  1.6 5.1 %collective-permute-start.7 = (bf16[128,256]{1,0:T(8,128)(2,1)S(1)}, bf16[128,256]{1,0:T(8,128)(2,1)S(1)}, u32[]{:S(2)}, u32[]{:S(2)}) collective-permute-start(bf16[128,256]{1,0:T(8,128)(2,1)S(1)} %shard_map.68.refs_1_), channel_id=1, source_target_pairs={{0,10},{2,8},{4,14},{6,12},{8,2},{10,0},{12,6},{14,4},{1,11},{3,9}... | collective-permute-start | bytes 196616 | tf_op jit(solution)/shard_map/ppermute | solution.py:56
  6.7 1.3 %collective-permute-start.6 = (bf16[128,256]{1,0:T(8,128)(2,1)S(1)}, bf16[128,256]{1,0:T(8,128)(2,1)S(1)}, u32[]{:S(2)}, u32[]{:S(2)}) collective-permute-start(bf16[128,256]{1,0:T(8,128)(2,1)S(1)} %shard_map.68.refs_1_), channel_id=1, source_target_pairs={{0,14},{2,12},{4,10},{6,8},{8,6},{10,4},{12,2},{14,0},{1,15},{3,13... | collective-permute-start | bytes 196616 | tf_op jit(solution)/shard_map/ppermute | solution.py:56
  8.0 1.5 %collective-permute-start.5 = (bf16[128,256]{1,0:T(8,128)(2,1)S(1)}, bf16[128,256]{1,0:T(8,128)(2,1)S(1)}, u32[]{:S(2)}, u32[]{:S(2)}) collective-permute-start(bf16[128,256]{1,0:T(8,128)(2,1)S(1)} %shard_map.68.refs_1_), channel_id=1, source_target_pairs={{0,2},{2,0},{4,6},{6,4},{8,10},{10,8},{12,14},{14,12},{1,3},{3,1},... | collective-permute-start | bytes 196616 | tf_op jit(solution)/shard_map/ppermute | solution.py:56
  10.5 0.9 %shard_map.71.refs_5_ = bf16[64,128,128]{2,1,0:T(8,128)(2,1)S(1)} custom-call(s32[24]{0:T(128)S(1)} %bitcast.3, s32[1,1]{1,0:T(1,128)S(6)} %copy.7.count, s32[24,128,128]{2,1,0:T(8,128)S(1)} %bitcast.2), custom_call_target="tpu_custom_call" | custom-call | flops 10000000000 | tf_op jit(solution)/shard_map/pallas_call | solution.py:44
  11.5 2.8 %collective-permute-start.2 = (bf16[128,256]{1,0:T(8,128)(2,1)S(1)}, bf16[128,256]{1,0:T(8,128)(2,1)S(1)}, u32[]{:S(2)}, u32[]{:S(2)}) collective-permute-start(bf16[128,256]{1,0:T(8,128)(2,1)S(1)} %shard_map.68.refs_1_), channel_id=1, source_target_pairs={{0,12},{2,14},{4,8},{6,10},{8,4},{10,6},{12,0},{14,2},{1,13},{3,15... | collective-permute-start | bytes 196616 | tf_op jit(solution)/shard_map/ppermute | solution.py:56
  14.9 1.3 %collective-permute-start = (bf16[128,256]{1,0:T(8,128)(2,1)S(1)}, bf16[128,256]{1,0:T(8,128)(2,1)S(1)}, u32[]{:S(2)}, u32[]{:S(2)}) collective-permute-start(bf16[128,256]{1,0:T(8,128)(2,1)S(1)} %shard_map.68.refs_1_), channel_id=1, source_target_pairs={{0,4},{2,6},{4,0},{6,2},{8,12},{10,14},{12,8},{14,10},{1,5},{3,7},... | collective-permute-start | bytes 196616 | tf_op jit(solution)/shard_map/ppermute | solution.py:56
  16.2 1.0 %shard_map.73 = (bf16[512,1024]{1,0:T(8,128)(2,1)S(1)}, bf16[512,256]{1,0:T(8,128)(2,1)S(1)}, bf16[4,128,256]{2,1,0:T(8,128)(2,1)S(1)}) custom-call(bf16[128,256]{1,0:T(8,128)(2,1)S(1)} %collective-permute-done.4.refs_0_, bf16[128,256]{1,0:T(8,128)(2,1)S(1)} %collective-permute-done.5.refs_1_, bf16[128,256]{1,0:T(8,128)(2,1)S(1)} %collective-permute-done.6.refs_2_, ...), custom_call_target="tpu_custom_call" | custom-call | flops 10000000000 | tf_op jit(solution)/shard_map/pallas_call | solution.py:44
  17.1 1.6 %collective-permute-start.8 = (bf16[4,128,256]{2,1,0:T(8,128)(2,1)S(1)}, bf16[4,128,256]{2,1,0:T(8,128)(2,1)S(1)}, u32[]{:S(2)}, u32[]{:S(2)}) collective-permute-start(bf16[4,128,256]{2,1,0:T(8,128)(2,1)S(1)} %get-tuple-element.33), channel_id=1, source_target_pairs={{0,2},{2,0},{4,6},{6,4},{8,10},{10,8},{12,14},{14,12},{1,3},{3,1},... | collective-permute-start | bytes 786440 | tf_op jit(solution)/shard_map/ppermute | solution.py:56
  18.7 2.7 %collective-permute-done.1.refs_2_ = bf16[128,256]{1,0:T(8,128)(2,1)S(1)} collective-permute-done((bf16[128,256]{1,0:T(8,128)(2,1)S(1)}, bf16[128,256]{1,0:T(8,128)(2,1)S(1)}, u32[]{:S(2)}, u32[]{:S(2)}) %collective-permute-start.1) | collective-permute-done | bytes 65568 | tf_op jit(solution)/shard_map/ppermute | solution.py:56
  21.4 1.0 %shard_map.72 = (bf16[512,1024]{1,0:T(8,128)(2,1)S(1)}, bf16[512,256]{1,0:T(8,128)(2,1)S(1)}, f32[4,128,256]{2,1,0:T(8,128)S(1)}) custom-call(bf16[128,256]{1,0:T(8,128)(2,1)S(1)} %collective-permute-done.refs_0_, bf16[128,256]{1,0:T(8,128)(2,1)S(1)} %shard_map.68.refs_1_, bf16[128,256]{1,0:T(8,128)(2,1)S(1)} %collective-permute-done.1.refs_2_, ...), custom_call_target="tpu_custom_call" | custom-call | flops 10000000000 | tf_op jit(solution)/shard_map/pallas_call | solution.py:44
  22.3 0.9 %shard_map.76 = (f32[512,256]{1,0:T(8,128)S(1)}, bf16[512,256]{1,0:T(8,128)(2,1)S(1)}) custom-call(bf16[512,1024]{1,0:T(8,128)(2,1)S(1)} %get-tuple-element.40.refs_0_, bf16[512,1024]{1,0:T(8,128)(2,1)S(1)} %get-tuple-element.41.refs_1_, bf16[512,256]{1,0:T(8,128)(2,1)S(1)} %get-tuple-element.42.refs_2_, bf16[512,256]{1,0:T(8,128)(2,1)S(1)} %get-tuple-element.43.refs_3_), custom_call_target="tpu_custom_call" | custom-call | flops 10000000000 | tf_op jit(solution)/shard_map/pallas_call | solution.py:44
  23.3 1.7 %collective-permute-done.8.other = bf16[4,128,256]{2,1,0:T(8,128)(2,1)S(1)} collective-permute-done((bf16[4,128,256]{2,1,0:T(8,128)(2,1)S(1)}, bf16[4,128,256]{2,1,0:T(8,128)(2,1)S(1)}, u32[]{:S(2)}, u32[]{:S(2)}) %collective-permute-start.8) | collective-permute-done | bytes 262176 | tf_op jit(solution)/shard_map/ppermute | solution.py:56
  25.0 2.0 %collective-permute-start.9 = (bf16[128,256]{1,0:T(8,128)(2,1)S(1)}, bf16[128,256]{1,0:T(8,128)(2,1)S(1)}, u32[]{:S(2)}, u32[]{:S(2)}) collective-permute-start(bf16[128,256]{1,0:T(8,128)(2,1)S(1)} %get-tuple-element.35), channel_id=1, source_target_pairs={{0,8},{2,10},{4,12},{6,14},{8,0},{10,2},{12,4},{14,6},{1,9},{3,11}... | collective-permute-start | bytes 196616 | tf_op jit(solution)/shard_map/ppermute | solution.py:56
  27.0 1.3 %collective-permute-start.10 = (bf16[128,256]{1,0:T(8,128)(2,1)S(1)}, bf16[128,256]{1,0:T(8,128)(2,1)S(1)}, u32[]{:S(2)}, u32[]{:S(2)}) collective-permute-start(bf16[128,256]{1,0:T(8,128)(2,1)S(1)} %get-tuple-element.36), channel_id=1, source_target_pairs={{0,12},{2,14},{4,8},{6,10},{8,4},{10,6},{12,0},{14,2},{1,13},{3,15... | collective-permute-start | bytes 196616 | tf_op jit(solution)/shard_map/ppermute | solution.py:56
  28.8 3.2 %collective-permute-done.9.refs_1_ = bf16[128,256]{1,0:T(8,128)(2,1)S(1)} collective-permute-done((bf16[128,256]{1,0:T(8,128)(2,1)S(1)}, bf16[128,256]{1,0:T(8,128)(2,1)S(1)}, u32[]{:S(2)}, u32[]{:S(2)}) %collective-permute-start.9) | collective-permute-done | bytes 65568 | tf_op jit(solution)/shard_map/ppermute | solution.py:56
  32.0 1.3 %collective-permute-done.10.refs_2_ = bf16[128,256]{1,0:T(8,128)(2,1)S(1)} collective-permute-done((bf16[128,256]{1,0:T(8,128)(2,1)S(1)}, bf16[128,256]{1,0:T(8,128)(2,1)S(1)}, u32[]{:S(2)}, u32[]{:S(2)}) %collective-permute-start.10) | collective-permute-done | bytes 65568 | tf_op jit(solution)/shard_map/ppermute | solution.py:56
  33.4 2.3 %collective-permute-start.20 = (bf16[128,256]{1,0:T(8,128)(2,1)S(1)}, bf16[128,256]{1,0:T(8,128)(2,1)S(1)}, u32[]{:S(2)}, u32[]{:S(2)}) collective-permute-start(bf16[128,256]{1,0:T(8,128)(2,1)S(1)} %get-tuple-element.39.refs_1_), channel_id=1, source_target_pairs={{0,10},{2,8},{4,14},{6,12},{8,2},{10,0},{12,6},{14,4},{1,11},{3,9}... | collective-permute-start | bytes 196616 | tf_op jit(solution)/shard_map/ppermute | solution.py:56
  35.7 1.6 %collective-permute-start.19 = (bf16[128,256]{1,0:T(8,128)(2,1)S(1)}, bf16[128,256]{1,0:T(8,128)(2,1)S(1)}, u32[]{:S(2)}, u32[]{:S(2)}) collective-permute-start(bf16[128,256]{1,0:T(8,128)(2,1)S(1)} %get-tuple-element.39.refs_1_), channel_id=1, source_target_pairs={{0,14},{2,12},{4,10},{6,8},{8,6},{10,4},{12,2},{14,0},{1,15},{3,13... | collective-permute-start | bytes 196616 | tf_op jit(solution)/shard_map/ppermute | solution.py:56
  38.2 1.2 %collective-permute-start.17 = (bf16[128,256]{1,0:T(8,128)(2,1)S(1)}, bf16[128,256]{1,0:T(8,128)(2,1)S(1)}, u32[]{:S(2)}, u32[]{:S(2)}) collective-permute-start(bf16[128,256]{1,0:T(8,128)(2,1)S(1)} %get-tuple-element.39.refs_1_), channel_id=1, source_target_pairs={{0,6},{2,4},{4,2},{6,0},{8,14},{10,12},{12,10},{14,8},{1,7},{3,5},... | collective-permute-start | bytes 196616 | tf_op jit(solution)/shard_map/ppermute | solution.py:56
  39.4 2.2 %collective-permute-start.14 = (bf16[128,256]{1,0:T(8,128)(2,1)S(1)}, bf16[128,256]{1,0:T(8,128)(2,1)S(1)}, u32[]{:S(2)}, u32[]{:S(2)}) collective-permute-start(bf16[128,256]{1,0:T(8,128)(2,1)S(1)} %get-tuple-element.39.refs_1_), channel_id=1, source_target_pairs={{0,12},{2,14},{4,8},{6,10},{8,4},{10,6},{12,0},{14,2},{1,13},{3,15... | collective-permute-start | bytes 196616 | tf_op jit(solution)/shard_map/ppermute | solution.py:56
  42.7 2.4 %collective-permute-start.12 = (bf16[128,256]{1,0:T(8,128)(2,1)S(1)}, bf16[128,256]{1,0:T(8,128)(2,1)S(1)}, u32[]{:S(2)}, u32[]{:S(2)}) collective-permute-start(bf16[128,256]{1,0:T(8,128)(2,1)S(1)} %get-tuple-element.39.refs_1_), channel_id=1, source_target_pairs={{0,4},{2,6},{4,0},{6,2},{8,12},{10,14},{12,8},{14,10},{1,5},{3,7},... | collective-permute-start | bytes 196616 | tf_op jit(solution)/shard_map/ppermute | solution.py:56
  45.1 1.0 %shard_map.80 = (bf16[512,1024]{1,0:T(8,128)(2,1)S(1)}, bf16[512,256]{1,0:T(8,128)(2,1)S(1)}, bf16[4,128,256]{2,1,0:T(8,128)(2,1)S(1)}) custom-call(bf16[128,256]{1,0:T(8,128)(2,1)S(1)} %collective-permute-done.17.refs_0_, bf16[128,256]{1,0:T(8,128)(2,1)S(1)} %collective-permute-done.18.refs_1_, bf16[128,256]{1,0:T(8,128)(2,1)S(1)} %collective-permute-done.19.refs_2_, ...), custom_call_target="tpu_custom_call" | custom-call | flops 10000000000 | tf_op jit(solution)/shard_map/pallas_call | solution.py:44
  46.3 1.3 %collective-permute-done.13.refs_2_ = bf16[128,256]{1,0:T(8,128)(2,1)S(1)} collective-permute-done((bf16[128,256]{1,0:T(8,128)(2,1)S(1)}, bf16[128,256]{1,0:T(8,128)(2,1)S(1)}, u32[]{:S(2)}, u32[]{:S(2)}) %collective-permute-start.13) | collective-permute-done | bytes 65568 | tf_op jit(solution)/shard_map/ppermute | solution.py:56
  47.9 1.0 %shard_map.79 = (bf16[512,1024]{1,0:T(8,128)(2,1)S(1)}, bf16[512,256]{1,0:T(8,128)(2,1)S(1)}, f32[4,128,256]{2,1,0:T(8,128)S(1)}) custom-call(bf16[128,256]{1,0:T(8,128)(2,1)S(1)} %collective-permute-done.12.refs_0_, bf16[128,256]{1,0:T(8,128)(2,1)S(1)} %get-tuple-element.39.refs_1_, bf16[128,256]{1,0:T(8,128)(2,1)S(1)} %collective-permute-done.13.refs_2_, ...), custom_call_target="tpu_custom_call" | custom-call | flops 10000000000 | tf_op jit(solution)/shard_map/pallas_call | solution.py:44
  48.9 0.9 %shard_map.83 = (f32[512,256]{1,0:T(8,128)S(1)}, bf16[512,256]{1,0:T(8,128)(2,1)S(1)}) custom-call(bf16[512,1024]{1,0:T(8,128)(2,1)S(1)} %get-tuple-element.54.refs_0_, bf16[512,1024]{1,0:T(8,128)(2,1)S(1)} %get-tuple-element.55.refs_1_, bf16[512,256]{1,0:T(8,128)(2,1)S(1)} %get-tuple-element.56.refs_2_, bf16[512,256]{1,0:T(8,128)(2,1)S(1)} %get-tuple-element.57.refs_3_), custom_call_target="tpu_custom_call" | custom-call | flops 10000000000 | tf_op jit(solution)/shard_map/pallas_call | solution.py:44
  49.8 2.7 %collective-permute-done.21.other = bf16[4,128,256]{2,1,0:T(8,128)(2,1)S(1)} collective-permute-done((bf16[4,128,256]{2,1,0:T(8,128)(2,1)S(1)}, bf16[4,128,256]{2,1,0:T(8,128)(2,1)S(1)}, u32[]{:S(2)}, u32[]{:S(2)}) %collective-permute-start.21) | collective-permute-done | bytes 262176 | tf_op jit(solution)/shard_map/ppermute | solution.py:56
  53.4 1.6 %collective-permute-start.23 = (bf16[128,256]{1,0:T(8,128)(2,1)S(1)}, bf16[128,256]{1,0:T(8,128)(2,1)S(1)}, u32[]{:S(2)}, u32[]{:S(2)}) collective-permute-start(bf16[128,256]{1,0:T(8,128)(2,1)S(1)} %get-tuple-element.51), channel_id=1, source_target_pairs={{0,12},{2,14},{4,8},{6,10},{8,4},{10,6},{12,0},{14,2},{1,13},{3,15... | collective-permute-start | bytes 196616 | tf_op jit(solution)/shard_map/ppermute | solution.py:56
  55.0 1.1 %collective-permute-start.24 = (bf16[128,256]{1,0:T(8,128)(2,1)S(1)}, bf16[128,256]{1,0:T(8,128)(2,1)S(1)}, u32[]{:S(2)}, u32[]{:S(2)}) collective-permute-start(bf16[128,256]{1,0:T(8,128)(2,1)S(1)} %get-tuple-element.52), channel_id=1, source_target_pairs={{0,4},{2,6},{4,0},{6,2},{8,12},{10,14},{12,8},{14,10},{1,5},{3,7},... | collective-permute-start | bytes 196616 | tf_op jit(solution)/shard_map/ppermute | solution.py:56
  56.1 0.9 %shard_map.84 = f32[512,256]{1,0:T(8,128)} custom-call(f32[512,256]{1,0:T(8,128)S(1)} %get-tuple-element.53.own, f32[512,256]{1,0:T(8,128)S(1)} %get-tuple-element.58.refs_0_, bf16[512,256]{1,0:T(8,128)(2,1)S(1)} %collective-permute-done.25.refs_1_), custom_call_target="tpu_custom_call" | custom-call | flops 10000000000 | tf_op jit(solution)/shard_map/pallas_call | solution.py:44
  57.0 1.2 %collective-permute-done.22.refs_1_ = bf16[128,256]{1,0:T(8,128)(2,1)S(1)} collective-permute-done((bf16[128,256]{1,0:T(8,128)(2,1)S(1)}, bf16[128,256]{1,0:T(8,128)(2,1)S(1)}, u32[]{:S(2)}, u32[]{:S(2)}) %collective-permute-start.22) | collective-permute-done | bytes 65568 | tf_op jit(solution)/shard_map/ppermute | solution.py:56
  58.2 1.4 %collective-permute-done.23.refs_2_ = bf16[128,256]{1,0:T(8,128)(2,1)S(1)} collective-permute-done((bf16[128,256]{1,0:T(8,128)(2,1)S(1)}, bf16[128,256]{1,0:T(8,128)(2,1)S(1)}, u32[]{:S(2)}, u32[]{:S(2)}) %collective-permute-start.23) | collective-permute-done | bytes 65568 | tf_op jit(solution)/shard_map/ppermute | solution.py:56
  (47 shorter events, 6.1 us)
Async XLA Ops:
  0.6 9.1 %copy-start.1 = (f32[512,256]{1,0:T(8,128)S(1)}, f32[512,256]{1,0:T(8,128)}, u32[]{:S(2)}) copy-start(f32[512,256]{1,0:T(8,128)} %own.3) | copy-start | bytes 1572868
  0.6 1.0 %copy-start.2 = (f32[128,256]{1,0:T(8,128)S(1)}, f32[128,256]{1,0:T(8,128)}, u32[]{:S(2)}) copy-start(f32[128,256]{1,0:T(8,128)} %own.2) | copy-start | bytes 393220
  1.6 8.9 %copy-start = (s32[1,1,24,128,128]{4,3,2,1,0:T(8,128)S(1)}, s32[1,1,24,128,128]{4,3,2,1,0:T(8,128)}, u32[]{:S(2)}) copy-start(s32[1,1,24,128,128]{4,3,2,1,0:T(8,128)} %param.9) | copy-start | bytes 4718596
  1.6 8.9 %copy-start.4 = (s32[1,1,24]{2,1,0:T(1,128)S(1)}, s32[1,1,24]{2,1,0:T(1,128)}, u32[]{:S(2)}) copy-start(s32[1,1,24]{2,1,0:T(1,128)} %param.7) | copy-start | bytes 292
  1.6 12.7 %collective-permute-start.7 = (bf16[128,256]{1,0:T(8,128)(2,1)S(1)}, bf16[128,256]{1,0:T(8,128)(2,1)S(1)}, u32[]{:S(2)}, u32[]{:S(2)}) collective-permute-start(bf16[128,256]{1,0:T(8,128)(2,1)S(1)} %shard_map.68.refs_1_), channel_id=1, source_target_pairs={{0,10},{2,8},{4,14},{6,12},{8,2},{10,0},{12,6},{14,4},{1,11},{3,9}... | collective-permute-start | bytes 196616 | tf_op jit(solution)/shard_map/ppermute | solution.py:56
  6.7 8.2 %collective-permute-start.6 = (bf16[128,256]{1,0:T(8,128)(2,1)S(1)}, bf16[128,256]{1,0:T(8,128)(2,1)S(1)}, u32[]{:S(2)}, u32[]{:S(2)}) collective-permute-start(bf16[128,256]{1,0:T(8,128)(2,1)S(1)} %shard_map.68.refs_1_), channel_id=1, source_target_pairs={{0,14},{2,12},{4,10},{6,8},{8,6},{10,4},{12,2},{14,0},{1,15},{3,13... | collective-permute-start | bytes 196616 | tf_op jit(solution)/shard_map/ppermute | solution.py:56
  8.0 8.2 %collective-permute-start.5 = (bf16[128,256]{1,0:T(8,128)(2,1)S(1)}, bf16[128,256]{1,0:T(8,128)(2,1)S(1)}, u32[]{:S(2)}, u32[]{:S(2)}) collective-permute-start(bf16[128,256]{1,0:T(8,128)(2,1)S(1)} %shard_map.68.refs_1_), channel_id=1, source_target_pairs={{0,2},{2,0},{4,6},{6,4},{8,10},{10,8},{12,14},{14,12},{1,3},{3,1},... | collective-permute-start | bytes 196616 | tf_op jit(solution)/shard_map/ppermute | solution.py:56
  9.5 6.6 %collective-permute-start.4 = (bf16[128,256]{1,0:T(8,128)(2,1)S(1)}, bf16[128,256]{1,0:T(8,128)(2,1)S(1)}, u32[]{:S(2)}, u32[]{:S(2)}) collective-permute-start(bf16[128,256]{1,0:T(8,128)(2,1)S(1)} %shard_map.68.refs_1_), channel_id=1, source_target_pairs={{0,6},{2,4},{4,2},{6,0},{8,14},{10,12},{12,10},{14,8},{1,7},{3,5},... | collective-permute-start | bytes 196616 | tf_op jit(solution)/shard_map/ppermute | solution.py:56
  9.8 1.7 %collective-permute-start.3 = (bf16[512,256]{1,0:T(8,128)(2,1)S(1)}, bf16[512,256]{1,0:T(8,128)(2,1)S(1)}, u32[]{:S(2)}, u32[]{:S(2)}) collective-permute-start(bf16[512,256]{1,0:T(8,128)(2,1)S(1)} %shard_map.69.mine), channel_id=1, source_target_pairs={{0,1},{1,0},{2,3},{3,2},{4,5},{5,4},{6,7},{7,6},{8,9},{9,8},{10,11... | collective-permute-start | bytes 786440 | tf_op jit(solution)/shard_map/ppermute | solution.py:56
  11.5 7.2 %collective-permute-start.2 = (bf16[128,256]{1,0:T(8,128)(2,1)S(1)}, bf16[128,256]{1,0:T(8,128)(2,1)S(1)}, u32[]{:S(2)}, u32[]{:S(2)}) collective-permute-start(bf16[128,256]{1,0:T(8,128)(2,1)S(1)} %shard_map.68.refs_1_), channel_id=1, source_target_pairs={{0,12},{2,14},{4,8},{6,10},{8,4},{10,6},{12,0},{14,2},{1,13},{3,15... | collective-permute-start | bytes 196616 | tf_op jit(solution)/shard_map/ppermute | solution.py:56
  14.4 7.0 %collective-permute-start.1 = (bf16[128,256]{1,0:T(8,128)(2,1)S(1)}, bf16[128,256]{1,0:T(8,128)(2,1)S(1)}, u32[]{:S(2)}, u32[]{:S(2)}) collective-permute-start(bf16[128,256]{1,0:T(8,128)(2,1)S(1)} %shard_map.68.refs_1_), channel_id=1, source_target_pairs={{0,8},{2,10},{4,12},{6,14},{8,0},{10,2},{12,4},{14,6},{1,9},{3,11}... | collective-permute-start | bytes 196616 | tf_op jit(solution)/shard_map/ppermute | solution.py:56
  14.9 6.5 %collective-permute-start = (bf16[128,256]{1,0:T(8,128)(2,1)S(1)}, bf16[128,256]{1,0:T(8,128)(2,1)S(1)}, u32[]{:S(2)}, u32[]{:S(2)}) collective-permute-start(bf16[128,256]{1,0:T(8,128)(2,1)S(1)} %shard_map.68.refs_1_), channel_id=1, source_target_pairs={{0,4},{2,6},{4,0},{6,2},{8,12},{10,14},{12,8},{14,10},{1,5},{3,7},... | collective-permute-start | bytes 196616 | tf_op jit(solution)/shard_map/ppermute | solution.py:56
  17.1 7.9 %collective-permute-start.8 = (bf16[4,128,256]{2,1,0:T(8,128)(2,1)S(1)}, bf16[4,128,256]{2,1,0:T(8,128)(2,1)S(1)}, u32[]{:S(2)}, u32[]{:S(2)}) collective-permute-start(bf16[4,128,256]{2,1,0:T(8,128)(2,1)S(1)} %get-tuple-element.33), channel_id=1, source_target_pairs={{0,2},{2,0},{4,6},{6,4},{8,10},{10,8},{12,14},{14,12},{1,3},{3,1},... | collective-permute-start | bytes 786440 | tf_op jit(solution)/shard_map/ppermute | solution.py:56
  23.2 5.4 %collective-permute-start.15 = (bf16[512,256]{1,0:T(8,128)(2,1)S(1)}, bf16[512,256]{1,0:T(8,128)(2,1)S(1)}, u32[]{:S(2)}, u32[]{:S(2)}) collective-permute-start(bf16[512,256]{1,0:T(8,128)(2,1)S(1)} %get-tuple-element.45), channel_id=1, source_target_pairs={{0,1},{1,0},{2,3},{3,2},{4,5},{5,4},{6,7},{7,6},{8,9},{9,8},{10,11... | collective-permute-start | bytes 786440 | tf_op jit(solution)/shard_map/ppermute | solution.py:56
  25.0 6.9 %collective-permute-start.9 = (bf16[128,256]{1,0:T(8,128)(2,1)S(1)}, bf16[128,256]{1,0:T(8,128)(2,1)S(1)}, u32[]{:S(2)}, u32[]{:S(2)}) collective-permute-start(bf16[128,256]{1,0:T(8,128)(2,1)S(1)} %get-tuple-element.35), channel_id=1, source_target_pairs={{0,8},{2,10},{4,12},{6,14},{8,0},{10,2},{12,4},{14,6},{1,9},{3,11}... | collective-permute-start | bytes 196616 | tf_op jit(solution)/shard_map/ppermute | solution.py:56
  27.0 6.2 %collective-permute-start.10 = (bf16[128,256]{1,0:T(8,128)(2,1)S(1)}, bf16[128,256]{1,0:T(8,128)(2,1)S(1)}, u32[]{:S(2)}, u32[]{:S(2)}) collective-permute-start(bf16[128,256]{1,0:T(8,128)(2,1)S(1)} %get-tuple-element.36), channel_id=1, source_target_pairs={{0,12},{2,14},{4,8},{6,10},{8,4},{10,6},{12,0},{14,2},{1,13},{3,15... | collective-permute-start | bytes 196616 | tf_op jit(solution)/shard_map/ppermute | solution.py:56
  28.3 5.0 %collective-permute-start.11 = (bf16[128,256]{1,0:T(8,128)(2,1)S(1)}, bf16[128,256]{1,0:T(8,128)(2,1)S(1)}, u32[]{:S(2)}, u32[]{:S(2)}) collective-permute-start(bf16[128,256]{1,0:T(8,128)(2,1)S(1)} %get-tuple-element.37), channel_id=1, source_target_pairs={{0,4},{2,6},{4,0},{6,2},{8,12},{10,14},{12,8},{14,10},{1,5},{3,7},... | collective-permute-start | bytes 196616 | tf_op jit(solution)/shard_map/ppermute | solution.py:56
  28.6 4.8 %copy-start.3 = (f32[128,256]{1,0:T(8,128)S(1)}, f32[128,256]{1,0:T(8,128)}, u32[]{:S(2)}) copy-start(f32[128,256]{1,0:T(8,128)} %own.2) | copy-start | bytes 393220
  28.7 10.6 %collective-permute-start.16 = (bf16[512,256]{1,0:T(8,128)(2,1)S(1)}, bf16[512,256]{1,0:T(8,128)(2,1)S(1)}, u32[]{:S(2)}, u32[]{:S(2)}) collective-permute-start(bf16[512,256]{1,0:T(8,128)(2,1)S(1)} %get-tuple-element.46.mine), channel_id=1, source_target_pairs={{0,1},{1,0},{2,3},{3,2},{4,5},{5,4},{6,7},{7,6},{8,9},{9,8},{10,11... | collective-permute-start | bytes 786440 | tf_op jit(solution)/shard_map/ppermute | solution.py:56
  33.4 8.2 %collective-permute-start.20 = (bf16[128,256]{1,0:T(8,128)(2,1)S(1)}, bf16[128,256]{1,0:T(8,128)(2,1)S(1)}, u32[]{:S(2)}, u32[]{:S(2)}) collective-permute-start(bf16[128,256]{1,0:T(8,128)(2,1)S(1)} %get-tuple-element.39.refs_1_), channel_id=1, source_target_pairs={{0,10},{2,8},{4,14},{6,12},{8,2},{10,0},{12,6},{14,4},{1,11},{3,9}... | collective-permute-start | bytes 196616 | tf_op jit(solution)/shard_map/ppermute | solution.py:56
  35.7 7.0 %collective-permute-start.19 = (bf16[128,256]{1,0:T(8,128)(2,1)S(1)}, bf16[128,256]{1,0:T(8,128)(2,1)S(1)}, u32[]{:S(2)}, u32[]{:S(2)}) collective-permute-start(bf16[128,256]{1,0:T(8,128)(2,1)S(1)} %get-tuple-element.39.refs_1_), channel_id=1, source_target_pairs={{0,14},{2,12},{4,10},{6,8},{8,6},{10,4},{12,2},{14,0},{1,15},{3,13... | collective-permute-start | bytes 196616 | tf_op jit(solution)/shard_map/ppermute | solution.py:56
  37.3 7.8 %collective-permute-start.18 = (bf16[128,256]{1,0:T(8,128)(2,1)S(1)}, bf16[128,256]{1,0:T(8,128)(2,1)S(1)}, u32[]{:S(2)}, u32[]{:S(2)}) collective-permute-start(bf16[128,256]{1,0:T(8,128)(2,1)S(1)} %get-tuple-element.39.refs_1_), channel_id=1, source_target_pairs={{0,2},{2,0},{4,6},{6,4},{8,10},{10,8},{12,14},{14,12},{1,3},{3,1},... | collective-permute-start | bytes 196616 | tf_op jit(solution)/shard_map/ppermute | solution.py:56
  38.2 6.9 %collective-permute-start.17 = (bf16[128,256]{1,0:T(8,128)(2,1)S(1)}, bf16[128,256]{1,0:T(8,128)(2,1)S(1)}, u32[]{:S(2)}, u32[]{:S(2)}) collective-permute-start(bf16[128,256]{1,0:T(8,128)(2,1)S(1)} %get-tuple-element.39.refs_1_), channel_id=1, source_target_pairs={{0,6},{2,4},{4,2},{6,0},{8,14},{10,12},{12,10},{14,8},{1,7},{3,5},... | collective-permute-start | bytes 196616 | tf_op jit(solution)/shard_map/ppermute | solution.py:56
  39.4 7.0 %collective-permute-start.14 = (bf16[128,256]{1,0:T(8,128)(2,1)S(1)}, bf16[128,256]{1,0:T(8,128)(2,1)S(1)}, u32[]{:S(2)}, u32[]{:S(2)}) collective-permute-start(bf16[128,256]{1,0:T(8,128)(2,1)S(1)} %get-tuple-element.39.refs_1_), channel_id=1, source_target_pairs={{0,12},{2,14},{4,8},{6,10},{8,4},{10,6},{12,0},{14,2},{1,13},{3,15... | collective-permute-start | bytes 196616 | tf_op jit(solution)/shard_map/ppermute | solution.py:56
  41.6 6.0 %collective-permute-start.13 = (bf16[128,256]{1,0:T(8,128)(2,1)S(1)}, bf16[128,256]{1,0:T(8,128)(2,1)S(1)}, u32[]{:S(2)}, u32[]{:S(2)}) collective-permute-start(bf16[128,256]{1,0:T(8,128)(2,1)S(1)} %get-tuple-element.39.refs_1_), channel_id=1, source_target_pairs={{0,8},{2,10},{4,12},{6,14},{8,0},{10,2},{12,4},{14,6},{1,9},{3,11}... | collective-permute-start | bytes 196616 | tf_op jit(solution)/shard_map/ppermute | solution.py:56
  42.7 5.2 %collective-permute-start.12 = (bf16[128,256]{1,0:T(8,128)(2,1)S(1)}, bf16[128,256]{1,0:T(8,128)(2,1)S(1)}, u32[]{:S(2)}, u32[]{:S(2)}) collective-permute-start(bf16[128,256]{1,0:T(8,128)(2,1)S(1)} %get-tuple-element.39.refs_1_), channel_id=1, source_target_pairs={{0,4},{2,6},{4,0},{6,2},{8,12},{10,14},{12,8},{14,10},{1,5},{3,7},... | collective-permute-start | bytes 196616 | tf_op jit(solution)/shard_map/ppermute | solution.py:56
  46.1 6.4 %collective-permute-start.21 = (bf16[4,128,256]{2,1,0:T(8,128)(2,1)S(1)}, bf16[4,128,256]{2,1,0:T(8,128)(2,1)S(1)}, u32[]{:S(2)}, u32[]{:S(2)}) collective-permute-start(bf16[4,128,256]{2,1,0:T(8,128)(2,1)S(1)} %get-tuple-element.48), channel_id=1, source_target_pairs={{0,2},{2,0},{4,6},{6,4},{8,10},{10,8},{12,14},{14,12},{1,3},{3,1},... | collective-permute-start | bytes 786440 | tf_op jit(solution)/shard_map/ppermute | solution.py:56
  49.7 6.4 %collective-permute-start.25 = (bf16[512,256]{1,0:T(8,128)(2,1)S(1)}, bf16[512,256]{1,0:T(8,128)(2,1)S(1)}, u32[]{:S(2)}, u32[]{:S(2)}) collective-permute-start(bf16[512,256]{1,0:T(8,128)(2,1)S(1)} %get-tuple-element.59), channel_id=1, source_target_pairs={{0,1},{1,0},{2,3},{3,2},{4,5},{5,4},{6,7},{7,6},{8,9},{9,8},{10,11... | collective-permute-start | bytes 786440 | tf_op jit(solution)/shard_map/ppermute | solution.py:56
  52.6 5.6 %collective-permute-start.22 = (bf16[128,256]{1,0:T(8,128)(2,1)S(1)}, bf16[128,256]{1,0:T(8,128)(2,1)S(1)}, u32[]{:S(2)}, u32[]{:S(2)}) collective-permute-start(bf16[128,256]{1,0:T(8,128)(2,1)S(1)} %get-tuple-element.50), channel_id=1, source_target_pairs={{0,8},{2,10},{4,12},{6,14},{8,0},{10,2},{12,4},{14,6},{1,9},{3,11}... | collective-permute-start | bytes 196616 | tf_op jit(solution)/shard_map/ppermute | solution.py:56
  53.4 6.2 %collective-permute-start.23 = (bf16[128,256]{1,0:T(8,128)(2,1)S(1)}, bf16[128,256]{1,0:T(8,128)(2,1)S(1)}, u32[]{:S(2)}, u32[]{:S(2)}) collective-permute-start(bf16[128,256]{1,0:T(8,128)(2,1)S(1)} %get-tuple-element.51), channel_id=1, source_target_pairs={{0,12},{2,14},{4,8},{6,10},{8,4},{10,6},{12,0},{14,2},{1,13},{3,15... | collective-permute-start | bytes 196616 | tf_op jit(solution)/shard_map/ppermute | solution.py:56
  55.0 5.0 %collective-permute-start.24 = (bf16[128,256]{1,0:T(8,128)(2,1)S(1)}, bf16[128,256]{1,0:T(8,128)(2,1)S(1)}, u32[]{:S(2)}, u32[]{:S(2)}) collective-permute-start(bf16[128,256]{1,0:T(8,128)(2,1)S(1)} %get-tuple-element.52), channel_id=1, source_target_pairs={{0,4},{2,6},{4,0},{6,2},{8,12},{10,14},{12,8},{14,10},{1,5},{3,7},... | collective-permute-start | bytes 196616 | tf_op jit(solution)/shard_map/ppermute | solution.py:56

commit v7 on v6

--- a/solution.py
+++ b/solution.py
@@ -10,7 +10,7 @@
 
 ITERS = 2
 TALL = 2
-COST = 10**10
+COST = 3 * 10**10
 
 learn_rate = 0.05
 decay_rate = 0.1

time: 60.9 us -> 61.1 us (level)
  waiting for transfers between devices: 16.5 us -> 14.4 us
  Pallas kernels: 8.5 us -> 10.1 us
    ppermute x26, waiting for transfers between devices: 16.5 us -> 14.4 us  [swap(): return lax.ppermute(x, axis, [(i, i ^ k) for i in range(n)])]
    pallas_call x17, Pallas kernels: 8.5 us -> 10.1 us  [call(): pl.pallas_call(body, out_shape=tuple(out_shape), in_specs=[smem()] * len(...]
  transfers between devices with their start and end apart: 26 -> 26, of which waited for: 12 -> 8; matrix products, arithmetic and copies ran while one was open for 0% -> 0% of each run, Pallas kernels for 13% -> 15%
where the time goes in v7:
time: 61.1 us; the launch traced here: 60.9 us
  starting transfers between devices  33.8 us (55%)
  waiting for transfers between devices  14.4 us (24%)
  Pallas kernels  10.1 us (17%)
  between operations  1.47 us (2%)
  local copies, waits for them, and re-layouts  0.98 us (2%)
    ppermute x26, starting transfers between devices, swap(): return lax.ppermute(x, axis, [(i, i ^ k) for i in range(n)])  33.8 us
    ppermute x26, waiting for transfers between devices, swap(): return lax.ppermute(x, axis, [(i, i ^ k) for i in range(n)])  14.4 us
    pallas_call x17, Pallas kernels, call(): pl.pallas_call(body, out_shape=tuple(out_shape), in_specs=[smem()] * len(...  10.1 us
  transfers between devices with their start and end apart: 26, of which 8 were waited for; matrix products, arithmetic and copies ran while one was open for 0% of the time, Pallas kernels for 15%

profile of v7, /device:TPU:0, one launch (start us, length us, event | category | flops | bytes accessed | tf_op | source)
XLA Modules:
  0.0 60.9 jit_solution(1481628348545000490)
XLA Ops:
  0.7 1.0 %copy-done.3 = f32[128,256]{1,0:T(8,128)S(1)} copy-done((f32[128,256]{1,0:T(8,128)S(1)}, f32[128,256]{1,0:T(8,128)}, u32[]{:S(2)}) %copy-start.3) | copy-done | bytes 131096
  1.6 5.1 %collective-permute-start.7 = (bf16[128,256]{1,0:T(8,128)(2,1)S(1)}, bf16[128,256]{1,0:T(8,128)(2,1)S(1)}, u32[]{:S(2)}, u32[]{:S(2)}) collective-permute-start(bf16[128,256]{1,0:T(8,128)(2,1)S(1)} %shard_map.68.refs_1_), channel_id=1, source_target_pairs={{0,10},{2,8},{4,14},{6,12},{8,2},{10,0},{12,6},{14,4},{1,11},{3,9}... | collective-permute-start | bytes 196616 | tf_op jit(solution)/shard_map/ppermute | solution.py:56
  6.7 1.3 %collective-permute-start.6 = (bf16[128,256]{1,0:T(8,128)(2,1)S(1)}, bf16[128,256]{1,0:T(8,128)(2,1)S(1)}, u32[]{:S(2)}, u32[]{:S(2)}) collective-permute-start(bf16[128,256]{1,0:T(8,128)(2,1)S(1)} %shard_map.68.refs_1_), channel_id=1, source_target_pairs={{0,14},{2,12},{4,10},{6,8},{8,6},{10,4},{12,2},{14,0},{1,15},{3,13... | collective-permute-start | bytes 196616 | tf_op jit(solution)/shard_map/ppermute | solution.py:56
  8.0 1.5 %collective-permute-start.5 = (bf16[128,256]{1,0:T(8,128)(2,1)S(1)}, bf16[128,256]{1,0:T(8,128)(2,1)S(1)}, u32[]{:S(2)}, u32[]{:S(2)}) collective-permute-start(bf16[128,256]{1,0:T(8,128)(2,1)S(1)} %shard_map.68.refs_1_), channel_id=1, source_target_pairs={{0,2},{2,0},{4,6},{6,4},{8,10},{10,8},{12,14},{14,12},{1,3},{3,1},... | collective-permute-start | bytes 196616 | tf_op jit(solution)/shard_map/ppermute | solution.py:56
  11.4 3.0 %collective-permute-start.2 = (bf16[128,256]{1,0:T(8,128)(2,1)S(1)}, bf16[128,256]{1,0:T(8,128)(2,1)S(1)}, u32[]{:S(2)}, u32[]{:S(2)}) collective-permute-start(bf16[128,256]{1,0:T(8,128)(2,1)S(1)} %shard_map.68.refs_1_), channel_id=1, source_target_pairs={{0,12},{2,14},{4,8},{6,10},{8,4},{10,6},{12,0},{14,2},{1,13},{3,15... | collective-permute-start | bytes 196616 | tf_op jit(solution)/shard_map/ppermute | solution.py:56
  14.9 1.3 %collective-permute-start = (bf16[128,256]{1,0:T(8,128)(2,1)S(1)}, bf16[128,256]{1,0:T(8,128)(2,1)S(1)}, u32[]{:S(2)}, u32[]{:S(2)}) collective-permute-start(bf16[128,256]{1,0:T(8,128)(2,1)S(1)} %shard_map.68.refs_1_), channel_id=1, source_target_pairs={{0,4},{2,6},{4,0},{6,2},{8,12},{10,14},{12,8},{14,10},{1,5},{3,7},... | collective-permute-start | bytes 196616 | tf_op jit(solution)/shard_map/ppermute | solution.py:56
  16.2 1.0 %shard_map.73 = (bf16[512,1024]{1,0:T(8,128)(2,1)S(1)}, bf16[512,256]{1,0:T(8,128)(2,1)S(1)}, bf16[4,128,256]{2,1,0:T(8,128)(2,1)S(1)}) custom-call(bf16[128,256]{1,0:T(8,128)(2,1)S(1)} %collective-permute-done.4.refs_0_, bf16[128,256]{1,0:T(8,128)(2,1)S(1)} %collective-permute-done.5.refs_1_, bf16[128,256]{1,0:T(8,128)(2,1)S(1)} %collective-permute-done.6.refs_2_, ...), custom_call_target="tpu_custom_call" | custom-call | flops 30000001024 | tf_op jit(solution)/shard_map/pallas_call | solution.py:44
  17.1 1.6 %collective-permute-start.8 = (bf16[4,128,256]{2,1,0:T(8,128)(2,1)S(1)}, bf16[4,128,256]{2,1,0:T(8,128)(2,1)S(1)}, u32[]{:S(2)}, u32[]{:S(2)}) collective-permute-start(bf16[4,128,256]{2,1,0:T(8,128)(2,1)S(1)} %get-tuple-element.33), channel_id=1, source_target_pairs={{0,2},{2,0},{4,6},{6,4},{8,10},{10,8},{12,14},{14,12},{1,3},{3,1},... | collective-permute-start | bytes 786440 | tf_op jit(solution)/shard_map/ppermute | solution.py:56
  18.7 2.7 %collective-permute-done.1.refs_2_ = bf16[128,256]{1,0:T(8,128)(2,1)S(1)} collective-permute-done((bf16[128,256]{1,0:T(8,128)(2,1)S(1)}, bf16[128,256]{1,0:T(8,128)(2,1)S(1)}, u32[]{:S(2)}, u32[]{:S(2)}) %collective-permute-start.1) | collective-permute-done | bytes 65568 | tf_op jit(solution)/shard_map/ppermute | solution.py:56
  21.4 1.0 %shard_map.72 = (bf16[512,1024]{1,0:T(8,128)(2,1)S(1)}, bf16[512,256]{1,0:T(8,128)(2,1)S(1)}, f32[4,128,256]{2,1,0:T(8,128)S(1)}) custom-call(bf16[128,256]{1,0:T(8,128)(2,1)S(1)} %collective-permute-done.refs_0_, bf16[128,256]{1,0:T(8,128)(2,1)S(1)} %shard_map.68.refs_1_, bf16[128,256]{1,0:T(8,128)(2,1)S(1)} %collective-permute-done.1.refs_2_, ...), custom_call_target="tpu_custom_call" | custom-call | flops 30000001024 | tf_op jit(solution)/shard_map/pallas_call | solution.py:44
  23.3 1.6 %collective-permute-done.8.other = bf16[4,128,256]{2,1,0:T(8,128)(2,1)S(1)} collective-permute-done((bf16[4,128,256]{2,1,0:T(8,128)(2,1)S(1)}, bf16[4,128,256]{2,1,0:T(8,128)(2,1)S(1)}, u32[]{:S(2)}, u32[]{:S(2)}) %collective-permute-start.8) | collective-permute-done | bytes 262176 | tf_op jit(solution)/shard_map/ppermute | solution.py:56
  24.9 2.1 %collective-permute-start.9 = (bf16[128,256]{1,0:T(8,128)(2,1)S(1)}, bf16[128,256]{1,0:T(8,128)(2,1)S(1)}, u32[]{:S(2)}, u32[]{:S(2)}) collective-permute-start(bf16[128,256]{1,0:T(8,128)(2,1)S(1)} %get-tuple-element.35), channel_id=1, source_target_pairs={{0,8},{2,10},{4,12},{6,14},{8,0},{10,2},{12,4},{14,6},{1,9},{3,11}... | collective-permute-start | bytes 196616 | tf_op jit(solution)/shard_map/ppermute | solution.py:56
  27.1 1.2 %collective-permute-start.10 = (bf16[128,256]{1,0:T(8,128)(2,1)S(1)}, bf16[128,256]{1,0:T(8,128)(2,1)S(1)}, u32[]{:S(2)}, u32[]{:S(2)}) collective-permute-start(bf16[128,256]{1,0:T(8,128)(2,1)S(1)} %get-tuple-element.36), channel_id=1, source_target_pairs={{0,12},{2,14},{4,8},{6,10},{8,4},{10,6},{12,0},{14,2},{1,13},{3,15... | collective-permute-start | bytes 196616 | tf_op jit(solution)/shard_map/ppermute | solution.py:56
  29.3 2.5 %collective-permute-done.9.refs_1_ = bf16[128,256]{1,0:T(8,128)(2,1)S(1)} collective-permute-done((bf16[128,256]{1,0:T(8,128)(2,1)S(1)}, bf16[128,256]{1,0:T(8,128)(2,1)S(1)}, u32[]{:S(2)}, u32[]{:S(2)}) %collective-permute-start.9) | collective-permute-done | bytes 65568 | tf_op jit(solution)/shard_map/ppermute | solution.py:56
  31.8 1.5 %collective-permute-done.10.refs_2_ = bf16[128,256]{1,0:T(8,128)(2,1)S(1)} collective-permute-done((bf16[128,256]{1,0:T(8,128)(2,1)S(1)}, bf16[128,256]{1,0:T(8,128)(2,1)S(1)}, u32[]{:S(2)}, u32[]{:S(2)}) %collective-permute-start.10) | collective-permute-done | bytes 65568 | tf_op jit(solution)/shard_map/ppermute | solution.py:56
  33.3 2.4 %collective-permute-start.20 = (bf16[128,256]{1,0:T(8,128)(2,1)S(1)}, bf16[128,256]{1,0:T(8,128)(2,1)S(1)}, u32[]{:S(2)}, u32[]{:S(2)}) collective-permute-start(bf16[128,256]{1,0:T(8,128)(2,1)S(1)} %get-tuple-element.39.refs_1_), channel_id=1, source_target_pairs={{0,10},{2,8},{4,14},{6,12},{8,2},{10,0},{12,6},{14,4},{1,11},{3,9}... | collective-permute-start | bytes 196616 | tf_op jit(solution)/shard_map/ppermute | solution.py:56
  35.7 1.0 %collective-permute-start.19 = (bf16[128,256]{1,0:T(8,128)(2,1)S(1)}, bf16[128,256]{1,0:T(8,128)(2,1)S(1)}, u32[]{:S(2)}, u32[]{:S(2)}) collective-permute-start(bf16[128,256]{1,0:T(8,128)(2,1)S(1)} %get-tuple-element.39.refs_1_), channel_id=1, source_target_pairs={{0,14},{2,12},{4,10},{6,8},{8,6},{10,4},{12,2},{14,0},{1,15},{3,13... | collective-permute-start | bytes 196616 | tf_op jit(solution)/shard_map/ppermute | solution.py:56
  36.7 2.0 %collective-permute-start.18 = (bf16[128,256]{1,0:T(8,128)(2,1)S(1)}, bf16[128,256]{1,0:T(8,128)(2,1)S(1)}, u32[]{:S(2)}, u32[]{:S(2)}) collective-permute-start(bf16[128,256]{1,0:T(8,128)(2,1)S(1)} %get-tuple-element.39.refs_1_), channel_id=1, source_target_pairs={{0,2},{2,0},{4,6},{6,4},{8,10},{10,8},{12,14},{14,12},{1,3},{3,1},... | collective-permute-start | bytes 196616 | tf_op jit(solution)/shard_map/ppermute | solution.py:56
  39.3 2.3 %collective-permute-start.14 = (bf16[128,256]{1,0:T(8,128)(2,1)S(1)}, bf16[128,256]{1,0:T(8,128)(2,1)S(1)}, u32[]{:S(2)}, u32[]{:S(2)}) collective-permute-start(bf16[128,256]{1,0:T(8,128)(2,1)S(1)} %get-tuple-element.39.refs_1_), channel_id=1, source_target_pairs={{0,12},{2,14},{4,8},{6,10},{8,4},{10,6},{12,0},{14,2},{1,13},{3,15... | collective-permute-start | bytes 196616 | tf_op jit(solution)/shard_map/ppermute | solution.py:56
  41.6 1.1 %shard_map.78.refs_4_ = bf16[1024,256]{1,0:T(8,128)(2,1)S(1)} custom-call(bf16[512,256]{1,0:T(8,128)(2,1)} %get-tuple-element.46.mine, bf16[512,256]{1,0:T(8,128)(2,1)} %collective-permute-done.16.other), custom_call_target="tpu_custom_call" | custom-call | flops 30000001024 | tf_op jit(solution)/shard_map/pallas_call | solution.py:44
  42.9 1.9 %collective-permute-start.12 = (bf16[128,256]{1,0:T(8,128)(2,1)S(1)}, bf16[128,256]{1,0:T(8,128)(2,1)S(1)}, u32[]{:S(2)}, u32[]{:S(2)}) collective-permute-start(bf16[128,256]{1,0:T(8,128)(2,1)S(1)} %get-tuple-element.39.refs_1_), channel_id=1, source_target_pairs={{0,4},{2,6},{4,0},{6,2},{8,12},{10,14},{12,8},{14,10},{1,5},{3,7},... | collective-permute-start | bytes 196616 | tf_op jit(solution)/shard_map/ppermute | solution.py:56
  44.8 1.0 %shard_map.80 = (bf16[512,1024]{1,0:T(8,128)(2,1)S(1)}, bf16[512,256]{1,0:T(8,128)(2,1)S(1)}, bf16[4,128,256]{2,1,0:T(8,128)(2,1)S(1)}) custom-call(bf16[128,256]{1,0:T(8,128)(2,1)S(1)} %collective-permute-done.17.refs_0_, bf16[128,256]{1,0:T(8,128)(2,1)S(1)} %collective-permute-done.18.refs_1_, bf16[128,256]{1,0:T(8,128)(2,1)S(1)} %collective-permute-done.19.refs_2_, ...), custom_call_target="tpu_custom_call" | custom-call | flops 30000001024 | tf_op jit(solution)/shard_map/pallas_call | solution.py:44
  45.8 1.7 %collective-permute-start.21 = (bf16[4,128,256]{2,1,0:T(8,128)(2,1)S(1)}, bf16[4,128,256]{2,1,0:T(8,128)(2,1)S(1)}, u32[]{:S(2)}, u32[]{:S(2)}) collective-permute-start(bf16[4,128,256]{2,1,0:T(8,128)(2,1)S(1)} %get-tuple-element.48), channel_id=1, source_target_pairs={{0,2},{2,0},{4,6},{6,4},{8,10},{10,8},{12,14},{14,12},{1,3},{3,1},... | collective-permute-start | bytes 786440 | tf_op jit(solution)/shard_map/ppermute | solution.py:56
  47.5 1.0 %collective-permute-done.13.refs_2_ = bf16[128,256]{1,0:T(8,128)(2,1)S(1)} collective-permute-done((bf16[128,256]{1,0:T(8,128)(2,1)S(1)}, bf16[128,256]{1,0:T(8,128)(2,1)S(1)}, u32[]{:S(2)}, u32[]{:S(2)}) %collective-permute-start.13) | collective-permute-done | bytes 65568 | tf_op jit(solution)/shard_map/ppermute | solution.py:56
  48.6 1.0 %shard_map.79 = (bf16[512,1024]{1,0:T(8,128)(2,1)S(1)}, bf16[512,256]{1,0:T(8,128)(2,1)S(1)}, f32[4,128,256]{2,1,0:T(8,128)S(1)}) custom-call(bf16[128,256]{1,0:T(8,128)(2,1)S(1)} %collective-permute-done.12.refs_0_, bf16[128,256]{1,0:T(8,128)(2,1)S(1)} %get-tuple-element.39.refs_1_, bf16[128,256]{1,0:T(8,128)(2,1)S(1)} %collective-permute-done.13.refs_2_, ...), custom_call_target="tpu_custom_call" | custom-call | flops 30000001024 | tf_op jit(solution)/shard_map/pallas_call | solution.py:44
  50.5 1.7 %collective-permute-done.21.other = bf16[4,128,256]{2,1,0:T(8,128)(2,1)S(1)} collective-permute-done((bf16[4,128,256]{2,1,0:T(8,128)(2,1)S(1)}, bf16[4,128,256]{2,1,0:T(8,128)(2,1)S(1)}, u32[]{:S(2)}, u32[]{:S(2)}) %collective-permute-start.21) | collective-permute-done | bytes 262176 | tf_op jit(solution)/shard_map/ppermute | solution.py:56
  52.3 1.7 %collective-permute-start.22 = (bf16[128,256]{1,0:T(8,128)(2,1)S(1)}, bf16[128,256]{1,0:T(8,128)(2,1)S(1)}, u32[]{:S(2)}, u32[]{:S(2)}) collective-permute-start(bf16[128,256]{1,0:T(8,128)(2,1)S(1)} %get-tuple-element.50), channel_id=1, source_target_pairs={{0,8},{2,10},{4,12},{6,14},{8,0},{10,2},{12,4},{14,6},{1,9},{3,11}... | collective-permute-start | bytes 196616 | tf_op jit(solution)/shard_map/ppermute | solution.py:56
  54.0 0.9 %collective-permute-start.23 = (bf16[128,256]{1,0:T(8,128)(2,1)S(1)}, bf16[128,256]{1,0:T(8,128)(2,1)S(1)}, u32[]{:S(2)}, u32[]{:S(2)}) collective-permute-start(bf16[128,256]{1,0:T(8,128)(2,1)S(1)} %get-tuple-element.51), channel_id=1, source_target_pairs={{0,12},{2,14},{4,8},{6,10},{8,4},{10,6},{12,0},{14,2},{1,13},{3,15... | collective-permute-start | bytes 196616 | tf_op jit(solution)/shard_map/ppermute | solution.py:56
  54.9 0.9 %collective-permute-start.24 = (bf16[128,256]{1,0:T(8,128)(2,1)S(1)}, bf16[128,256]{1,0:T(8,128)(2,1)S(1)}, u32[]{:S(2)}, u32[]{:S(2)}) collective-permute-start(bf16[128,256]{1,0:T(8,128)(2,1)S(1)} %get-tuple-element.52), channel_id=1, source_target_pairs={{0,4},{2,6},{4,0},{6,2},{8,12},{10,14},{12,8},{14,10},{1,5},{3,7},... | collective-permute-start | bytes 196616 | tf_op jit(solution)/shard_map/ppermute | solution.py:56
  55.8 0.9 %shard_map.84 = f32[512,256]{1,0:T(8,128)} custom-call(f32[512,256]{1,0:T(8,128)S(1)} %get-tuple-element.53.own, f32[512,256]{1,0:T(8,128)S(1)} %get-tuple-element.58.refs_0_, bf16[512,256]{1,0:T(8,128)(2,1)S(1)} %collective-permute-done.25.refs_1_), custom_call_target="tpu_custom_call" | custom-call | flops 30000001024 | tf_op jit(solution)/shard_map/pallas_call | solution.py:44
  56.7 2.0 %collective-permute-done.22.refs_1_ = bf16[128,256]{1,0:T(8,128)(2,1)S(1)} collective-permute-done((bf16[128,256]{1,0:T(8,128)(2,1)S(1)}, bf16[128,256]{1,0:T(8,128)(2,1)S(1)}, u32[]{:S(2)}, u32[]{:S(2)}) %collective-permute-start.22) | collective-permute-done | bytes 65568 | tf_op jit(solution)/shard_map/ppermute | solution.py:56
  58.8 1.4 %collective-permute-done.23.refs_2_ = bf16[128,256]{1,0:T(8,128)(2,1)S(1)} collective-permute-done((bf16[128,256]{1,0:T(8,128)(2,1)S(1)}, bf16[128,256]{1,0:T(8,128)(2,1)S(1)}, u32[]{:S(2)}, u32[]{:S(2)}) %collective-permute-start.23) | collective-permute-done | bytes 65568 | tf_op jit(solution)/shard_map/ppermute | solution.py:56
  (49 shorter events, 6.3 us)
Async XLA Ops:
  0.6 9.1 %copy-start.1 = (f32[512,256]{1,0:T(8,128)S(1)}, f32[512,256]{1,0:T(8,128)}, u32[]{:S(2)}) copy-start(f32[512,256]{1,0:T(8,128)} %own.3) | copy-start | bytes 1572868
  0.6 1.0 %copy-start.3 = (f32[128,256]{1,0:T(8,128)S(1)}, f32[128,256]{1,0:T(8,128)}, u32[]{:S(2)}) copy-start(f32[128,256]{1,0:T(8,128)} %own.2) | copy-start | bytes 393220
  1.6 8.9 %copy-start = (s32[1,1,24,128,128]{4,3,2,1,0:T(8,128)S(1)}, s32[1,1,24,128,128]{4,3,2,1,0:T(8,128)}, u32[]{:S(2)}) copy-start(s32[1,1,24,128,128]{4,3,2,1,0:T(8,128)} %param.9) | copy-start | bytes 4718596
  1.6 8.9 %copy-start.5 = (s32[1,1,24]{2,1,0:T(1,128)S(1)}, s32[1,1,24]{2,1,0:T(1,128)}, u32[]{:S(2)}) copy-start(s32[1,1,24]{2,1,0:T(1,128)} %param.7) | copy-start | bytes 292
  1.6 12.8 %collective-permute-start.7 = (bf16[128,256]{1,0:T(8,128)(2,1)S(1)}, bf16[128,256]{1,0:T(8,128)(2,1)S(1)}, u32[]{:S(2)}, u32[]{:S(2)}) collective-permute-start(bf16[128,256]{1,0:T(8,128)(2,1)S(1)} %shard_map.68.refs_1_), channel_id=1, source_target_pairs={{0,10},{2,8},{4,14},{6,12},{8,2},{10,0},{12,6},{14,4},{1,11},{3,9}... | collective-permute-start | bytes 196616 | tf_op jit(solution)/shard_map/ppermute | solution.py:56
  6.7 8.2 %collective-permute-start.6 = (bf16[128,256]{1,0:T(8,128)(2,1)S(1)}, bf16[128,256]{1,0:T(8,128)(2,1)S(1)}, u32[]{:S(2)}, u32[]{:S(2)}) collective-permute-start(bf16[128,256]{1,0:T(8,128)(2,1)S(1)} %shard_map.68.refs_1_), channel_id=1, source_target_pairs={{0,14},{2,12},{4,10},{6,8},{8,6},{10,4},{12,2},{14,0},{1,15},{3,13... | collective-permute-start | bytes 196616 | tf_op jit(solution)/shard_map/ppermute | solution.py:56
  8.0 8.2 %collective-permute-start.5 = (bf16[128,256]{1,0:T(8,128)(2,1)S(1)}, bf16[128,256]{1,0:T(8,128)(2,1)S(1)}, u32[]{:S(2)}, u32[]{:S(2)}) collective-permute-start(bf16[128,256]{1,0:T(8,128)(2,1)S(1)} %shard_map.68.refs_1_), channel_id=1, source_target_pairs={{0,2},{2,0},{4,6},{6,4},{8,10},{10,8},{12,14},{14,12},{1,3},{3,1},... | collective-permute-start | bytes 196616 | tf_op jit(solution)/shard_map/ppermute | solution.py:56
  9.5 6.6 %collective-permute-start.4 = (bf16[128,256]{1,0:T(8,128)(2,1)S(1)}, bf16[128,256]{1,0:T(8,128)(2,1)S(1)}, u32[]{:S(2)}, u32[]{:S(2)}) collective-permute-start(bf16[128,256]{1,0:T(8,128)(2,1)S(1)} %shard_map.68.refs_1_), channel_id=1, source_target_pairs={{0,6},{2,4},{4,2},{6,0},{8,14},{10,12},{12,10},{14,8},{1,7},{3,5},... | collective-permute-start | bytes 196616 | tf_op jit(solution)/shard_map/ppermute | solution.py:56
  9.8 1.6 %collective-permute-start.3 = (bf16[512,256]{1,0:T(8,128)(2,1)S(1)}, bf16[512,256]{1,0:T(8,128)(2,1)S(1)}, u32[]{:S(2)}, u32[]{:S(2)}) collective-permute-start(bf16[512,256]{1,0:T(8,128)(2,1)S(1)} %shard_map.69.mine), channel_id=1, source_target_pairs={{0,1},{1,0},{2,3},{3,2},{4,5},{5,4},{6,7},{7,6},{8,9},{9,8},{10,11... | collective-permute-start | bytes 786440 | tf_op jit(solution)/shard_map/ppermute | solution.py:56
  11.4 7.3 %collective-permute-start.2 = (bf16[128,256]{1,0:T(8,128)(2,1)S(1)}, bf16[128,256]{1,0:T(8,128)(2,1)S(1)}, u32[]{:S(2)}, u32[]{:S(2)}) collective-permute-start(bf16[128,256]{1,0:T(8,128)(2,1)S(1)} %shard_map.68.refs_1_), channel_id=1, source_target_pairs={{0,12},{2,14},{4,8},{6,10},{8,4},{10,6},{12,0},{14,2},{1,13},{3,15... | collective-permute-start | bytes 196616 | tf_op jit(solution)/shard_map/ppermute | solution.py:56
  14.4 6.9 %collective-permute-start.1 = (bf16[128,256]{1,0:T(8,128)(2,1)S(1)}, bf16[128,256]{1,0:T(8,128)(2,1)S(1)}, u32[]{:S(2)}, u32[]{:S(2)}) collective-permute-start(bf16[128,256]{1,0:T(8,128)(2,1)S(1)} %shard_map.68.refs_1_), channel_id=1, source_target_pairs={{0,8},{2,10},{4,12},{6,14},{8,0},{10,2},{12,4},{14,6},{1,9},{3,11}... | collective-permute-start | bytes 196616 | tf_op jit(solution)/shard_map/ppermute | solution.py:56
  14.9 6.5 %collective-permute-start = (bf16[128,256]{1,0:T(8,128)(2,1)S(1)}, bf16[128,256]{1,0:T(8,128)(2,1)S(1)}, u32[]{:S(2)}, u32[]{:S(2)}) collective-permute-start(bf16[128,256]{1,0:T(8,128)(2,1)S(1)} %shard_map.68.refs_1_), channel_id=1, source_target_pairs={{0,4},{2,6},{4,0},{6,2},{8,12},{10,14},{12,8},{14,10},{1,5},{3,7},... | collective-permute-start | bytes 196616 | tf_op jit(solution)/shard_map/ppermute | solution.py:56
  17.1 7.7 %collective-permute-start.8 = (bf16[4,128,256]{2,1,0:T(8,128)(2,1)S(1)}, bf16[4,128,256]{2,1,0:T(8,128)(2,1)S(1)}, u32[]{:S(2)}, u32[]{:S(2)}) collective-permute-start(bf16[4,128,256]{2,1,0:T(8,128)(2,1)S(1)} %get-tuple-element.33), channel_id=1, source_target_pairs={{0,2},{2,0},{4,6},{6,4},{8,10},{10,8},{12,14},{14,12},{1,3},{3,1},... | collective-permute-start | bytes 786440 | tf_op jit(solution)/shard_map/ppermute | solution.py:56
  23.2 5.3 %collective-permute-start.15 = (bf16[512,256]{1,0:T(8,128)(2,1)S(1)}, bf16[512,256]{1,0:T(8,128)(2,1)S(1)}, u32[]{:S(2)}, u32[]{:S(2)}) collective-permute-start(bf16[512,256]{1,0:T(8,128)(2,1)S(1)} %get-tuple-element.45), channel_id=1, source_target_pairs={{0,1},{1,0},{2,3},{3,2},{4,5},{5,4},{6,7},{7,6},{8,9},{9,8},{10,11... | collective-permute-start | bytes 786440 | tf_op jit(solution)/shard_map/ppermute | solution.py:56
  24.9 3.6 %copy-start.2 = (f32[512,256]{1,0:T(8,128)S(1)}, f32[512,256]{1,0:T(8,128)}, u32[]{:S(2)}) copy-start(f32[512,256]{1,0:T(8,128)} %own.3) | copy-start | bytes 1572868
  24.9 6.9 %collective-permute-start.9 = (bf16[128,256]{1,0:T(8,128)(2,1)S(1)}, bf16[128,256]{1,0:T(8,128)(2,1)S(1)}, u32[]{:S(2)}, u32[]{:S(2)}) collective-permute-start(bf16[128,256]{1,0:T(8,128)(2,1)S(1)} %get-tuple-element.35), channel_id=1, source_target_pairs={{0,8},{2,10},{4,12},{6,14},{8,0},{10,2},{12,4},{14,6},{1,9},{3,11}... | collective-permute-start | bytes 196616 | tf_op jit(solution)/shard_map/ppermute | solution.py:56
  27.1 6.2 %collective-permute-start.10 = (bf16[128,256]{1,0:T(8,128)(2,1)S(1)}, bf16[128,256]{1,0:T(8,128)(2,1)S(1)}, u32[]{:S(2)}, u32[]{:S(2)}) collective-permute-start(bf16[128,256]{1,0:T(8,128)(2,1)S(1)} %get-tuple-element.36), channel_id=1, source_target_pairs={{0,12},{2,14},{4,8},{6,10},{8,4},{10,6},{12,0},{14,2},{1,13},{3,15... | collective-permute-start | bytes 196616 | tf_op jit(solution)/shard_map/ppermute | solution.py:56
  28.3 5.0 %collective-permute-start.11 = (bf16[128,256]{1,0:T(8,128)(2,1)S(1)}, bf16[128,256]{1,0:T(8,128)(2,1)S(1)}, u32[]{:S(2)}, u32[]{:S(2)}) collective-permute-start(bf16[128,256]{1,0:T(8,128)(2,1)S(1)} %get-tuple-element.37), channel_id=1, source_target_pairs={{0,4},{2,6},{4,0},{6,2},{8,12},{10,14},{12,8},{14,10},{1,5},{3,7},... | collective-permute-start | bytes 196616 | tf_op jit(solution)/shard_map/ppermute | solution.py:56
  28.5 4.8 %copy-start.4 = (f32[128,256]{1,0:T(8,128)S(1)}, f32[128,256]{1,0:T(8,128)}, u32[]{:S(2)}) copy-start(f32[128,256]{1,0:T(8,128)} %own.2) | copy-start | bytes 393220
  29.3 9.9 %collective-permute-start.16 = (bf16[512,256]{1,0:T(8,128)(2,1)}, bf16[512,256]{1,0:T(8,128)(2,1)}, u32[]{:S(2)}, u32[]{:S(2)}) collective-permute-start(bf16[512,256]{1,0:T(8,128)(2,1)} %get-tuple-element.46.mine), channel_id=1, source_target_pairs={{0,1},{1,0},{2,3},{3,2},{4,5},{5,4},{6,7},{7,6},{8,9},{9,8},{10,11... | collective-permute-start | bytes 786440 | tf_op jit(solution)/shard_map/ppermute | solution.py:56
  33.3 9.3 %collective-permute-start.20 = (bf16[128,256]{1,0:T(8,128)(2,1)S(1)}, bf16[128,256]{1,0:T(8,128)(2,1)S(1)}, u32[]{:S(2)}, u32[]{:S(2)}) collective-permute-start(bf16[128,256]{1,0:T(8,128)(2,1)S(1)} %get-tuple-element.39.refs_1_), channel_id=1, source_target_pairs={{0,10},{2,8},{4,14},{6,12},{8,2},{10,0},{12,6},{14,4},{1,11},{3,9}... | collective-permute-start | bytes 196616 | tf_op jit(solution)/shard_map/ppermute | solution.py:56
  35.7 7.2 %collective-permute-start.19 = (bf16[128,256]{1,0:T(8,128)(2,1)S(1)}, bf16[128,256]{1,0:T(8,128)(2,1)S(1)}, u32[]{:S(2)}, u32[]{:S(2)}) collective-permute-start(bf16[128,256]{1,0:T(8,128)(2,1)S(1)} %get-tuple-element.39.refs_1_), channel_id=1, source_target_pairs={{0,14},{2,12},{4,10},{6,8},{8,6},{10,4},{12,2},{14,0},{1,15},{3,13... | collective-permute-start | bytes 196616 | tf_op jit(solution)/shard_map/ppermute | solution.py:56
  36.7 8.1 %collective-permute-start.18 = (bf16[128,256]{1,0:T(8,128)(2,1)S(1)}, bf16[128,256]{1,0:T(8,128)(2,1)S(1)}, u32[]{:S(2)}, u32[]{:S(2)}) collective-permute-start(bf16[128,256]{1,0:T(8,128)(2,1)S(1)} %get-tuple-element.39.refs_1_), channel_id=1, source_target_pairs={{0,2},{2,0},{4,6},{6,4},{8,10},{10,8},{12,14},{14,12},{1,3},{3,1},... | collective-permute-start | bytes 196616 | tf_op jit(solution)/shard_map/ppermute | solution.py:56
  38.7 6.1 %collective-permute-start.17 = (bf16[128,256]{1,0:T(8,128)(2,1)S(1)}, bf16[128,256]{1,0:T(8,128)(2,1)S(1)}, u32[]{:S(2)}, u32[]{:S(2)}) collective-permute-start(bf16[128,256]{1,0:T(8,128)(2,1)S(1)} %get-tuple-element.39.refs_1_), channel_id=1, source_target_pairs={{0,6},{2,4},{4,2},{6,0},{8,14},{10,12},{12,10},{14,8},{1,7},{3,5},... | collective-permute-start | bytes 196616 | tf_op jit(solution)/shard_map/ppermute | solution.py:56
  39.3 8.3 %collective-permute-start.14 = (bf16[128,256]{1,0:T(8,128)(2,1)S(1)}, bf16[128,256]{1,0:T(8,128)(2,1)S(1)}, u32[]{:S(2)}, u32[]{:S(2)}) collective-permute-start(bf16[128,256]{1,0:T(8,128)(2,1)S(1)} %get-tuple-element.39.refs_1_), channel_id=1, source_target_pairs={{0,12},{2,14},{4,8},{6,10},{8,4},{10,6},{12,0},{14,2},{1,13},{3,15... | collective-permute-start | bytes 196616 | tf_op jit(solution)/shard_map/ppermute | solution.py:56
  42.6 5.9 %collective-permute-start.13 = (bf16[128,256]{1,0:T(8,128)(2,1)S(1)}, bf16[128,256]{1,0:T(8,128)(2,1)S(1)}, u32[]{:S(2)}, u32[]{:S(2)}) collective-permute-start(bf16[128,256]{1,0:T(8,128)(2,1)S(1)} %get-tuple-element.39.refs_1_), channel_id=1, source_target_pairs={{0,8},{2,10},{4,12},{6,14},{8,0},{10,2},{12,4},{14,6},{1,9},{3,11}... | collective-permute-start | bytes 196616 | tf_op jit(solution)/shard_map/ppermute | solution.py:56
  42.9 5.6 %collective-permute-start.12 = (bf16[128,256]{1,0:T(8,128)(2,1)S(1)}, bf16[128,256]{1,0:T(8,128)(2,1)S(1)}, u32[]{:S(2)}, u32[]{:S(2)}) collective-permute-start(bf16[128,256]{1,0:T(8,128)(2,1)S(1)} %get-tuple-element.39.refs_1_), channel_id=1, source_target_pairs={{0,4},{2,6},{4,0},{6,2},{8,12},{10,14},{12,8},{14,10},{1,5},{3,7},... | collective-permute-start | bytes 196616 | tf_op jit(solution)/shard_map/ppermute | solution.py:56
  45.8 6.4 %collective-permute-start.21 = (bf16[4,128,256]{2,1,0:T(8,128)(2,1)S(1)}, bf16[4,128,256]{2,1,0:T(8,128)(2,1)S(1)}, u32[]{:S(2)}, u32[]{:S(2)}) collective-permute-start(bf16[4,128,256]{2,1,0:T(8,128)(2,1)S(1)} %get-tuple-element.48), channel_id=1, source_target_pairs={{0,2},{2,0},{4,6},{6,4},{8,10},{10,8},{12,14},{14,12},{1,3},{3,1},... | collective-permute-start | bytes 786440 | tf_op jit(solution)/shard_map/ppermute | solution.py:56
  50.4 5.4 %collective-permute-start.25 = (bf16[512,256]{1,0:T(8,128)(2,1)S(1)}, bf16[512,256]{1,0:T(8,128)(2,1)S(1)}, u32[]{:S(2)}, u32[]{:S(2)}) collective-permute-start(bf16[512,256]{1,0:T(8,128)(2,1)S(1)} %get-tuple-element.59), channel_id=1, source_target_pairs={{0,1},{1,0},{2,3},{3,2},{4,5},{5,4},{6,7},{7,6},{8,9},{9,8},{10,11... | collective-permute-start | bytes 786440 | tf_op jit(solution)/shard_map/ppermute | solution.py:56
  52.3 6.5 %collective-permute-start.22 = (bf16[128,256]{1,0:T(8,128)(2,1)S(1)}, bf16[128,256]{1,0:T(8,128)(2,1)S(1)}, u32[]{:S(2)}, u32[]{:S(2)}) collective-permute-start(bf16[128,256]{1,0:T(8,128)(2,1)S(1)} %get-tuple-element.50), channel_id=1, source_target_pairs={{0,8},{2,10},{4,12},{6,14},{8,0},{10,2},{12,4},{14,6},{1,9},{3,11}... | collective-permute-start | bytes 196616 | tf_op jit(solution)/shard_map/ppermute | solution.py:56
  54.0 6.2 %collective-permute-start.23 = (bf16[128,256]{1,0:T(8,128)(2,1)S(1)}, bf16[128,256]{1,0:T(8,128)(2,1)S(1)}, u32[]{:S(2)}, u32[]{:S(2)}) collective-permute-start(bf16[128,256]{1,0:T(8,128)(2,1)S(1)} %get-tuple-element.51), channel_id=1, source_target_pairs={{0,12},{2,14},{4,8},{6,10},{8,4},{10,6},{12,0},{14,2},{1,13},{3,15... | collective-permute-start | bytes 196616 | tf_op jit(solution)/shard_map/ppermute | solution.py:56
  54.9 5.2 %collective-permute-start.24 = (bf16[128,256]{1,0:T(8,128)(2,1)S(1)}, bf16[128,256]{1,0:T(8,128)(2,1)S(1)}, u32[]{:S(2)}, u32[]{:S(2)}) collective-permute-start(bf16[128,256]{1,0:T(8,128)(2,1)S(1)} %get-tuple-element.52), channel_id=1, source_target_pairs={{0,4},{2,6},{4,0},{6,2},{8,12},{10,14},{12,8},{14,10},{1,5},{3,7},... | collective-permute-start | bytes 196616 | tf_op jit(solution)/shard_map/ppermute | solution.py:56
